TPU v7x, 512 devices: a whole 4x8x8 slice. The times are simulated.
512 devices in a mesh: gx: 16 (over x_hi, y), gy: 8 (over z), gz: 4 (over x_lo, core).
Axes of the slice: x: 4 (x_hi: 2, x_lo: 2; x = x_hi * 2 + x_lo), y: 8, z: 8, core: 2. Of those that a mesh axis runs over, the one named last changes fastest.
Arguments:
- features: float32 [32, 16, 8, 8, 128], P('gx', 'gy', 'gz'), may hold values from -6 to 6
- offsets: float32 [32, 16, 8, 3, 8], P('gx', 'gy', 'gz'), may hold values from 0 to 1
- counts: int32 [32, 16, 8], P('gx', 'gy', 'gz'), may hold values from 0 to 8, as said below
- species: int32 [32, 16, 8, 8], P('gx', 'gy', 'gz'), may hold values from 0 to 7
- neighbours: int32 [32, 16, 8, 8, 32], P('gx', 'gy', 'gz'), may hold values from 0 to 215, as said below
- w_radial: float32 [8, 128], replicated, may hold values from -2 to 2
- w_vector: float32 [8, 128], replicated, may hold values from -2 to 2
- w_mix: float32 [128, 128], replicated, may hold values from -0.5 to 0.5
- w_out: float32 [128], replicated, may hold values from -0.5 to 0.5
- w_charge: float32 [128, 16], replicated, may hold values from -0.5 to 0.5
- species_shift: float32 [8], replicated, may hold values from -4 to 4
Outputs:
- atom_energy: float32 [32, 16, 8, 8], P('gx', 'gy', 'gz')
- forces: float32 [32, 16, 8, 3, 8], P('gx', 'gy', 'gz')
Inputs may be any that keep to these rules, and one draw needn't show every extreme that they name: `counts`: at most 8 atoms in a cell and some cell holds exactly 8; the live atoms of a cell fill its first slots; the mean count differs strongly from domain to domain. `neighbours`: entries index the 27 cells around the atom's cell times 8 slots; an atom never lists its own slot; entries may name empty slots and may repeat.
All inputs are finite; a program needn't handle non-finite values.
Results may differ from a plain program's by a relative error of at most 0.0003.
Values sent between devices are 32-bit elements; how exact they have to be, the bound alone decides.
No kernel may reach another device: no remote copies, remote signals or barrier semaphores. Data moves between devices by JAX's collectives and lax.ppermute only.
A program may use at most 64 MiB of HBM per device.

v0:
```python
import math

import jax
import jax.numpy as jnp
from jax import lax
from jax.sharding import PartitionSpec as P

KX = 16
KY = 8
KZ = 8


HIGH = lax.Precision.HIGHEST


def shifted_2(value, axis, steps):
    count = lax.axis_size(axis)
    pairs = [(source, (source + steps) % count) for source in range(count)]
    return lax.ppermute(value, axis, pairs)


def with_halo(block, sides, width):
    for axis, dim in sides:
        count = lax.axis_size(axis)
        forward = [(i, i + 1) for i in range(count - 1)]
        forward.append((count - 1, 0))
        backward = [(target, source) for source, target in forward]
        low = lax.ppermute(
            lax.slice_in_dim(block, block.shape[dim] - width, None, axis=dim), axis, forward
        )
        high = lax.ppermute(lax.slice_in_dim(block, 0, width, axis=dim), axis, backward)
        block = jnp.concatenate([low, block, high], axis=dim)
    return block


def wave_table(grid_x, grid_y, grid_z):
    number = jnp.arange(KX * KY * KZ, dtype=jnp.int32)
    index_x = (number // (KY * KZ) - KX // 2).astype(jnp.float32)
    index_y = (number // KZ % KY - KY // 2).astype(jnp.float32)
    index_z = (number % KZ - KZ // 2).astype(jnp.float32)
    waves = 2.0 * math.pi * jnp.stack([index_x / grid_x, index_y / grid_y, index_z / grid_z], 0)
    length_sq = jnp.sum(waves * waves, 0)
    weights = jnp.exp(-0.5 * length_sq) / (length_sq + 1.0)
    return (waves, weights)


def short_range(pos_ext, feat_ext, occupied, neighbours, w_radial, w_vector, w_mix, w_out):
    extent_x, extent_y, extent_z, slots_cell, channels = feat_ext.shape
    listed = neighbours.shape[-1]
    stencil = neighbours // slots_cell
    within = neighbours % slots_cell
    step_x = stencil // 9
    step_y = stencil // 3 % 3
    step_z = stencil % 3
    cell_x = lax.broadcasted_iota(jnp.int32, neighbours.shape, 0)
    cell_y = lax.broadcasted_iota(jnp.int32, neighbours.shape, 1)
    cell_z = lax.broadcasted_iota(jnp.int32, neighbours.shape, 2)
    target = (
        ((cell_x + step_x) * extent_y + cell_y + step_y) * extent_z + cell_z + step_z
    ) * slots_cell + within
    target = target.reshape(-1, listed)
    others = feat_ext.reshape(-1, channels)[target]
    points = jnp.moveaxis(pos_ext, 3, 4).reshape(-1, 3)
    centre = jnp.moveaxis(pos_ext[1:-1, 1:-1, 1:-1], 3, 4).reshape(-1, 1, 3)
    crossing = (
        jnp.stack([step_x - 1, step_y - 1, step_z - 1], -1)
        .reshape(-1, listed, 3)
        .astype(jnp.float32)
    )
    vectors = crossing + points[target] - centre
    dist_sq = jnp.sum(vectors * vectors, -1)
    envelope = (1.0 - dist_sq / 16.0) ** 2
    decays = 2.0 ** (jnp.arange(w_radial.shape[0], dtype=jnp.float32) - 4.0)
    basis = jnp.exp(-dist_sq[..., None] * decays)
    radial = jnp.einsum("akb,bc->akc", basis, w_radial, precision=HIGH) * envelope[..., None]
    angular = jnp.einsum("akb,bc->akc", basis, w_vector, precision=HIGH) * envelope[..., None]
    norm_scale = 1.0 / math.sqrt(listed)
    scalar = jnp.sum(radial * others, 1) * norm_scale
    vector = jnp.einsum("akd,akc->adc", vectors, angular * others, precision=HIGH) * norm_scale
    product = scalar + jnp.sum(vector * vector, 1)
    mixed = jnp.dot(product, w_mix, precision=HIGH)
    own = feat_ext[1:-1, 1:-1, 1:-1].reshape(-1, channels)
    updated = own + jax.nn.silu(mixed)
    return jnp.dot(updated, w_out, precision=HIGH) * occupied.reshape(-1)


def structure_terms(centres, charges, waves):
    phase = jnp.dot(centres, waves, precision=HIGH)
    cosine = jnp.cos(phase)
    sine = jnp.sin(phase)
    part_cos = jnp.dot(charges.T, cosine, precision=HIGH)
    part_sin = jnp.dot(charges.T, sine, precision=HIGH)
    return (cosine, sine, part_cos, part_sin)


def ewald_terms(cosine, sine, charges, total_cos, total_sin, waves, weights, scale):
    field_cos = jnp.dot(charges, total_cos * weights, precision=HIGH)
    field_sin = jnp.dot(charges, total_sin * weights, precision=HIGH)
    long_range = 0.5 * scale * jnp.sum(cosine * field_cos + sine * field_sin, 1)
    turning = scale * (cosine * field_sin - sine * field_cos)
    pull = jnp.dot(turning, waves.T, precision=HIGH)
    return (long_range, pull)


def rim_first(piece, direction):
    return shifted_2(piece, "gx", direction)


def rim_second(piece, direction):
    return shifted_2(piece, "gy", direction)


def rim_third(piece, direction):
    return shifted_2(piece, "gz", direction)


def fold(grads, axis_dim, mover):
    length = grads.shape[axis_dim]
    upper = lax.slice_in_dim(grads, length - 1, length, axis=axis_dim)
    lower = lax.slice_in_dim(grads, 0, 1, axis=axis_dim)
    arrived = []
    for direction in (1, -1):
        arrived.append(mover(upper if direction == 1 else lower, direction))
    inner = lax.slice_in_dim(grads, 1, length - 1, axis=axis_dim)
    size = length - 2
    head = lax.slice_in_dim(inner, 0, 1, axis=axis_dim) + arrived[0]
    tail = lax.slice_in_dim(inner, size - 1, size, axis=axis_dim) + arrived[1]
    middle = lax.slice_in_dim(inner, 1, size - 1, axis=axis_dim)
    return jnp.concatenate([head, middle, tail], axis_dim)


def body(
    features,
    offsets,
    counts,
    species,
    neighbours,
    w_radial,
    w_vector,
    w_mix,
    w_out,
    w_charge,
    species_shift,
):
    cells_x, cells_y, cells_z, slots_cell, channels = features.shape
    block_shape = (cells_x, cells_y, cells_z, slots_cell)
    occupied = (lax.broadcasted_iota(jnp.int32, block_shape, 3) < counts[..., None]).astype(
        jnp.float32
    )
    masked = features * occupied[..., None]
    charges = jnp.dot(masked.reshape(-1, channels), w_charge, precision=HIGH)
    grid_x = cells_x * lax.axis_size("gx")
    grid_y = cells_y * lax.axis_size("gy")
    grid_z = cells_z * lax.axis_size("gz")
    waves, weights = wave_table(grid_x, grid_y, grid_z)
    scale = 1.0 / math.sqrt(grid_x * grid_y * grid_z * slots_cell * KX * KY * KZ)
    place_x = lax.broadcasted_iota(jnp.int32, block_shape, 0) + lax.axis_index("gx") * cells_x
    place_y = lax.broadcasted_iota(jnp.int32, block_shape, 1) + lax.axis_index("gy") * cells_y
    place_z = lax.broadcasted_iota(jnp.int32, block_shape, 2) + lax.axis_index("gz") * cells_z
    centres = jnp.stack([place_x, place_y, place_z], -1).astype(jnp.float32) + jnp.moveaxis(
        offsets, 3, 4
    )
    cosine, sine, part_cos, part_sin = structure_terms(centres.reshape(-1, 3), charges, waves)
    total_cos, total_sin = lax.psum((part_cos, part_sin), ("gx", "gy", "gz"))
    feat_ext, pos_ext = (
        with_halo(masked, (("gx", 0), ("gy", 1), ("gz", 2)), 1),
        with_halo(offsets, (("gx", 0), ("gy", 1), ("gz", 2)), 1),
    )

    def local_total(moved):
        energies = short_range(
            moved, feat_ext, occupied, neighbours, w_radial, w_vector, w_mix, w_out
        )
        return (jnp.sum(energies), energies)

    _, backward, short = jax.vjp(local_total, pos_ext, has_aux=True)
    grad_ext = backward(jnp.float32(1.0))[0]
    grad_short = fold(fold(fold(grad_ext, 0, rim_first), 1, rim_second), 2, rim_third)
    long_range, pull = ewald_terms(
        cosine, sine, charges, total_cos, total_sin, waves, weights, scale
    )
    table = (species[..., None] == jnp.arange(species_shift.shape[0], dtype=jnp.int32)).astype(
        jnp.float32
    )
    shifted = jnp.dot(table.reshape(-1, species_shift.shape[0]), species_shift, precision=HIGH)
    atom_energy = (short + long_range + shifted * occupied.reshape(-1)).reshape(block_shape)
    pull_cells = jnp.moveaxis(pull.reshape(cells_x, cells_y, cells_z, slots_cell, 3), 4, 3)
    forces = -(grad_short + pull_cells)
    return (atom_energy, forces)


def solution(mesh):
    in_specs = (
        P("gx", "gy", "gz", None, None),
        P("gx", "gy", "gz", None, None),
        P("gx", "gy", "gz"),
        P("gx", "gy", "gz", None),
        P("gx", "gy", "gz", None, None),
        P(),
        P(),
        P(),
        P(),
        P(),
        P(),
    )
    out_specs = (P("gx", "gy", "gz", None), P("gx", "gy", "gz", None, None))
    return jax.shard_map(body, mesh=mesh, in_specs=in_specs, out_specs=out_specs, check_vma=False)
```

profile of v0, /device:TPU:1, one launch (start us, length us, event | category | flops | bytes accessed | tf_op | source)
XLA Modules:
  0.0 317.6 jit_solution(3093688207495036439)
XLA Ops:
  7.9 8.4 %collective-permute-start.1 = (f32[1,2,2,3,8]{4,2,3,1,0:T(2,128)S(1)}, f32[1,2,2,3,8]{4,2,3,1,0:T(2,128)S(1)}, u32[]{:S(2)}, u32[]{:S(2)}) collective-permute-start(f32[1,2,2,3,8]{4,2,3,1,0:T(2,128)S(1)} %get-tuple-element.42), channel_id=1, source_target_pairs={{32,0},{64,32},{96,64},{128,96},{160,128},{192,160},{224,192},{256... | collective-permute-start | bytes 1160 | tf_op jit(solution)/shard_map/ppermute | solution.py:31
  16.3 1.9 collective-permute-start
  19.1 1.9 collective-permute-start.6
  21.0 7.0 %collective-permute-start.7 = (f32[1,2,2,8,128]{4,3,2,1,0:T(8,128)S(1)}, f32[1,2,2,8,128]{4,3,2,1,0:T(8,128)S(1)}, u32[]{:S(2)}, u32[]{:S(2)}) collective-permute-start(f32[1,2,2,8,128]{4,3,2,1,0:T(8,128)S(1)} %get-tuple-element.33), channel_id=1, source_target_pairs={{32,0},{64,32},{96,64},{128,96},{160,128},{192,160},{224,192},{256... | collective-permute-start | bytes 49160 | tf_op jit(solution)/shard_map/ppermute | solution.py:31
  33.8 4.0 %collective-permute-start.2 = (f32[4,1,2,3,8]{4,2,3,1,0:T(2,128)S(1)}, f32[4,1,2,3,8]{4,2,3,1,0:T(2,128)S(1)}, u32[]{:S(2)}, u32[]{:S(2)}) collective-permute-start(f32[4,1,2,3,8]{4,2,3,1,0:T(2,128)S(1)} %get-tuple-element.40), channel_id=1, source_target_pairs={{0,4},{4,8},{8,12},{12,16},{16,20},{20,24},{24,28},{28,0},{1,5},{5... | collective-permute-start | bytes 2312 | tf_op jit(solution)/shard_map/ppermute | solution.py:28
  37.8 8.6 %collective-permute-start.3 = (f32[4,1,2,3,8]{4,2,3,1,0:T(2,128)S(1)}, f32[4,1,2,3,8]{4,2,3,1,0:T(2,128)S(1)}, u32[]{:S(2)}, u32[]{:S(2)}) collective-permute-start(f32[4,1,2,3,8]{4,2,3,1,0:T(2,128)S(1)} %get-tuple-element.41), channel_id=1, source_target_pairs={{4,0},{8,4},{12,8},{16,12},{20,16},{24,20},{28,24},{0,28},{5,1},{9... | collective-permute-start | bytes 2312 | tf_op jit(solution)/shard_map/ppermute | solution.py:31
  47.3 4.5 %collective-permute-start.4 = (f32[4,4,1,3,8]{4,2,3,1,0:T(1,128)S(1)}, f32[4,4,1,3,8]{4,2,3,1,0:T(1,128)S(1)}, u32[]{:S(2)}, u32[]{:S(2)}) collective-permute-start(f32[4,4,1,3,8]{4,2,3,1,0:T(1,128)S(1)} %get-tuple-element.28), channel_id=1, source_target_pairs={{0,1},{1,2},{2,3},{3,0},{4,5},{5,6},{6,7},{7,4},{8,9},{9,10},{10,1... | collective-permute-start | bytes 4616 | tf_op jit(solution)/shard_map/ppermute | solution.py:28
  51.7 1.9 collective-permute-start.5
  53.7 3.6 %collective-permute-done.5 = f32[4,4,1,3,8]{4,2,3,1,0:T(1,128)S(1)} collective-permute-done((f32[4,4,1,3,8]{4,2,3,1,0:T(1,128)S(1)}, f32[4,4,1,3,8]{4,2,3,1,0:T(1,128)S(1)}, u32[]{:S(2)}, u32[]{:S(2)}) %collective-permute-start.5) | collective-permute-done | bytes 1568 | tf_op jit(solution)/shard_map/ppermute | solution.py:31
  57.8 5.5 %gather_fusion = f32[2048,3]{1,0:T(8,128)S(1)} fusion(f32[512,3]{1,0:T(8,128)S(1)} %bitcast.80, s32[2048]{0:T(1024)S(1)} %broadcast_clamp_fusion), kind=kCustom, calls=%fused_computation | custom fusion | bytes 57344 | tf_op jit(solution)/shard_map/jvp()/gather | solution.py:70
  64.0 1.9 collective-permute-start.8
  66.0 4.7 %collective-permute-start.9 = (f32[4,1,2,8,128]{4,3,2,1,0:T(8,128)S(1)}, f32[4,1,2,8,128]{4,3,2,1,0:T(8,128)S(1)}, u32[]{:S(2)}, u32[]{:S(2)}) collective-permute-start(f32[4,1,2,8,128]{4,3,2,1,0:T(8,128)S(1)} %get-tuple-element.25), channel_id=1, source_target_pairs={{4,0},{8,4},{12,8},{16,12},{20,16},{24,20},{28,24},{0,28},{5,1},{9... | collective-permute-start | bytes 98312 | tf_op jit(solution)/shard_map/ppermute | solution.py:31
  71.8 2.8 collective-permute-start.10
  74.5 1.9 collective-permute-start.11
  76.5 1.9 fusion.21
  78.4 2.1 collective-permute-done.11
  80.6 5.6 %gather_fusion.1 = f32[2048,128]{1,0:T(8,128)S(1)} fusion(f32[512,128]{1,0:T(8,128)S(1)} %bitcast.79, s32[2048]{0:T(1024)S(1)} %broadcast_clamp_fusion), kind=kCustom, calls=%fused_computation.1 | custom fusion | bytes 2105344 | tf_op jit(solution)/shard_map/jvp()/gather | solution.py:62
  86.2 2.1 multiply_reduce_fusion.2
  90.8 2.0 multiply_reduce_fusion.1
  92.8 4.2 %fusion.9 = f32[64,32,8]{1,2,0:T(8,128)S(1)} fusion(f32[64,32,128]{2,1,0:T(8,128)S(1)} %get-tuple-element.54, f32[64,32]{1,0:T(8,128)S(1)} %get-tuple-element.30, f32[8,128]{1,0:T(8,128)S(1)} %copy-done.5), kind=kOutput, calls=%fused_computation.20 | convolution fusion | flops 25427968 | bytes 1126400 | tf_op jit(solution)/shard_map/transpose(jvp(akb,bc->akc))/dot_general | solution.py:76
  97.1 4.3 %fusion.2 = f32[64,32]{1,0:T(8,128)S(1)} fusion(f32[64,32,8]{1,2,0:T(8,128)S(1)} %fusion.9, f32[64,32,128]{2,1,0:T(8,128)S(1)} %bitcast.84, f32[64,128]{1,0:T(8,128)S(1)} %convolution_multiply_fusion.1, f32[64,32]{1,0:T(8,128)S(1)} %get-tuple-element.30, f32[8]{0:T(128)S(1)} %add_power_fusion, f32[64,32]{1,0:T(8,128)S(1)} %get-tuple-element.31, ...), kind=kOutput, calls=%fused_computation.7 | convolution fusion | flops 25769984 | bytes 1175584 | tf_op jit(solution)/shard_map/transpose(jvp(akb,bc->akc))/dot_general | solution.py:75
  101.3 1.9 fusion.108
  103.9 11.8 %scatter_custom_fusion = f32[512,3]{1,0:T(8,128)S(1)} fusion(s32[2048]{0:T(1024)S(1)} %reshape.261, f32[2048,3]{1,0:T(8,128)S(1)} %bitcast.89, f32[]{:T(128)} %constant.137.clone.1), kind=kCustom, calls=%fused_computation.45 | custom fusion | flops 6144 | bytes 6148 | tf_op jit(solution)/shard_map/transpose(jvp())/scatter-add | solution.py:70
  116.2 1.9 collective-permute-start.12
  118.2 6.5 %collective-permute-done.12 = f32[1,4,4,3,8]{4,2,1,0,3:T(4,128)S(1)} collective-permute-done((f32[1,4,4,3,8]{4,2,1,0,3:T(4,128)S(1)}, f32[1,4,4,3,8]{4,2,1,0,3:T(4,128)S(1)}, u32[]{:S(2)}, u32[]{:S(2)}) %collective-permute-start.12) | collective-permute-done | bytes 1568 | tf_op jit(solution)/shard_map/ppermute | solution.py:19
  124.8 1.9 collective-permute-start.13
  126.9 2.4 collective-permute-done.13
  129.4 4.0 %collective-permute-start.14 = (f32[2,1,4,3,8]{4,2,1,0,3:T(4,128)S(1)}, f32[2,1,4,3,8]{4,2,1,0,3:T(4,128)S(1)}, u32[]{:S(2)}, u32[]{:S(2)}) collective-permute-start(f32[2,1,4,3,8]{4,2,1,0,3:T(4,128)S(1)} %fusion.68), channel_id=1, source_target_pairs={{0,4},{4,8},{8,12},{12,16},{16,20},{20,24},{24,28},{28,0},{1,5},{5... | collective-permute-start | bytes 2312 | tf_op jit(solution)/shard_map/ppermute | solution.py:19
  133.4 161.6 %all-reduce.4.cloned.1.call-done = (f32[16,1024]{1,0:T(8,128)}, f32[16,1024]{1,0:T(8,128)}) async-done(((f32[16,1024]{1,0:T(8,128)}, f32[16,1024]{1,0:T(8,128)}), (f32[16,1024]{1,0:T(8,128)}, f32[16,1024]{1,0:T(8,128)})) %all-reduce.4.cloned.1.call-update) | async-done | bytes 131088 | tf_op jit(solution)/shard_map/psum | solution.py:164
  296.3 2.8 collective-permute-start.15
  300.8 3.0 collective-permute-start.16
  304.6 4.1 %collective-permute-start.17 = (f32[2,2,1,3,8]{4,2,1,0,3:T(1,128)S(1)}, f32[2,2,1,3,8]{4,2,1,0,3:T(1,128)S(1)}, u32[]{:S(2)}, u32[]{:S(2)}) collective-permute-start(f32[2,2,1,3,8]{4,2,1,0,3:T(1,128)S(1)} %get-tuple-element.39), channel_id=1, source_target_pairs={{0,3},{1,0},{2,1},{3,2},{4,7},{5,4},{6,5},{7,6},{8,11},{9,8},{10,9... | collective-permute-start | bytes 1160 | tf_op jit(solution)/shard_map/ppermute | solution.py:19
  (112 shorter events, 20.1 us)
Async XLA Ops:
  7.2 82.3 %copy-start = (f32[128,128]{1,0:T(8,128)S(1)}, f32[128,128]{1,0:T(8,128)}, u32[]{:S(2)}) copy-start(f32[128,128]{1,0:T(8,128)} %param.18) | copy-start | bytes 196612
  7.2 11.8 %copy-start.4 = (f32[2,2,2,8,128]{4,3,2,1,0:T(8,128)S(1)}, f32[2,2,2,8,128]{4,3,2,1,0:T(8,128)}, u32[]{:S(2)}) copy-start(f32[2,2,2,8,128]{4,3,2,1,0:T(8,128)} %param.11) | copy-start | bytes 98308
  7.2 287.8 %all-reduce.4.cloned.1.call-start = ((), (), s32[]{:S(2)}) async-start(), calls=%async_computation | async-start | bytes 262144 | tf_op jit(solution)/shard_map/psum | solution.py:164
  7.9 25.8 %collective-permute-start.1 = (f32[1,2,2,3,8]{4,2,3,1,0:T(2,128)S(1)}, f32[1,2,2,3,8]{4,2,3,1,0:T(2,128)S(1)}, u32[]{:S(2)}, u32[]{:S(2)}) collective-permute-start(f32[1,2,2,3,8]{4,2,3,1,0:T(2,128)S(1)} %get-tuple-element.42), channel_id=1, source_target_pairs={{32,0},{64,32},{96,64},{128,96},{160,128},{192,160},{224,192},{256... | collective-permute-start | bytes 1160 | tf_op jit(solution)/shard_map/ppermute | solution.py:31
  16.3 17.4 %collective-permute-start = (f32[1,2,2,3,8]{4,2,3,1,0:T(2,128)S(1)}, f32[1,2,2,3,8]{4,2,3,1,0:T(2,128)S(1)}, u32[]{:S(2)}, u32[]{:S(2)}) collective-permute-start(f32[1,2,2,3,8]{4,2,3,1,0:T(2,128)S(1)} %get-tuple-element.43), channel_id=1, source_target_pairs={{0,32},{32,64},{64,96},{96,128},{128,160},{160,192},{192,224},{224... | collective-permute-start | bytes 1160 | tf_op jit(solution)/shard_map/ppermute | solution.py:28
  19.1 44.9 %collective-permute-start.6 = (f32[1,2,2,8,128]{4,3,2,1,0:T(8,128)S(1)}, f32[1,2,2,8,128]{4,3,2,1,0:T(8,128)S(1)}, u32[]{:S(2)}, u32[]{:S(2)}) collective-permute-start(f32[1,2,2,8,128]{4,3,2,1,0:T(8,128)S(1)} %get-tuple-element.32), channel_id=1, source_target_pairs={{0,32},{32,64},{64,96},{96,128},{128,160},{160,192},{192,224},{224... | collective-permute-start | bytes 49160 | tf_op jit(solution)/shard_map/ppermute | solution.py:28
  21.0 43.0 %collective-permute-start.7 = (f32[1,2,2,8,128]{4,3,2,1,0:T(8,128)S(1)}, f32[1,2,2,8,128]{4,3,2,1,0:T(8,128)S(1)}, u32[]{:S(2)}, u32[]{:S(2)}) collective-permute-start(f32[1,2,2,8,128]{4,3,2,1,0:T(8,128)S(1)} %get-tuple-element.33), channel_id=1, source_target_pairs={{32,0},{64,32},{96,64},{128,96},{160,128},{192,160},{224,192},{256... | collective-permute-start | bytes 49160 | tf_op jit(solution)/shard_map/ppermute | solution.py:31
  28.1 0.7 copy-start.1
  28.8 0.7 copy-start.7
  32.7 0.8 copy-start.3
  33.8 12.8 %collective-permute-start.2 = (f32[4,1,2,3,8]{4,2,3,1,0:T(2,128)S(1)}, f32[4,1,2,3,8]{4,2,3,1,0:T(2,128)S(1)}, u32[]{:S(2)}, u32[]{:S(2)}) collective-permute-start(f32[4,1,2,3,8]{4,2,3,1,0:T(2,128)S(1)} %get-tuple-element.40), channel_id=1, source_target_pairs={{0,4},{4,8},{8,12},{12,16},{16,20},{20,24},{24,28},{28,0},{1,5},{5... | collective-permute-start | bytes 2312 | tf_op jit(solution)/shard_map/ppermute | solution.py:28
  37.8 9.4 %collective-permute-start.3 = (f32[4,1,2,3,8]{4,2,3,1,0:T(2,128)S(1)}, f32[4,1,2,3,8]{4,2,3,1,0:T(2,128)S(1)}, u32[]{:S(2)}, u32[]{:S(2)}) collective-permute-start(f32[4,1,2,3,8]{4,2,3,1,0:T(2,128)S(1)} %get-tuple-element.41), channel_id=1, source_target_pairs={{4,0},{8,4},{12,8},{16,12},{20,16},{24,20},{28,24},{0,28},{5,1},{9... | collective-permute-start | bytes 2312 | tf_op jit(solution)/shard_map/ppermute | solution.py:31
  47.3 6.5 %collective-permute-start.4 = (f32[4,4,1,3,8]{4,2,3,1,0:T(1,128)S(1)}, f32[4,4,1,3,8]{4,2,3,1,0:T(1,128)S(1)}, u32[]{:S(2)}, u32[]{:S(2)}) collective-permute-start(f32[4,4,1,3,8]{4,2,3,1,0:T(1,128)S(1)} %get-tuple-element.28), channel_id=1, source_target_pairs={{0,1},{1,2},{2,3},{3,0},{4,5},{5,6},{6,7},{7,4},{8,9},{9,10},{10,1... | collective-permute-start | bytes 4616 | tf_op jit(solution)/shard_map/ppermute | solution.py:28
  51.7 5.5 %collective-permute-start.5 = (f32[4,4,1,3,8]{4,2,3,1,0:T(1,128)S(1)}, f32[4,4,1,3,8]{4,2,3,1,0:T(1,128)S(1)}, u32[]{:S(2)}, u32[]{:S(2)}) collective-permute-start(f32[4,4,1,3,8]{4,2,3,1,0:T(1,128)S(1)} %get-tuple-element.29), channel_id=1, source_target_pairs={{1,0},{2,1},{3,2},{0,3},{5,4},{6,5},{7,6},{4,7},{9,8},{10,9},{11,1... | collective-permute-start | bytes 4616 | tf_op jit(solution)/shard_map/ppermute | solution.py:31
  64.0 6.7 %collective-permute-start.8 = (f32[4,1,2,8,128]{4,3,2,1,0:T(8,128)S(1)}, f32[4,1,2,8,128]{4,3,2,1,0:T(8,128)S(1)}, u32[]{:S(2)}, u32[]{:S(2)}) collective-permute-start(f32[4,1,2,8,128]{4,3,2,1,0:T(8,128)S(1)} %get-tuple-element.24), channel_id=1, source_target_pairs={{0,4},{4,8},{8,12},{12,16},{16,20},{20,24},{24,28},{28,0},{1,5},{5... | collective-permute-start | bytes 98312 | tf_op jit(solution)/shard_map/ppermute | solution.py:28
  66.0 5.7 %collective-permute-start.9 = (f32[4,1,2,8,128]{4,3,2,1,0:T(8,128)S(1)}, f32[4,1,2,8,128]{4,3,2,1,0:T(8,128)S(1)}, u32[]{:S(2)}, u32[]{:S(2)}) collective-permute-start(f32[4,1,2,8,128]{4,3,2,1,0:T(8,128)S(1)} %get-tuple-element.25), channel_id=1, source_target_pairs={{4,0},{8,4},{12,8},{16,12},{20,16},{24,20},{28,24},{0,28},{5,1},{9... | collective-permute-start | bytes 98312 | tf_op jit(solution)/shard_map/ppermute | solution.py:31
  71.7 4.7 %copy-start.5 = (f32[8,128]{1,0:T(8,128)S(1)}, f32[8,128]{1,0:T(8,128)}, u32[]{:S(2)}) copy-start(f32[8,128]{1,0:T(8,128)} %param.17) | copy-start | bytes 12292
  71.8 6.6 %collective-permute-start.10 = (f32[4,4,1,8,128]{4,3,2,1,0:T(8,128)S(1)}, f32[4,4,1,8,128]{4,3,2,1,0:T(8,128)S(1)}, u32[]{:S(2)}, u32[]{:S(2)}) collective-permute-start(f32[4,4,1,8,128]{4,3,2,1,0:T(8,128)S(1)} %get-tuple-element.20), channel_id=1, source_target_pairs={{0,1},{1,2},{2,3},{3,0},{4,5},{5,6},{6,7},{7,4},{8,9},{9,10},{10,1... | collective-permute-start | bytes 196616 | tf_op jit(solution)/shard_map/ppermute | solution.py:28
  74.5 6.0 %collective-permute-start.11 = (f32[4,4,1,8,128]{4,3,2,1,0:T(8,128)S(1)}, f32[4,4,1,8,128]{4,3,2,1,0:T(8,128)S(1)}, u32[]{:S(2)}, u32[]{:S(2)}) collective-permute-start(f32[4,4,1,8,128]{4,3,2,1,0:T(8,128)S(1)} %get-tuple-element.21), channel_id=1, source_target_pairs={{1,0},{2,1},{3,2},{0,3},{5,4},{6,5},{7,6},{4,7},{9,8},{10,9},{11,1... | collective-permute-start | bytes 196616 | tf_op jit(solution)/shard_map/ppermute | solution.py:31
  80.5 5.7 %copy-start.6 = (f32[8,128]{1,0:T(8,128)S(1)}, f32[8,128]{1,0:T(8,128)}, u32[]{:S(2)}) copy-start(f32[8,128]{1,0:T(8,128)} %param.16) | copy-start | bytes 12292
  89.5 0.7 copy-start.10
  116.2 2.0 copy-start.8
  116.2 8.6 %collective-permute-start.12 = (f32[1,4,4,3,8]{4,2,1,0,3:T(4,128)S(1)}, f32[1,4,4,3,8]{4,2,1,0,3:T(4,128)S(1)}, u32[]{:S(2)}, u32[]{:S(2)}) collective-permute-start(f32[1,4,4,3,8]{4,2,1,0,3:T(4,128)S(1)} %slice.120), channel_id=1, source_target_pairs={{0,32},{32,64},{64,96},{96,128},{128,160},{160,192},{192,224},{224... | collective-permute-start | bytes 4616 | tf_op jit(solution)/shard_map/ppermute | solution.py:19
  124.7 1.9 copy-start.9
  124.8 4.6 %collective-permute-start.13 = (f32[1,4,4,3,8]{4,2,1,0,3:T(4,128)S(1)}, f32[1,4,4,3,8]{4,2,1,0,3:T(4,128)S(1)}, u32[]{:S(2)}, u32[]{:S(2)}) collective-permute-start(f32[1,4,4,3,8]{4,2,1,0,3:T(4,128)S(1)} %get-tuple-element.23), channel_id=1, source_target_pairs={{0,480},{32,0},{64,32},{96,64},{128,96},{160,128},{192,160},{224,1... | collective-permute-start | bytes 4616 | tf_op jit(solution)/shard_map/ppermute | solution.py:19
  129.4 166.9 %collective-permute-start.14 = (f32[2,1,4,3,8]{4,2,1,0,3:T(4,128)S(1)}, f32[2,1,4,3,8]{4,2,1,0,3:T(4,128)S(1)}, u32[]{:S(2)}, u32[]{:S(2)}) collective-permute-start(f32[2,1,4,3,8]{4,2,1,0,3:T(4,128)S(1)} %fusion.68), channel_id=1, source_target_pairs={{0,4},{4,8},{8,12},{12,16},{16,20},{20,24},{24,28},{28,0},{1,5},{5... | collective-permute-start | bytes 2312 | tf_op jit(solution)/shard_map/ppermute | solution.py:19
  296.3 2.8 copy-start.2
  296.3 4.4 %collective-permute-start.15 = (f32[2,1,4,3,8]{4,2,1,0,3:T(4,128)S(1)}, f32[2,1,4,3,8]{4,2,1,0,3:T(4,128)S(1)}, u32[]{:S(2)}, u32[]{:S(2)}) collective-permute-start(f32[2,1,4,3,8]{4,2,1,0,3:T(4,128)S(1)} %get-tuple-element.27), channel_id=1, source_target_pairs={{0,28},{4,0},{8,4},{12,8},{16,12},{20,16},{24,20},{28,24},{1,29},{... | collective-permute-start | bytes 2312 | tf_op jit(solution)/shard_map/ppermute | solution.py:19
  300.8 3.8 %collective-permute-start.16 = (f32[2,2,1,3,8]{4,2,1,0,3:T(1,128)S(1)}, f32[2,2,1,3,8]{4,2,1,0,3:T(1,128)S(1)}, u32[]{:S(2)}, u32[]{:S(2)}) collective-permute-start(f32[2,2,1,3,8]{4,2,1,0,3:T(1,128)S(1)} %fusion.75), channel_id=1, source_target_pairs={{0,1},{1,2},{2,3},{3,0},{4,5},{5,6},{6,7},{7,4},{8,9},{9,10},{10,1... | collective-permute-start | bytes 1160 | tf_op jit(solution)/shard_map/ppermute | solution.py:19
  304.6 5.5 %collective-permute-start.17 = (f32[2,2,1,3,8]{4,2,1,0,3:T(1,128)S(1)}, f32[2,2,1,3,8]{4,2,1,0,3:T(1,128)S(1)}, u32[]{:S(2)}, u32[]{:S(2)}) collective-permute-start(f32[2,2,1,3,8]{4,2,1,0,3:T(1,128)S(1)} %get-tuple-element.39), channel_id=1, source_target_pairs={{0,3},{1,0},{2,1},{3,2},{4,7},{5,4},{6,5},{7,6},{8,11},{9,8},{10,9... | collective-permute-start | bytes 1160 | tf_op jit(solution)/shard_map/ppermute | solution.py:19
Sparse Core Ops, SparseCore 0:
  32.9 262.0 all-reduce.3
where the time goes:
time: 319 us; the launch traced here: 318 us
  waiting for transfers between devices  180 us (56%)
  starting transfers between devices  67.3 us (21%)
  matrix products  23.7 us (7%)
  local copies, waits for them, and re-layouts  18.3 us (6%)
  between operations  14.7 us (5%)
  other arithmetic  13.8 us (4%)
    psum x1, waiting for transfers between devices, body(): total_cos, total_sin = lax.psum((part_cos, part_sin), ('gx', 'gy', 'gz'))  162 us
    ppermute x6, starting transfers between devices, with_halo(): lax.ppermute(lax.slice_in_dim(block, 0, width, axis=dim), axis, backward)  32.5 us
    ppermute x6, starting transfers between devices, shifted_2(): return lax.ppermute(value, axis, pairs)  17.7 us
    ppermute x6, starting transfers between devices, with_halo(): lax.ppermute(lax.slice_in_dim(block, block.shape[dim] - width, None, axis...  17 us
    scatter-add x1, other arithmetic, short_range(): vectors = crossing + points[target] - centre  11.8 us
    ppermute x6, waiting for transfers between devices, shifted_2(): return lax.ppermute(value, axis, pairs)  10.9 us
    ppermute x6, waiting for transfers between devices, with_halo(): lax.ppermute(lax.slice_in_dim(block, 0, width, axis=dim), axis, backward)  7.24 us
  transfers between devices with their start and end apart: 19, of which 10 were waited for; matrix products, arithmetic and copies ran while one was open for 16% of the time, Pallas kernels for 0%

commit v1 on v0

v1 whole, which is shorter than its diff:
```python
import math

import jax
import jax.numpy as jnp
from jax import lax
from jax.experimental import pallas as pl
from jax.experimental.pallas import tpu as pltpu
from jax.sharding import PartitionSpec as P

KX = 16
KY = 8
KZ = 8
MODES = KX * KY * KZ
HIGH = lax.Precision.HIGHEST
F32 = jnp.float32
BF16 = jnp.bfloat16
PARAMS = pltpu.CompilerParams(vmem_limit_bytes=48 * 1024 * 1024)


def iota(shape, dim):
    return lax.broadcasted_iota(jnp.int32, shape, dim)


def split(value):
    high = value.astype(BF16)
    low = (value - high.astype(F32)).astype(BF16)
    return high, low


def contract(left, right, dims, precision=None):
    return lax.dot_general(
        left, right, (dims, ((), ())), precision=precision, preferred_element_type=F32
    )


def swap_halves(value):
    return pltpu.roll(value, 64, value.ndim - 1)


def pack_kernel(feat_ref, pos_ref, count_ref, near_ref, charge_ref, slab_ref, rest_ref, message_ref):
    row = iota((64, 128), 0)
    lane = iota((8, 128), 1)
    count_col = jnp.zeros((64, 128), jnp.int32)
    count_row = jnp.zeros((8, 128), jnp.int32)
    for cell in range(8):
        count = count_ref[cell // 4][cell // 2 % 2 : cell // 2 % 2 + 1, cell % 2 : cell % 2 + 1]
        count_col = jnp.where(row // 8 == cell, count, count_col)
        count_row = jnp.where(lane // 8 == cell, count, count_row)
    occupied = (row % 8 < count_col).astype(F32)
    occupied_row = (lane % 8 < count_row).astype(F32)
    masked = feat_ref[...] * occupied
    charges = contract(
        charge_ref[...], jnp.concatenate([masked, masked], 0), (((1,), (1,))), HIGH
    )
    spots = pos_ref[...]
    sub = iota((8, 128), 0)
    tile = jnp.concatenate([spots, jnp.zeros((5, 64), F32)], 0)
    tile = jnp.concatenate([tile, jnp.zeros((8, 64), F32)], 1)
    tile = jnp.where(sub == 3, occupied_row, tile)
    cell_x, cell_y, cell_z = lane // 32 % 2, lane // 16 % 2, lane // 8 % 2
    corner_x = 2 * lax.axis_index("gx")
    corner_y = 2 * lax.axis_index("gy")
    corner_z = 2 * lax.axis_index("gz")
    corner = jnp.where(
        sub == 0, cell_x + corner_x, jnp.where(sub == 1, cell_y + corner_y, cell_z + corner_z)
    )
    places = tile + corner.astype(F32)
    lane_low = lane < 64
    message = jnp.concatenate(
        [jnp.where(lane_low, charges[0:8], charges[8:16]), places], 0
    )
    for member in range(message_ref.shape[0]):
        message_ref[member] = message
    turned = jnp.concatenate(
        [jnp.zeros((32, 128), F32), tile, jnp.zeros((88, 128), F32)], 0
    ).T
    near = near_ref[...]
    atom = iota((64, 32), 0)
    stencil = near >> 3
    slot = near & 7
    step_x = (stencil * 57) >> 9
    line = (stencil * 171) >> 9
    step_z = stencil - 3 * line
    step_y = line - 3 * step_x
    spot_x = step_x + 1 - ((atom >> 5) & 1)
    spot_y = step_y + 1 - ((atom >> 4) & 1)
    spot_z = step_z + 1 - ((atom >> 3) & 1)
    block = (spot_z >> 1) * 4 + (spot_y >> 1) * 2 + (spot_x >> 1)
    cell = (spot_x & 1) * 4 + (spot_y & 1) * 2 + (spot_z & 1)
    target = (block * 64 + cell * 8 + slot).astype(F32)
    slab_ref[0:64] = masked
    slab_ref[64:72] = tile
    slab_ref[72:104] = turned[0:32]
    slab_ref[72:104, 0:32] = target[0:32]
    rest_ref[...] = turned[32:64]
    rest_ref[:, 0:32] = target[32:64]


def wave_numbers(member, shape, dim):
    index = iota(shape, dim) % 32
    number_y = (index // 8 + (member % 2) * 4 - KY // 2).astype(F32)
    number_z = (index % 8 - KZ // 2).astype(F32)
    number_x = (member // 2 - KX // 2).astype(F32)
    return number_x, number_y, number_z


def sine_cosine(turns):
    part = turns - jnp.floor(turns + 0.5)
    angle = part * (2.0 * math.pi)
    square = angle * angle
    sine = jnp.full_like(square, 1.0 / math.factorial(19) * -1.0)
    for power in range(17, 0, -2):
        sign = 1.0 if power // 2 % 2 == 0 else -1.0
        sine = sine * square + sign / math.factorial(power)
    cosine = jnp.full_like(square, -1.0 / math.factorial(18))
    for power in range(16, -1, -2):
        sign = 1.0 if power // 2 % 2 == 0 else -1.0
        cosine = cosine * square + sign / math.factorial(power)
    return sine * angle, cosine


def waves_kernel(grid, atoms_ref, message_ref, phase_ref, charge_ref):
    member = lax.axis_index("gy") * 4 + lax.axis_index("gz")
    low = iota((8, 128), 1) < 64
    upper, lower, places = [], [], []
    for pair in range(16):
        first, second = atoms_ref[2 * pair], atoms_ref[2 * pair + 1]
        turned_first, turned_second = swap_halves(first), swap_halves(second)
        upper.append(jnp.where(low, first[0:8], turned_second[0:8]))
        lower.append(jnp.where(low, turned_first[0:8], second[0:8]))
        places.append(jnp.where(low, first[8:16], turned_second[8:16]))
    charges = jnp.concatenate(
        [jnp.concatenate(upper, 1), jnp.concatenate(lower, 1)], 0
    )
    places = jnp.concatenate(places, 1)
    number_x, number_y, number_z = wave_numbers(member, (32, 1), 0)
    turns = (
        number_x * (places[0:1] * (1.0 / grid[0]))
        + number_y * (places[1:2] * (1.0 / grid[1]))
        + number_z * (places[2:3] * (1.0 / grid[2]))
    )
    sine, cosine = sine_cosine(turns)
    phases = jnp.concatenate([cosine, sine], 0)
    phase_ref[...] = phases
    charge_ref[...] = charges
    charge_stack = jnp.concatenate(split(charges), 0)
    phase_stack = jnp.concatenate(split(phases), 0)
    sums = contract(charge_stack, phase_stack, (((1,), (1,))))
    partial = sums[0:16] + sums[16:32]
    for other in range(message_ref.shape[0]):
        message_ref[other] = partial


def field_kernel(grid, scale, sums_ref, phase_ref, charge_ref, kept_ref, came_ref, out_ref):
    at_y, at_z = lax.axis_index("gy"), lax.axis_index("gz")
    member = at_y * 4 + at_z
    total = sums_ref[0]
    for other in range(1, sums_ref.shape[0]):
        total = total + sums_ref[other]
    total = total + swap_halves(total)
    two_pi = 2.0 * math.pi
    number_x, number_y, number_z = wave_numbers(member, (16, 128), 1)
    wave_x, wave_y, wave_z = (
        number_x * (two_pi / grid[0]),
        number_y * (two_pi / grid[1]),
        number_z * (two_pi / grid[2]),
    )
    length_sq = wave_x * wave_x + wave_y * wave_y + wave_z * wave_z
    total = total * (jnp.exp(-0.5 * length_sq) / (length_sq + 1.0))
    high = total.astype(BF16).astype(F32)
    low = total - high
    left = jnp.concatenate([high, low, high, jnp.zeros((80, 128), F32)], 0).T[0:64, 0:64]
    charge_high, charge_low = split(charge_ref[...])
    right = jnp.concatenate(
        [charge_high, charge_high, charge_low, jnp.zeros_like(charge_low)], 0
    )
    fields = contract(left.astype(BF16), right, (((1,), (0,))))
    cosine, sine = phase_ref[0:32], phase_ref[32:64]
    field_cos, field_sin = fields[0:32], fields[32:64]
    energy = (0.5 * scale) * jnp.sum(cosine * field_cos + sine * field_sin, 0, keepdims=True)
    turning = scale * (cosine * field_sin - sine * field_cos)
    number_x, number_y, number_z = wave_numbers(member, (32, 1), 0)
    pull_x = (number_x * (two_pi / grid[0])) * jnp.sum(turning, 0, keepdims=True)
    pull_y = jnp.sum(turning * (number_y * (two_pi / grid[1])), 0, keepdims=True)
    pull_z = jnp.sum(turning * (number_z * (two_pi / grid[2])), 0, keepdims=True)
    rows = jnp.concatenate([energy, pull_x, pull_y, pull_z], 0)
    for target in range(32):
        out_ref[target] = rows[:, target // 2 * 128 : target // 2 * 128 + 128]
    half = iota((4, 128), 1) // 64
    for block in range(4):
        by, bz = block % 2, block // 2
        to_z = (at_z + bz) % 4
        to = ((at_y + by) % 8) * 4 + to_z
        folded = kept_ref[block] + came_ref[block]
        out_ref[to] = out_ref[to] + jnp.where(half == to_z % 2, folded, 0.0)


def short_kernel(
    own_ref, rest_ref, in_x_ref, in_y_ref, in_z_ref,
    radial_ref, vector_ref, mix_ref, out_weight_ref, kept_ref, sent_ref,
):
    bases = [
        (own_ref, 0), (in_x_ref, 0), (in_y_ref, 0), (in_y_ref, 72),
        (in_z_ref, 0), (in_z_ref, 72), (in_z_ref, 144), (in_z_ref, 216),
    ]
    feats = jnp.concatenate([ref[at : at + 64] for ref, at in bases], 0)
    low_lane = iota((8, 128), 1) < 64
    spots = []
    for pair in range(4):
        (ref_a, at_a), (ref_b, at_b) = bases[2 * pair], bases[2 * pair + 1]
        spots.append(
            jnp.where(
                low_lane,
                ref_a[at_a + 64 : at_a + 72],
                swap_halves(ref_b[at_b + 64 : at_b + 72]),
            )
        )
    spots = jnp.concatenate(spots, 1)
    tiles = [
        rest_ref[24:32], in_x_ref[96:104], in_y_ref[152:160], in_y_ref[168:176],
        in_z_ref[288:296], in_z_ref[296:304], in_z_ref[304:312], in_z_ref[312:320],
    ]
    centres = jnp.concatenate(tiles, 0)
    own = []
    for unit in range(8):
        ux, uy, uz = unit % 2, unit // 2 % 2, unit // 4
        ref, at = bases[unit]
        at = at + ((1 - ux) * 4 + (1 - uy) * 2 + (1 - uz)) * 8
        own.append(ref[at : at + 8])
    own = jnp.concatenate(own, 0)
    occupied = centres[:, 35:36]
    lane = iota((1, 512), 1)
    block = lane // 64
    cell = lane // 8 % 8
    spot = (
        spots[0:1] + ((block % 2) * 2 + cell // 4).astype(F32),
        spots[1:2] + ((block // 2 % 2) * 2 + cell // 2 % 2).astype(F32),
        spots[2:3] + ((block // 4) * 2 + cell % 2).astype(F32),
    )
    atom = iota((64, 1), 0)
    unit = atom // 8
    middle = (
        centres[:, 32:33] + (unit % 2 + 1).astype(F32),
        centres[:, 33:34] + (unit // 2 % 2 + 1).astype(F32),
        centres[:, 34:35] + (unit // 4 + 1).astype(F32),
    )
    delta = [spot[a] - middle[a] for a in range(3)]
    dist_sq = delta[0] * delta[0] + delta[1] * delta[1] + delta[2] * delta[2]
    near = 1.0 - dist_sq * (1.0 / 16.0)
    envelope = near * near
    lane_f = iota((64, 512), 1).astype(F32)
    times = jnp.zeros((64, 512), F32)
    for entry in range(32):
        times = times + jnp.where(centres[:, entry : entry + 1] == lane_f, 1.0, 0.0)
    bases_m = []
    power = None
    for b in range(8):
        if b % 4 == 0:
            power = jnp.exp(dist_sq * (-(2.0 ** (b - 4))))
        else:
            power = power * power
        bases_m.append(power * times)
    feat_high, feat_low = split(feats)
    feat_both = jnp.concatenate([feat_high, feat_low], 1)
    norm = 1.0 / math.sqrt(32.0)
    sums = [jnp.zeros((64, 128), F32) for _ in range(4)]
    for b in range(8):
        weight = bases_m[b] * envelope
        left = jnp.concatenate([weight] + [weight * delta[a] for a in range(3)], 0)
        left_high, left_low = split(left)
        first = contract(left_high, feat_both, (((1,), (0,))))
        second = contract(left_low, feat_high, (((1,), (0,))))
        made = first[:, 0:128] + first[:, 128:256] + second
        sums[0] = sums[0] + made[0:64] * radial_ref[b : b + 1]
        for a in range(3):
            sums[1 + a] = sums[1 + a] + made[64 * (1 + a) : 64 * (2 + a)] * vector_ref[b : b + 1]
    sums = [value * norm for value in sums]
    product = sums[0] + sums[1] * sums[1] + sums[2] * sums[2] + sums[3] * sums[3]
    mixed = contract(product, mix_ref[...], (((1,), (0,))), HIGH)
    gate = 1.0 / (1.0 + jnp.exp(-mixed))
    out_weight = out_weight_ref[...]
    energy = jnp.sum((own + mixed * gate) * out_weight, 1, keepdims=True) * occupied
    slope = gate * (1.0 + mixed * (1.0 - gate)) * (out_weight * occupied)
    grad = contract(slope, mix_ref[...], (((1,), (1,))), HIGH) * norm
    grads = [grad] + [2.0 * grad * sums[1 + a] for a in range(3)]
    right = jnp.concatenate([feat_high, feat_high, feat_low], 1)
    linear = [jnp.zeros((64, 512), F32) for _ in range(3)]
    plain = jnp.zeros((64, 512), F32)
    decayed = jnp.zeros((64, 512), F32)
    for b in range(8):
        left = jnp.concatenate(
            [grads[0] * radial_ref[b : b + 1]]
            + [grads[1 + a] * vector_ref[b : b + 1] for a in range(3)],
            0,
        )
        left_high, left_low = split(left)
        pulled = contract(
            jnp.concatenate([left_high, left_low, left_high], 1), right, (((1,), (1,)))
        )
        parts = [pulled[64 * (1 + a) : 64 * (2 + a)] for a in range(3)]
        full = pulled[0:64] + parts[0] * delta[0] + parts[1] * delta[1] + parts[2] * delta[2]
        weighted = bases_m[b] * full
        plain = plain + weighted
        decayed = decayed + weighted * (2.0 ** (b - 4))
        for a in range(3):
            linear[a] = linear[a] + bases_m[b] * parts[a]
    radial_slope = 2.0 * (near * (-0.125) * plain - envelope * decayed)
    lane_i = iota((64, 512), 1)
    row_i = iota((64, 512), 0)
    ux, uy, uz = row_i // 8 % 2, row_i // 16 % 2, row_i // 32
    self_at = (row_i // 8) * 64 + ((1 - ux) * 4 + (1 - uy) * 2 + (1 - uz)) * 8 + row_i % 8
    own_slot = lane_i == self_at
    rows = [jnp.sum(jnp.where(own_slot, energy, 0.0), 0, keepdims=True)]
    for a in range(3):
        push = envelope * linear[a] + delta[a] * radial_slope
        back = jnp.sum(push, 1, keepdims=True)
        rows.append(jnp.sum(push - jnp.where(own_slot, back, 0.0), 0, keepdims=True))
    rows = jnp.concatenate(rows, 0)
    low = iota((4, 128), 1) < 64
    for k in range(4):
        piece = rows[:, 128 * k : 128 * k + 128]
        turned = swap_halves(piece)
        kept_ref[k] = jnp.where(low, piece, turned)
        sent_ref[k] = jnp.where(low, turned, piece)


def sum_kernel(parts_ref, out_ref):
    total = parts_ref[0]
    for member in range(1, parts_ref.shape[0]):
        total = total + parts_ref[member]
    odd = lax.axis_index("gz") % 2
    total = jnp.where(odd == 1, swap_halves(total), total)
    out_ref[...] = total


def call(kernel, out, *operands):
    return pl.pallas_call(
        kernel,
        out_shape=[jax.ShapeDtypeStruct(shape, F32) for shape in out],
        compiler_params=PARAMS,
    )(*operands)


def moved(value, axis, steps):
    count = lax.axis_size(axis)
    return lax.ppermute(value, axis, [(i, (i + steps) % count) for i in range(count)])


def body(
    features, offsets, counts, species, neighbours,
    w_radial, w_vector, w_mix, w_out, w_charge, species_shift,
):
    cells_x, cells_y, cells_z, slots_cell, channels = features.shape
    block_shape = (cells_x, cells_y, cells_z, slots_cell)
    grid = (
        cells_x * lax.axis_size("gx"),
        cells_y * lax.axis_size("gy"),
        cells_z * lax.axis_size("gz"),
    )
    scale = 1.0 / math.sqrt(grid[0] * grid[1] * grid[2] * slots_cell * MODES)
    spots = jnp.transpose(offsets, (3, 0, 1, 2, 4)).reshape(3, 64)
    slab, rest, message = call(
        pack_kernel,
        [(104, 128), (32, 128), (32, 16, 128)],
        features.reshape(64, 128),
        spots,
        counts,
        neighbours.reshape(64, 32),
        w_charge.T,
    )
    in_x = moved(slab, "gx", -1)
    atoms = lax.all_to_all(message, ("gy", "gz"), 0, 0)
    in_y = moved(
        jnp.concatenate([slab[0:72], in_x[0:72], rest[0:16], in_x[72:88]], 0), "gy", -1
    )
    partial, phases, charges = call(
        lambda *refs: waves_kernel(grid, *refs),
        [(16, 16, 128), (64, 2048), (16, 2048)],
        atoms,
    )
    sums = lax.all_to_all(partial, "gx", 0, 0)
    in_z = moved(
        jnp.concatenate(
            [
                slab[0:72], in_x[0:72], in_y[0:144],
                rest[16:24], in_x[88:96], in_y[144:152], in_y[160:168],
            ],
            0,
        ),
        "gz",
        -1,
    )
    kept, sent = call(
        short_kernel,
        [(4, 4, 128), (4, 4, 128)],
        slab, rest, in_x, in_y, in_z, w_radial, w_vector, w_mix, w_out.reshape(1, 128),
    )
    came = moved(sent, "gx", 1)
    (parts,) = call(
        lambda *refs: field_kernel(grid, scale, *refs),
        [(32, 4, 128)],
        sums, phases, charges, kept, came,
    )
    (rows,) = call(sum_kernel, [(4, 128)], lax.all_to_all(parts, ("gy", "gz"), 0, 0))
    table = species[..., None] == jnp.arange(species_shift.shape[0], dtype=jnp.int32)
    shifted = jnp.sum(jnp.where(table, species_shift, 0.0), -1)
    occupied = iota(block_shape, 3) < counts[..., None]
    atom_energy = rows[0, 0:64].reshape(block_shape) + jnp.where(occupied, shifted, 0.0)
    forces = -rows[1:4, 0:64].reshape((3,) + block_shape)
    return (atom_energy, jnp.transpose(forces, (1, 2, 3, 0, 4)))


def solution(mesh):
    spread = P("gx", "gy", "gz")
    in_specs = (spread,) * 5 + (P(),) * 6
    return jax.shard_map(
        body, mesh=mesh, in_specs=in_specs, out_specs=(spread, spread), check_vma=False
    )
```

time: 319 us -> 85.3 us (0.27)
  waiting for transfers between devices: 180 us -> 29.8 us
  starting transfers between devices: 67.3 us -> 42.2 us
  matrix products: 23.7 us -> 0 us
  local copies, waits for them, and re-layouts: 18.3 us -> 3.11 us
  between operations: 14.7 us -> 0.84 us
  other arithmetic: 13.8 us -> 0.84 us
  Pallas kernels: 0 us -> 7.78 us
    psum x1 -> x0, waiting for transfers between devices: 162 us -> none  [body(): total_cos, total_sin = lax.psum((part_cos, part_sin), ('gx', 'gy', 'gz'))]
    ppermute x18 -> x4, starting transfers between devices: 67.2 us -> 25.9 us  [moved(): lax.ppermute(value, axis, [(i, (i + steps) % count) for i in range(count)])]
    dot_general x18 -> x0, matrix products: 23.7 us -> none  [the longest x2 6.37 us: short_range(): jnp.einsum('akb,bc->akc', basis, w_radial, precision=HIGH)]
    all_to_all x0 -> x3, waiting for transfers between devices: none -> 19.5 us  [the longest x1 11.4 us: body(): atoms = lax.all_to_all(message, ('gy', 'gz'), 0, 0)]
    all_to_all x0 -> x3, starting transfers between devices: none -> 16.3 us  [the longest x1 7.2 us: body(): sums = lax.all_to_all(partial, 'gx', 0, 0)]
    scatter-add x1 -> x0, other arithmetic: 11.8 us -> none  [short_range(): vectors = crossing + points[target] - centre]
    gather x3 -> x0, local copies, waits for them, and re-layouts: 11.6 us -> none  [the longest x2 5.91 us: short_range(): vectors = crossing + points[target] - centre]
    ppermute x18 -> x4, waiting for transfers between devices: 18.2 us -> 10.3 us  [moved(): lax.ppermute(value, axis, [(i, (i + steps) % count) for i in range(count)])]
  transfers between devices with their start and end apart: 19 -> 7, of which waited for: 10 -> 5; matrix products, arithmetic and copies ran while one was open for 16% -> 0% of each run, Pallas kernels for 0% -> 5%
where the time goes in v1:
time: 85.3 us; the launch traced here: 84.6 us
  starting transfers between devices  42.2 us (49%)
  waiting for transfers between devices  29.8 us (35%)
  Pallas kernels  7.78 us (9%)
  local copies, waits for them, and re-layouts  3.11 us (4%)
    ppermute x4, starting transfers between devices, moved(): lax.ppermute(value, axis, [(i, (i + steps) % count) for i in range(count)])  25.9 us
    all_to_all x1, waiting for transfers between devices, body(): atoms = lax.all_to_all(message, ('gy', 'gz'), 0, 0)  11.4 us
    ppermute x4, waiting for transfers between devices, moved(): lax.ppermute(value, axis, [(i, (i + steps) % count) for i in range(count)])  10.3 us
    all_to_all x1, waiting for transfers between devices, body(): lax.all_to_all(parts, ('gy', 'gz'), 0, 0)  8.13 us
    pallas_call x5, Pallas kernels, call(): pl.pallas_call(kernel, out_shape=[jax.ShapeDtypeStruct(shape, F32) for sh...  7.78 us
    all_to_all x1, starting transfers between devices, body(): sums = lax.all_to_all(partial, 'gx', 0, 0)  7.2 us
    all_to_all x1, starting transfers between devices, body(): atoms = lax.all_to_all(message, ('gy', 'gz'), 0, 0)  5.34 us
    all_to_all x1, starting transfers between devices, body(): lax.all_to_all(parts, ('gy', 'gz'), 0, 0)  3.77 us
  transfers between devices with their start and end apart: 7, of which 5 were waited for; matrix products, arithmetic and copies ran while one was open for 0% of the time, Pallas kernels for 5%

profile of v1, /device:TPU:1, one launch (start us, length us, event | category | flops | bytes accessed | tf_op | source)
XLA Modules:
  0.0 84.6 jit_solution(5659503150439956772)
XLA Ops:
  0.6 0.7 copy.15
  1.4 0.1 reshape.21.pos_ref
  1.5 0.6 copy-done.3
  2.1 0.1 copy-done.4
  2.1 0.8 copy-done.2
  2.9 1.0 %shard_map.122 = (f32[104,128]{1,0:T(8,128)S(1)}, f32[32,128]{1,0:T(8,128)S(1)}, f32[32,16,128]{2,1,0:T(8,128)}) custom-call(f32[64,128]{1,0:T(8,128)S(1)} %bitcast.8, f32[3,64]{1,0:T(4,128)S(1)} %reshape.21.pos_ref, s32[2,2,2]{2,1,0:T(2,128)S(1)} %copy-done.4, s32[64,32]{1,0:T(8,128)S(1)} %bitcast.9, f32[16,128]{1,0:T(8,128)S(1)} %bitcast.10), custom_call_target="tpu_custom_call" | custom-call | tf_op jit(solution)/shard_map/pallas_call | solution.py:337
  3.9 8.4 %collective-permute-start = (f32[104,128]{1,0:T(8,128)S(1)}, f32[104,128]{1,0:T(8,128)S(1)}, u32[]{:S(2)}, u32[]{:S(2)}) collective-permute-start(f32[104,128]{1,0:T(8,128)S(1)} %get-tuple-element.14.own_ref), channel_id=1, source_target_pairs={{0,480},{32,0},{64,32},{96,64},{128,96},{160,128},{192,160},{224,1... | collective-permute-start | bytes 159752 | tf_op jit(solution)/shard_map/ppermute | solution.py:346
  12.3 1.2 %collective-permute-done.in_x_ref = f32[104,128]{1,0:T(8,128)S(1)} collective-permute-done((f32[104,128]{1,0:T(8,128)S(1)}, f32[104,128]{1,0:T(8,128)S(1)}, u32[]{:S(2)}, u32[]{:S(2)}) %collective-permute-start) | collective-permute-done | bytes 53280 | tf_op jit(solution)/shard_map/ppermute | solution.py:346
  13.5 10.7 %collective-permute-start.1 = (f32[176,128]{1,0:T(8,128)S(1)}, f32[176,128]{1,0:T(8,128)S(1)}, u32[]{:S(2)}, u32[]{:S(2)}) collective-permute-start(f32[176,128]{1,0:T(8,128)S(1)} %pad_maximum_fusion), channel_id=1, source_target_pairs={{0,28},{4,0},{8,4},{12,8},{16,12},{20,16},{24,20},{28,24},{1,29},{... | collective-permute-start | bytes 270344 | tf_op jit(solution)/shard_map/ppermute | solution.py:346
  24.2 5.3 %all-to-all-start = ((f32[32,16,128]{2,1,0:T(8,128)}), f32[32,16,128]{2,1,0:T(8,128)S(1)}, u32[]{:S(2)}, u32[]{:S(2)}) async-start(f32[32,16,128]{2,1,0:T(8,128)} %get-tuple-element.10), calls=%async_computation | async-start | bytes 524288 | tf_op jit(solution)/shard_map/all_to_all | solution.py:372
  29.5 0.0 collective-permute-done.1.in_y_ref
  29.6 11.4 %all-to-all-done.refs_0_ = f32[32,16,128]{2,1,0:T(8,128)S(1)} async-done(((f32[32,16,128]{2,1,0:T(8,128)}), f32[32,16,128]{2,1,0:T(8,128)S(1)}, u32[]{:S(2)}, u32[]{:S(2)}) %all-to-all-start) | async-done | bytes 262176 | tf_op jit(solution)/shard_map/all_to_all | solution.py:372
  41.0 1.3 %shard_map.123 = (f32[16,16,128]{2,1,0:T(8,128)}, f32[64,2048]{1,0:T(8,128)S(1)}, f32[16,2048]{1,0:T(8,128)S(1)}) custom-call(f32[32,16,128]{2,1,0:T(8,128)S(1)} %all-to-all-done.refs_0_), custom_call_target="tpu_custom_call" | custom-call | tf_op jit(solution)/shard_map/pallas_call | solution.py:337
  42.4 7.2 %all-to-all-start.1 = ((f32[16,16,128]{2,1,0:T(8,128)}), f32[16,16,128]{2,1,0:T(8,128)S(1)}, u32[]{:S(2)}, u32[]{:S(2)}) async-start(f32[16,16,128]{2,1,0:T(8,128)} %get-tuple-element.11), calls=%async_computation.1 | async-start | bytes 262144 | tf_op jit(solution)/shard_map/all_to_all | solution.py:381
  49.6 0.0 copy-start.5
  49.6 0.0 copy-start.6
  49.6 0.0 copy-start.7
  49.6 3.4 %collective-permute-start.2 = (f32[320,128]{1,0:T(8,128)S(1)}, f32[320,128]{1,0:T(8,128)S(1)}, u32[]{:S(2)}, u32[]{:S(2)}) collective-permute-start(f32[320,128]{1,0:T(8,128)S(1)} %constant_dynamic-update-slice_fusion), channel_id=1, source_target_pairs={{0,3},{1,0},{2,1},{3,2},{4,7},{5,4},{6,5},{7,6},{8,11},{9,8},{10,9... | collective-permute-start | bytes 491528 | tf_op jit(solution)/shard_map/ppermute | solution.py:346
  53.0 4.4 %collective-permute-done.2.in_z_ref = f32[320,128]{1,0:T(8,128)S(1)} collective-permute-done((f32[320,128]{1,0:T(8,128)S(1)}, f32[320,128]{1,0:T(8,128)S(1)}, u32[]{:S(2)}, u32[]{:S(2)}) %collective-permute-start.2) | collective-permute-done | bytes 163872 | tf_op jit(solution)/shard_map/ppermute | solution.py:346
  57.5 4.2 %shard_map.124 = (f32[4,4,128]{2,1,0:T(4,128)S(1)}, f32[4,4,128]{2,1,0:T(4,128)S(1)}) custom-call(f32[104,128]{1,0:T(8,128)S(1)} %get-tuple-element.14.own_ref, f32[32,128]{1,0:T(8,128)S(1)} %get-tuple-element.15.rest_ref, f32[104,128]{1,0:T(8,128)S(1)} %collective-permute-done.in_x_ref, f32[176,128]{1,0:T(8,128)S(1)} %collective-permute-done.1.in_y_ref, ...), custom_call_target="tpu_custom_call" | custom-call | tf_op jit(solution)/shard_map/pallas_call | solution.py:337
  61.7 3.4 %collective-permute-start.3 = (f32[4,4,128]{2,1,0:T(4,128)S(1)}, f32[4,4,128]{2,1,0:T(4,128)S(1)}, u32[]{:S(2)}, u32[]{:S(2)}) collective-permute-start(f32[4,4,128]{2,1,0:T(4,128)S(1)} %get-tuple-element.17), channel_id=1, source_target_pairs={{0,32},{32,64},{64,96},{96,128},{128,160},{160,192},{192,224},{224... | collective-permute-start | bytes 24584 | tf_op jit(solution)/shard_map/ppermute | solution.py:346
  65.1 4.7 %collective-permute-done.3.refs_4_ = f32[4,4,128]{2,1,0:T(4,128)S(1)} collective-permute-done((f32[4,4,128]{2,1,0:T(4,128)S(1)}, f32[4,4,128]{2,1,0:T(4,128)S(1)}, u32[]{:S(2)}, u32[]{:S(2)}) %collective-permute-start.3) | collective-permute-done | bytes 8224 | tf_op jit(solution)/shard_map/ppermute | solution.py:346
  69.8 0.0 all-to-all-done.1.refs_0_
  69.8 1.1 %shard_map.125 = f32[32,4,128]{2,1,0:T(4,128)} custom-call(f32[16,16,128]{2,1,0:T(8,128)S(1)} %all-to-all-done.1.refs_0_, f32[64,2048]{1,0:T(8,128)S(1)} %get-tuple-element.12.refs_1_, f32[16,2048]{1,0:T(8,128)S(1)} %get-tuple-element.13.refs_2_, f32[4,4,128]{2,1,0:T(4,128)S(1)} %get-tuple-element.16.refs_3_, f32[4,4,128]{2,1,0:T(4,128)S(1)} %collective-permute-done.3.refs_4_), custom_call_target="tpu_custom_call" | custom-call | tf_op jit(solution)/shard_map/pallas_call | solution.py:337
  70.9 3.8 %all-to-all-start.2 = ((f32[32,4,128]{2,1,0:T(4,128)}), f32[32,4,128]{2,1,0:T(4,128)S(1)}, u32[]{:S(2)}, u32[]{:S(2)}) async-start(f32[32,4,128]{2,1,0:T(4,128)} %shard_map.125), calls=%async_computation.2 | async-start | bytes 131072 | tf_op jit(solution)/shard_map/all_to_all | solution.py:404
  74.7 0.2 select_reduce_fusion
  74.9 8.1 %all-to-all-done.2.parts_ref = f32[32,4,128]{2,1,0:T(4,128)S(1)} async-done(((f32[32,4,128]{2,1,0:T(4,128)}), f32[32,4,128]{2,1,0:T(4,128)S(1)}, u32[]{:S(2)}, u32[]{:S(2)}) %all-to-all-start.2) | async-done | bytes 65568 | tf_op jit(solution)/shard_map/all_to_all | solution.py:404
  83.0 0.1 shard_map.126
  83.2 0.1 neg.7
  83.2 0.6 copy.18
  83.9 0.1 reshape_squeeze.3
  83.9 0.7 fusion
  (26 shorter events, 0.1 us)
Async XLA Ops:
  0.6 0.8 copy-start.1
  1.4 0.7 copy-start.3
  1.4 0.7 copy-start.4
  2.1 0.8 copy-start.2
  3.9 9.6 %collective-permute-start = (f32[104,128]{1,0:T(8,128)S(1)}, f32[104,128]{1,0:T(8,128)S(1)}, u32[]{:S(2)}, u32[]{:S(2)}) collective-permute-start(f32[104,128]{1,0:T(8,128)S(1)} %get-tuple-element.14.own_ref), channel_id=1, source_target_pairs={{0,480},{32,0},{64,32},{96,64},{128,96},{160,128},{192,160},{224,1... | collective-permute-start | bytes 159752 | tf_op jit(solution)/shard_map/ppermute | solution.py:346
  13.5 16.0 %collective-permute-start.1 = (f32[176,128]{1,0:T(8,128)S(1)}, f32[176,128]{1,0:T(8,128)S(1)}, u32[]{:S(2)}, u32[]{:S(2)}) collective-permute-start(f32[176,128]{1,0:T(8,128)S(1)} %pad_maximum_fusion), channel_id=1, source_target_pairs={{0,28},{4,0},{8,4},{12,8},{16,12},{20,16},{24,20},{28,24},{1,29},{... | collective-permute-start | bytes 270344 | tf_op jit(solution)/shard_map/ppermute | solution.py:346
  24.2 16.8 %all-to-all-start = ((f32[32,16,128]{2,1,0:T(8,128)}), f32[32,16,128]{2,1,0:T(8,128)S(1)}, u32[]{:S(2)}, u32[]{:S(2)}) async-start(f32[32,16,128]{2,1,0:T(8,128)} %get-tuple-element.10), calls=%async_computation | async-start | bytes 524288 | tf_op jit(solution)/shard_map/all_to_all | solution.py:372
  42.4 15.1 %copy-start = (f32[128,128]{1,0:T(8,128)S(1)}, f32[128,128]{1,0:T(8,128)}, u32[]{:S(2)}) copy-start(f32[128,128]{1,0:T(8,128)} %mix_ref.1) | copy-start | bytes 196612
  42.4 27.5 %all-to-all-start.1 = ((f32[16,16,128]{2,1,0:T(8,128)}), f32[16,16,128]{2,1,0:T(8,128)S(1)}, u32[]{:S(2)}, u32[]{:S(2)}) async-start(f32[16,16,128]{2,1,0:T(8,128)} %get-tuple-element.11), calls=%async_computation.1 | async-start | bytes 262144 | tf_op jit(solution)/shard_map/all_to_all | solution.py:381
  49.6 7.9 %copy-start.5 = (f32[8,128]{1,0:T(8,128)S(1)}, f32[8,128]{1,0:T(8,128)}, u32[]{:S(2)}) copy-start(f32[8,128]{1,0:T(8,128)} %radial_ref.1) | copy-start | bytes 12292
  49.6 7.9 %copy-start.6 = (f32[8,128]{1,0:T(8,128)S(1)}, f32[8,128]{1,0:T(8,128)}, u32[]{:S(2)}) copy-start(f32[8,128]{1,0:T(8,128)} %vector_ref.1) | copy-start | bytes 12292
  49.6 7.8 %copy-start.7 = (f32[128]{0:T(128)S(1)}, f32[128]{0:T(128)}, u32[]{:S(2)}) copy-start(f32[128]{0:T(128)} %param.19) | copy-start | bytes 1540
  49.6 7.8 %collective-permute-start.2 = (f32[320,128]{1,0:T(8,128)S(1)}, f32[320,128]{1,0:T(8,128)S(1)}, u32[]{:S(2)}, u32[]{:S(2)}) collective-permute-start(f32[320,128]{1,0:T(8,128)S(1)} %constant_dynamic-update-slice_fusion), channel_id=1, source_target_pairs={{0,3},{1,0},{2,1},{3,2},{4,7},{5,4},{6,5},{7,6},{8,11},{9,8},{10,9... | collective-permute-start | bytes 491528 | tf_op jit(solution)/shard_map/ppermute | solution.py:346
  61.7 8.2 %collective-permute-start.3 = (f32[4,4,128]{2,1,0:T(4,128)S(1)}, f32[4,4,128]{2,1,0:T(4,128)S(1)}, u32[]{:S(2)}, u32[]{:S(2)}) collective-permute-start(f32[4,4,128]{2,1,0:T(4,128)S(1)} %get-tuple-element.17), channel_id=1, source_target_pairs={{0,32},{32,64},{64,96},{96,128},{128,160},{160,192},{192,224},{224... | collective-permute-start | bytes 24584 | tf_op jit(solution)/shard_map/ppermute | solution.py:346
  70.9 3.8 %copy-start.8 = (s32[2,2,2,8]{3,2,1,0:T(2,128)S(1)}, s32[2,2,2,8]{3,2,1,0:T(2,128)}, u32[]{:S(2)}) copy-start(s32[2,2,2,8]{3,2,1,0:T(2,128)} %param.14) | copy-start | bytes 772
  70.9 3.8 %copy-start.9 = (f32[8]{0:T(128)S(1)}, f32[8]{0:T(128)}, u32[]{:S(2)}) copy-start(f32[8]{0:T(128)} %param.21) | copy-start | bytes 100
  70.9 12.1 %all-to-all-start.2 = ((f32[32,4,128]{2,1,0:T(4,128)}), f32[32,4,128]{2,1,0:T(4,128)S(1)}, u32[]{:S(2)}, u32[]{:S(2)}) async-start(f32[32,4,128]{2,1,0:T(4,128)} %shard_map.125), calls=%async_computation.2 | async-start | bytes 131072 | tf_op jit(solution)/shard_map/all_to_all | solution.py:404

commit v2 on v1

--- a/solution.py
+++ b/solution.py
@@ -1,3 +1,4 @@
+import functools
 import math
 
 import jax
@@ -14,7 +15,11 @@
 HIGH = lax.Precision.HIGHEST
 F32 = jnp.float32
 BF16 = jnp.bfloat16
-PARAMS = pltpu.CompilerParams(vmem_limit_bytes=48 * 1024 * 1024)
+STACK_MICROS = 50
+WAVES_MICROS = 500
+SHORT_MICROS = 1
+PACK_ROOM = 60
+LAST_ROOM = 48
 
 
 def iota(shape, dim):
@@ -37,7 +42,24 @@
     return pltpu.roll(value, 64, value.ndim - 1)
 
 
-def pack_kernel(feat_ref, pos_ref, count_ref, near_ref, charge_ref, slab_ref, rest_ref, message_ref):
+def position_rows(pos_ref, lane):
+    pieces = [pos_ref[x, y, d] for x in range(2) for y in range(2) for d in range(3)]
+    spread = (iota((8, 128), 1) % 8 == iota((8, 128), 0)).astype(F32)
+    wide = contract(jnp.concatenate(pieces, 0), spread, (((1,), (0,))), HIGH)
+    rows = []
+    for d in range(3):
+        row = jnp.zeros((1, 128), F32)
+        for cell in range(8):
+            at = (cell // 2) * 6 + d * 2 + cell % 2
+            row = jnp.where(lane[0:1] // 8 == cell, wide[at : at + 1], row)
+        rows.append(row)
+    return jnp.concatenate(rows + [jnp.zeros((5, 128), F32)], 0)
+
+
+def pack_kernel(
+    feat_ref, pos_ref, count_ref, near_ref, charge_ref,
+    to_x_ref, to_y_ref, to_xy_ref, rest_ref, message_ref,
+):
     row = iota((64, 128), 0)
     lane = iota((8, 128), 1)
     count_col = jnp.zeros((64, 128), jnp.int32)
@@ -52,10 +74,8 @@
     charges = contract(
         charge_ref[...], jnp.concatenate([masked, masked], 0), (((1,), (1,))), HIGH
     )
-    spots = pos_ref[...]
     sub = iota((8, 128), 0)
-    tile = jnp.concatenate([spots, jnp.zeros((5, 64), F32)], 0)
-    tile = jnp.concatenate([tile, jnp.zeros((8, 64), F32)], 1)
+    tile = position_rows(pos_ref, lane)
     tile = jnp.where(sub == 3, occupied_row, tile)
     cell_x, cell_y, cell_z = lane // 32 % 2, lane // 16 % 2, lane // 8 % 2
     corner_x = 2 * lax.axis_index("gx")
@@ -88,12 +108,21 @@
     block = (spot_z >> 1) * 4 + (spot_y >> 1) * 2 + (spot_x >> 1)
     cell = (spot_x & 1) * 4 + (spot_y & 1) * 2 + (spot_z & 1)
     target = (block * 64 + cell * 8 + slot).astype(F32)
-    slab_ref[0:64] = masked
-    slab_ref[64:72] = tile
-    slab_ref[72:104] = turned[0:32]
-    slab_ref[72:104, 0:32] = target[0:32]
-    rest_ref[...] = turned[32:64]
-    rest_ref[:, 0:32] = target[32:64]
+    for ref, first in ((to_xy_ref, 0), (to_x_ref, 16), (to_y_ref, 32)):
+        ref[0:64] = masked
+        ref[64:72] = tile
+        ref[72:88] = turned[first : first + 16]
+        ref[72:88, 0:32] = target[first : first + 16]
+    rest_ref[...] = turned[48:64]
+    rest_ref[:, 0:32] = target[48:64]
+
+
+def stack_kernel(own_ref, rest_ref, in_x_ref, in_y_ref, in_xy_ref, out_ref):
+    for block, ref in enumerate((own_ref, in_x_ref, in_y_ref, in_xy_ref)):
+        out_ref[72 * block : 72 * block + 72] = ref[0:72]
+    out_ref[288:296] = rest_ref[0:8]
+    for block, ref in enumerate((in_x_ref, in_y_ref, in_xy_ref)):
+        out_ref[296 + 8 * block : 304 + 8 * block] = ref[72:80]
 
 
 def wave_numbers(member, shape, dim):
@@ -119,7 +148,7 @@
     return sine * angle, cosine
 
 
-def waves_kernel(grid, atoms_ref, message_ref, phase_ref, charge_ref):
+def waves_kernel(grid, atoms_ref, partial_ref, phase_ref, charge_ref):
     member = lax.axis_index("gy") * 4 + lax.axis_index("gz")
     low = iota((8, 128), 1) < 64
     upper, lower, places = [], [], []
@@ -147,17 +176,38 @@
     phase_stack = jnp.concatenate(split(phases), 0)
     sums = contract(charge_stack, phase_stack, (((1,), (1,))))
     partial = sums[0:16] + sums[16:32]
-    for other in range(message_ref.shape[0]):
-        message_ref[other] = partial
-
-
-def field_kernel(grid, scale, sums_ref, phase_ref, charge_ref, kept_ref, came_ref, out_ref):
+    partial = partial + swap_halves(partial)
+    partial_ref[...] = jnp.where(low, partial[0:8], partial[8:16])
+
+
+def join_kernel(partial_ref, kept_ref, sent_ref, message_ref):
+    here = lax.axis_index("gx")
+    count = message_ref.shape[0]
+    partial = partial_ref[...]
+    for other in range(count):
+        message_ref[other, 0:8] = partial
+        message_ref[other, 8:16] = jnp.zeros((8, 128), F32)
+    message_ref[here, 8:16] = kept_ref[...]
+    message_ref[(here + 1) % count, 8:16] = sent_ref[...]
+
+
+def field_kernel(grid, scale, sums_ref, phase_ref, charge_ref, out_ref):
     at_y, at_z = lax.axis_index("gy"), lax.axis_index("gz")
     member = at_y * 4 + at_z
     total = sums_ref[0]
     for other in range(1, sums_ref.shape[0]):
         total = total + sums_ref[other]
-    total = total + swap_halves(total)
+    folded = total[8:16]
+    turned = swap_halves(total)
+    low_lane = iota((8, 128), 1) < 64
+    total = jnp.concatenate(
+        [
+            jnp.where(low_lane, total[0:8], turned[0:8]),
+            jnp.where(low_lane, turned[0:8], total[0:8]),
+        ],
+        0,
+    )
+    turned = turned[8:16]
     two_pi = 2.0 * math.pi
     number_x, number_y, number_z = wave_numbers(member, (16, 128), 1)
     wave_x, wave_y, wave_z = (
@@ -191,16 +241,17 @@
         by, bz = block % 2, block // 2
         to_z = (at_z + bz) % 4
         to = ((at_y + by) % 8) * 4 + to_z
-        folded = kept_ref[block] + came_ref[block]
-        out_ref[to] = out_ref[to] + jnp.where(half == to_z % 2, folded, 0.0)
+        rows_at = slice(4 * bz, 4 * bz + 4)
+        piece = jnp.where(to_z % 2 == by, folded[rows_at], turned[rows_at])
+        out_ref[to] = out_ref[to] + jnp.where(half == to_z % 2, piece, 0.0)
 
 
 def short_kernel(
-    own_ref, rest_ref, in_x_ref, in_y_ref, in_z_ref,
-    radial_ref, vector_ref, mix_ref, out_weight_ref, kept_ref, sent_ref,
+    own_ref, rest_ref, in_x_ref, in_y_ref, in_xy_ref, in_z_ref,
+    radial_ref, vector_ref, mix_ref, out_weight_ref, species_ref, shift_ref, kept_ref, sent_ref,
 ):
     bases = [
-        (own_ref, 0), (in_x_ref, 0), (in_y_ref, 0), (in_y_ref, 72),
+        (own_ref, 0), (in_x_ref, 0), (in_y_ref, 0), (in_xy_ref, 0),
         (in_z_ref, 0), (in_z_ref, 72), (in_z_ref, 144), (in_z_ref, 216),
     ]
     feats = jnp.concatenate([ref[at : at + 64] for ref, at in bases], 0)
@@ -217,7 +268,7 @@
         )
     spots = jnp.concatenate(spots, 1)
     tiles = [
-        rest_ref[24:32], in_x_ref[96:104], in_y_ref[152:160], in_y_ref[168:176],
+        rest_ref[8:16], in_x_ref[80:88], in_y_ref[80:88], in_xy_ref[80:88],
         in_z_ref[288:296], in_z_ref[296:304], in_z_ref[304:312], in_z_ref[312:320],
     ]
     centres = jnp.concatenate(tiles, 0)
@@ -317,33 +368,57 @@
         rows.append(jnp.sum(push - jnp.where(own_slot, back, 0.0), 0, keepdims=True))
     rows = jnp.concatenate(rows, 0)
     low = iota((4, 128), 1) < 64
-    for k in range(4):
-        piece = rows[:, 128 * k : 128 * k + 128]
-        turned = swap_halves(piece)
-        kept_ref[k] = jnp.where(low, piece, turned)
-        sent_ref[k] = jnp.where(low, turned, piece)
-
-
-def sum_kernel(parts_ref, out_ref):
+    kinds = [species_ref[x, y] for x in range(2) for y in range(2)]
+    spread = (iota((8, 128), 1) % 8 == iota((8, 128), 0)).astype(F32)
+    kinds = contract(jnp.concatenate(kinds, 0).astype(F32), spread, (((1,), (0,))))
+    shift = jnp.zeros((8, 128), F32)
+    for name in range(shift_ref.shape[1]):
+        shift = jnp.where(kinds == float(name), shift_ref[:, name : name + 1], shift)
+    mine = iota((8, 128), 1) // 8 == iota((8, 128), 0)
+    shift = jnp.sum(jnp.where(mine, shift, 0.0), 0, keepdims=True) * own_ref[67:68]
+    shift = jnp.where(iota((4, 128), 0) == 0, shift, 0.0)
+    for half in range(2):
+        first, second = (rows[:, 128 * k : 128 * k + 128] for k in (2 * half, 2 * half + 1))
+        at = slice(4 * half, 4 * half + 4)
+        first = first + shift if half == 0 else first
+        kept_ref[at] = jnp.where(low, first, swap_halves(second))
+        sent_ref[at] = jnp.where(low, swap_halves(first), second)
+
+
+def last_kernel(parts_ref, energy_ref, force_ref):
     total = parts_ref[0]
     for member in range(1, parts_ref.shape[0]):
         total = total + parts_ref[member]
     odd = lax.axis_index("gz") % 2
     total = jnp.where(odd == 1, swap_halves(total), total)
-    out_ref[...] = total
-
-
-def call(kernel, out, *operands):
+    for cell in range(8):
+        x, y, z = cell // 4, cell // 2 % 2, cell % 2
+        here = total if cell == 0 else pltpu.roll(total, 128 - 8 * cell, 1)
+        energy_ref[x, y, z : z + 1] = here[0:1, 0:8]
+        for d in range(3):
+            force_ref[x, y, d, z : z + 1] = -here[1 + d : 2 + d, 0:8]
+
+
+def call(kernel, out, *operands, micros=10, room=48):
+    cost = pl.CostEstimate(flops=micros * 10**8, bytes_accessed=micros * 3 * 10**5, transcendentals=0)
     return pl.pallas_call(
         kernel,
         out_shape=[jax.ShapeDtypeStruct(shape, F32) for shape in out],
-        compiler_params=PARAMS,
+        compiler_params=pltpu.CompilerParams(vmem_limit_bytes=room * 1024 * 1024),
+        cost_estimate=cost,
     )(*operands)
 
 
-def moved(value, axis, steps):
-    count = lax.axis_size(axis)
-    return lax.ppermute(value, axis, [(i, (i + steps) % count) for i in range(count)])
+def moved(value, axes, *steps):
+    counts = [lax.axis_size(axis) for axis in axes]
+    pairs = []
+    for source in range(math.prod(counts)):
+        rest, target, stride = source, 0, 1
+        for count, step in zip(counts[::-1], steps[::-1]):
+            target += (rest + step) % count * stride
+            rest, stride = rest // count, stride * count
+        pairs.append((source, target))
+    return lax.ppermute(value, axes, pairs)
 
 
 def body(
@@ -351,63 +426,51 @@
     w_radial, w_vector, w_mix, w_out, w_charge, species_shift,
 ):
     cells_x, cells_y, cells_z, slots_cell, channels = features.shape
-    block_shape = (cells_x, cells_y, cells_z, slots_cell)
     grid = (
         cells_x * lax.axis_size("gx"),
         cells_y * lax.axis_size("gy"),
         cells_z * lax.axis_size("gz"),
     )
     scale = 1.0 / math.sqrt(grid[0] * grid[1] * grid[2] * slots_cell * MODES)
-    spots = jnp.transpose(offsets, (3, 0, 1, 2, 4)).reshape(3, 64)
-    slab, rest, message = call(
+    to_x, to_y, to_xy, rest, message = call(
         pack_kernel,
-        [(104, 128), (32, 128), (32, 16, 128)],
+        [(88, 128), (88, 128), (88, 128), (16, 128), (32, 16, 128)],
         features.reshape(64, 128),
-        spots,
+        jnp.transpose(offsets, (0, 1, 3, 2, 4)),
         counts,
         neighbours.reshape(64, 32),
         w_charge.T,
-    )
-    in_x = moved(slab, "gx", -1)
+        room=PACK_ROOM,
+    )
     atoms = lax.all_to_all(message, ("gy", "gz"), 0, 0)
-    in_y = moved(
-        jnp.concatenate([slab[0:72], in_x[0:72], rest[0:16], in_x[72:88]], 0), "gy", -1
-    )
+    in_x = moved(to_x, ("gx",), -1)
+    in_y = moved(to_y, ("gy",), -1)
+    in_xy = moved(to_xy, ("gx", "gy"), -1, -1)
+    (to_z,) = call(
+        stack_kernel, [(320, 128)], to_x, rest, in_x, in_y, in_xy, micros=STACK_MICROS
+    )
+    in_z = moved(to_z, ("gz",), -1)
     partial, phases, charges = call(
-        lambda *refs: waves_kernel(grid, *refs),
-        [(16, 16, 128), (64, 2048), (16, 2048)],
+        functools.partial(waves_kernel, grid),
+        [(8, 128), (64, 2048), (16, 2048)],
         atoms,
-    )
-    sums = lax.all_to_all(partial, "gx", 0, 0)
-    in_z = moved(
-        jnp.concatenate(
-            [
-                slab[0:72], in_x[0:72], in_y[0:144],
-                rest[16:24], in_x[88:96], in_y[144:152], in_y[160:168],
-            ],
-            0,
-        ),
-        "gz",
-        -1,
+        micros=WAVES_MICROS,
     )
     kept, sent = call(
         short_kernel,
-        [(4, 4, 128), (4, 4, 128)],
-        slab, rest, in_x, in_y, in_z, w_radial, w_vector, w_mix, w_out.reshape(1, 128),
-    )
-    came = moved(sent, "gx", 1)
+        [(8, 128), (8, 128)],
+        to_x, rest, in_x, in_y, in_xy, in_z,
+        w_radial, w_vector, w_mix, w_out.reshape(1, 128), species, species_shift.reshape(1, 8),
+        micros=SHORT_MICROS,
+    )
+    (joined,) = call(join_kernel, [(16, 16, 128)], partial, kept, sent)
+    sums = lax.all_to_all(joined, "gx", 0, 0)
     (parts,) = call(
-        lambda *refs: field_kernel(grid, scale, *refs),
-        [(32, 4, 128)],
-        sums, phases, charges, kept, came,
-    )
-    (rows,) = call(sum_kernel, [(4, 128)], lax.all_to_all(parts, ("gy", "gz"), 0, 0))
-    table = species[..., None] == jnp.arange(species_shift.shape[0], dtype=jnp.int32)
-    shifted = jnp.sum(jnp.where(table, species_shift, 0.0), -1)
-    occupied = iota(block_shape, 3) < counts[..., None]
-    atom_energy = rows[0, 0:64].reshape(block_shape) + jnp.where(occupied, shifted, 0.0)
-    forces = -rows[1:4, 0:64].reshape((3,) + block_shape)
-    return (atom_energy, jnp.transpose(forces, (1, 2, 3, 0, 4)))
+        functools.partial(field_kernel, grid, scale), [(32, 4, 128)], sums, phases, charges
+    )
+    parts = lax.all_to_all(parts, ("gy", "gz"), 0, 0)
+    atom_energy, forces = call(last_kernel, [(2, 2, 2, 8), (2, 2, 3, 2, 8)], parts, room=LAST_ROOM)
+    return (atom_energy, jnp.transpose(forces, (0, 1, 3, 2, 4)))
 
 
 def solution(mesh):

time: 85.3 us -> 73.4 us (0.86)
  blocking collectives: 0 us -> 27.8 us
  waiting for transfers between devices: 29.8 us -> 5.93 us
  starting transfers between devices: 42.2 us -> 29.4 us
  local copies, waits for them, and re-layouts: 3.11 us -> 0.68 us
    all_to_all x0 -> x2, blocking collectives: none -> 27.8 us  [the longest x1 14.6 us: body(): parts = lax.all_to_all(parts, ('gy', 'gz'), 0, 0)]
    all_to_all x1, waiting for transfers between devices: 11.4 us -> 0.01 us  [body(): atoms = lax.all_to_all(message, ('gy', 'gz'), 0, 0)]
    all_to_all x2 -> x0, starting transfers between devices: 11 us -> none  [the longest x1 7.2 us: body(): sums = lax.all_to_all(partial, 'gx', 0, 0)]
    all_to_all x2 -> x0, waiting for transfers between devices: 8.13 us -> none  [the longest x1 8.13 us: body(): lax.all_to_all(parts, ('gy', 'gz'), 0, 0)]
    ppermute x4, waiting for transfers between devices: 10.3 us -> 5.93 us  [moved(): return lax.ppermute(value, axes, pairs)]
    ppermute x4, starting transfers between devices: 25.9 us -> 24.3 us  [moved(): return lax.ppermute(value, axes, pairs)]
    pallas_call x5 -> x7, Pallas kernels: 7.78 us -> 8.23 us  [call(): pl.pallas_call(kernel, out_shape=[jax.ShapeDtypeStruct(shape, F32) for sh...]
  transfers between devices with their start and end apart: 7 -> 5, of which waited for: 5 -> 1; matrix products, arithmetic and copies ran while one was open for 0% -> 0% of each run, Pallas kernels for 5% -> 6%
where the time goes in v2:
time: 73.4 us; the launch traced here: 72.9 us
  starting transfers between devices  29.4 us (40%)
  blocking collectives  27.8 us (38%)
  Pallas kernels  8.23 us (11%)
  waiting for transfers between devices  5.93 us (8%)
  between operations  0.8 us (1%)
    ppermute x4, starting transfers between devices, moved(): return lax.ppermute(value, axes, pairs)  24.3 us
    all_to_all x1, blocking collectives, body(): parts = lax.all_to_all(parts, ('gy', 'gz'), 0, 0)  14.6 us
    all_to_all x1, blocking collectives, body(): sums = lax.all_to_all(joined, 'gx', 0, 0)  13.3 us
    pallas_call x7, Pallas kernels, call(): pl.pallas_call(kernel, out_shape=[jax.ShapeDtypeStruct(shape, F32) for sh...  8.23 us
    ppermute x4, waiting for transfers between devices, moved(): return lax.ppermute(value, axes, pairs)  5.93 us
    all_to_all x1, starting transfers between devices, body(): atoms = lax.all_to_all(message, ('gy', 'gz'), 0, 0)  5.18 us
  transfers between devices with their start and end apart: 5, of which 1 were waited for; matrix products, arithmetic and copies ran while one was open for 0% of the time, Pallas kernels for 6%

profile of v2, /device:TPU:1, one launch (start us, length us, event | category | flops | bytes accessed | tf_op | source)
XLA Modules:
  0.0 72.9 jit_solution(5095898354242668974)
XLA Ops:
  0.6 2.0 %shard_map.122 = (f32[88,128]{1,0:T(8,128)}, f32[88,128]{1,0:T(8,128)}, f32[88,128]{1,0:T(8,128)}, f32[16,128]{1,0:T(8,128)}, f32[32,16,128]{2,1,0:T(8,128)}) custom-call(f32[64,128]{1,0:T(8,128)} %bitcast.9, f32[2,2,3,2,8]{4,3,2,1,0:T(2,128)} %bitcast.11, s32[2,2,2]{2,1,0:T(2,128)} %count_ref.1, s32[64,32]{1,0:T(8,128)} %bitcast.10, f32[16,128]{1,0:T(8,128)} %bitcast.12), custom_call_target="tpu_custom_call" | custom-call | flops 1000000000 | bytes 3000000 | tf_op jit(solution)/shard_map/pallas_call | solution.py:404
  2.6 11.5 %collective-permute-start.1 = (f32[88,128]{1,0:T(8,128)}, f32[88,128]{1,0:T(8,128)S(1)}, u32[]{:S(2)}, u32[]{:S(2)}) collective-permute-start(f32[88,128]{1,0:T(8,128)} %get-tuple-element.18), channel_id=1, source_target_pairs={{0,28},{4,0},{8,4},{12,8},{16,12},{20,16},{24,20},{28,24},{1,29},{... | collective-permute-start | bytes 135176 | tf_op jit(solution)/shard_map/ppermute | solution.py:421
  14.1 7.5 %collective-permute-start.2 = (f32[88,128]{1,0:T(8,128)}, f32[88,128]{1,0:T(8,128)S(1)}, u32[]{:S(2)}, u32[]{:S(2)}) collective-permute-start(f32[88,128]{1,0:T(8,128)} %get-tuple-element.19), channel_id=1, source_target_pairs={{0,508},{4,480},{8,484},{12,488},{16,492},{20,496},{24,500},{28,50... | collective-permute-start | bytes 135176 | tf_op jit(solution)/shard_map/ppermute | solution.py:421
  21.6 3.0 %collective-permute-start = (f32[88,128]{1,0:T(8,128)}, f32[88,128]{1,0:T(8,128)S(1)}, u32[]{:S(2)}, u32[]{:S(2)}) collective-permute-start(f32[88,128]{1,0:T(8,128)} %get-tuple-element.16.own_ref), channel_id=1, source_target_pairs={{0,480},{32,0},{64,32},{96,64},{128,96},{160,128},{192,160},{224,1... | collective-permute-start | bytes 135176 | tf_op jit(solution)/shard_map/ppermute | solution.py:421
  24.6 0.0 copy-start.1
  24.6 0.0 copy-start.2
  24.6 5.2 %all-to-all-start = ((f32[32,16,128]{2,1,0:T(8,128)}), f32[32,16,128]{2,1,0:T(8,128)S(1)}, u32[]{:S(2)}, u32[]{:S(2)}) async-start(f32[32,16,128]{2,1,0:T(8,128)} %get-tuple-element.14), calls=%async_computation | async-start | bytes 524288 | tf_op jit(solution)/shard_map/all_to_all | solution.py:445
  29.8 0.0 collective-permute-done.1.in_y_ref
  29.8 0.0 collective-permute-done.2.in_xy_ref
  29.8 0.0 collective-permute-done.in_x_ref
  29.9 0.0 copy-done.1
  29.9 0.0 copy-done.2
  29.9 0.0 copy-start
  29.9 0.0 copy-start.3
  29.9 0.0 copy-start.4
  29.9 0.0 copy-start.5
  29.9 2.3 %collective-permute-start.3 = (f32[320,128]{1,0:T(8,128)S(1)}, f32[320,128]{1,0:T(8,128)S(1)}, u32[]{:S(2)}, u32[]{:S(2)}) collective-permute-start(f32[320,128]{1,0:T(8,128)S(1)} %shard_map.124), channel_id=1, source_target_pairs={{0,3},{1,0},{2,1},{3,2},{4,7},{5,4},{6,5},{7,6},{8,11},{9,8},{10,9... | collective-permute-start | bytes 491528 | tf_op jit(solution)/shard_map/ppermute | solution.py:421
  32.2 5.9 %collective-permute-done.3.in_z_ref = f32[320,128]{1,0:T(8,128)S(1)} collective-permute-done((f32[320,128]{1,0:T(8,128)S(1)}, f32[320,128]{1,0:T(8,128)S(1)}, u32[]{:S(2)}, u32[]{:S(2)}) %collective-permute-start.3) | collective-permute-done | bytes 163872 | tf_op jit(solution)/shard_map/ppermute | solution.py:421
  38.1 0.0 copy-start.6
  38.1 0.0 copy-done
  38.1 0.0 copy-done.3
  38.1 0.0 copy-done.4
  38.2 0.0 copy-done.5
  38.2 0.6 copy-done.6
  38.8 0.0 copy-done.7
  38.8 4.2 %shard_map.125 = (f32[8,128]{1,0:T(8,128)S(1)}, f32[8,128]{1,0:T(8,128)S(1)}) custom-call(f32[88,128]{1,0:T(8,128)S(1)} %copy-done.1, f32[16,128]{1,0:T(8,128)S(1)} %copy-done.2, f32[88,128]{1,0:T(8,128)S(1)} %collective-permute-done.in_x_ref, f32[88,128]{1,0:T(8,128)S(1)} %collective-permute-done.1.in_y_ref, ...), custom_call_target="tpu_custom_call" | custom-call | flops 100000000 | bytes 300000 | tf_op jit(solution)/shard_map/pallas_call | solution.py:404
  43.0 0.0 all-to-all-done.atoms_ref
  43.0 0.7 %shard_map.123 = (f32[8,128]{1,0:T(8,128)S(1)}, f32[64,2048]{1,0:T(8,128)S(1)}, f32[16,2048]{1,0:T(8,128)S(1)}) custom-call(f32[32,16,128]{2,1,0:T(8,128)S(1)} %all-to-all-done.atoms_ref), custom_call_target="tpu_custom_call" | custom-call | flops 49999998976 | bytes 150000000 | tf_op jit(solution)/shard_map/pallas_call | solution.py:404
  43.8 13.3 %all_to_all.15.sums_ref = f32[16,16,128]{2,1,0:T(8,128)S(1)} all-to-all(f32[16,16,128]{2,1,0:T(8,128)S(1)} %shard_map.126), channel_id=1, replica_groups=mesh['gx'=16,'gy'=8,'gz'=4] {'gx'}, dimensions={0} | all-to-all | bytes 262144 | tf_op jit(solution)/shard_map/all_to_all | solution.py:467
  57.1 0.5 shard_map.127
  57.6 14.6 %all_to_all.16.parts_ref = f32[32,4,128]{2,1,0:T(4,128)S(1)} all-to-all(f32[32,4,128]{2,1,0:T(4,128)S(1)} %shard_map.127), channel_id=1, replica_groups=mesh['gx'=16,'gy'=8,'gz'=4] {'gy','gz'}, dimensions={0} | all-to-all | bytes 131072 | tf_op jit(solution)/shard_map/all_to_all | solution.py:471
  72.1 0.8 %shard_map.128 = (f32[2,2,2,8]{3,2,1,0:T(2,128)}, f32[2,2,3,2,8]{4,3,2,1,0:T(2,128)}) custom-call(f32[32,4,128]{2,1,0:T(4,128)S(1)} %all_to_all.16.parts_ref), custom_call_target="tpu_custom_call" | custom-call | flops 1000000000 | bytes 3000000 | tf_op jit(solution)/shard_map/pallas_call | solution.py:404
  (3 shorter events, 0.1 us)
Async XLA Ops:
  2.6 27.2 %collective-permute-start.1 = (f32[88,128]{1,0:T(8,128)}, f32[88,128]{1,0:T(8,128)S(1)}, u32[]{:S(2)}, u32[]{:S(2)}) collective-permute-start(f32[88,128]{1,0:T(8,128)} %get-tuple-element.18), channel_id=1, source_target_pairs={{0,28},{4,0},{8,4},{12,8},{16,12},{20,16},{24,20},{28,24},{1,29},{... | collective-permute-start | bytes 135176 | tf_op jit(solution)/shard_map/ppermute | solution.py:421
  14.1 15.8 %collective-permute-start.2 = (f32[88,128]{1,0:T(8,128)}, f32[88,128]{1,0:T(8,128)S(1)}, u32[]{:S(2)}, u32[]{:S(2)}) collective-permute-start(f32[88,128]{1,0:T(8,128)} %get-tuple-element.19), channel_id=1, source_target_pairs={{0,508},{4,480},{8,484},{12,488},{16,492},{20,496},{24,500},{28,50... | collective-permute-start | bytes 135176 | tf_op jit(solution)/shard_map/ppermute | solution.py:421
  21.6 8.2 %collective-permute-start = (f32[88,128]{1,0:T(8,128)}, f32[88,128]{1,0:T(8,128)S(1)}, u32[]{:S(2)}, u32[]{:S(2)}) collective-permute-start(f32[88,128]{1,0:T(8,128)} %get-tuple-element.16.own_ref), channel_id=1, source_target_pairs={{0,480},{32,0},{64,32},{96,64},{128,96},{160,128},{192,160},{224,1... | collective-permute-start | bytes 135176 | tf_op jit(solution)/shard_map/ppermute | solution.py:421
  24.6 5.2 %copy-start.1 = (f32[88,128]{1,0:T(8,128)S(1)}, f32[88,128]{1,0:T(8,128)}, u32[]{:S(2)}) copy-start(f32[88,128]{1,0:T(8,128)} %get-tuple-element.16.own_ref) | copy-start | bytes 135172
  24.6 5.2 %copy-start.2 = (f32[16,128]{1,0:T(8,128)S(1)}, f32[16,128]{1,0:T(8,128)}, u32[]{:S(2)}) copy-start(f32[16,128]{1,0:T(8,128)} %get-tuple-element.17.rest_ref) | copy-start | bytes 24580
  24.6 18.4 %all-to-all-start = ((f32[32,16,128]{2,1,0:T(8,128)}), f32[32,16,128]{2,1,0:T(8,128)S(1)}, u32[]{:S(2)}, u32[]{:S(2)}) async-start(f32[32,16,128]{2,1,0:T(8,128)} %get-tuple-element.14), calls=%async_computation | async-start | bytes 524288 | tf_op jit(solution)/shard_map/all_to_all | solution.py:445
  29.9 8.3 %copy-start = (f32[128,128]{1,0:T(8,128)S(1)}, f32[128,128]{1,0:T(8,128)}, u32[]{:S(2)}) copy-start(f32[128,128]{1,0:T(8,128)} %mix_ref.1) | copy-start | bytes 196612
  29.9 8.3 %copy-start.3 = (f32[8,128]{1,0:T(8,128)S(1)}, f32[8,128]{1,0:T(8,128)}, u32[]{:S(2)}) copy-start(f32[8,128]{1,0:T(8,128)} %radial_ref.1) | copy-start | bytes 12292
  29.9 8.2 %copy-start.4 = (f32[8,128]{1,0:T(8,128)S(1)}, f32[8,128]{1,0:T(8,128)}, u32[]{:S(2)}) copy-start(f32[8,128]{1,0:T(8,128)} %vector_ref.1) | copy-start | bytes 12292
  29.9 8.2 %copy-start.5 = (s32[2,2,2,8]{3,2,1,0:T(2,128)S(1)}, s32[2,2,2,8]{3,2,1,0:T(2,128)}, u32[]{:S(2)}) copy-start(s32[2,2,2,8]{3,2,1,0:T(2,128)} %species_ref.1) | copy-start | bytes 772
  29.9 8.2 %collective-permute-start.3 = (f32[320,128]{1,0:T(8,128)S(1)}, f32[320,128]{1,0:T(8,128)S(1)}, u32[]{:S(2)}, u32[]{:S(2)}) collective-permute-start(f32[320,128]{1,0:T(8,128)S(1)} %shard_map.124), channel_id=1, source_target_pairs={{0,3},{1,0},{2,1},{3,2},{4,7},{5,4},{6,5},{7,6},{8,11},{9,8},{10,9... | collective-permute-start | bytes 491528 | tf_op jit(solution)/shard_map/ppermute | solution.py:421
  38.1 0.7 copy-start.6
  38.1 0.7 copy-start.7

commit v3 on v2

--- a/solution.py
+++ b/solution.py
@@ -15,7 +15,8 @@
 HIGH = lax.Precision.HIGHEST
 F32 = jnp.float32
 BF16 = jnp.bfloat16
-STACK_MICROS = 50
+STACK_Y_MICROS = 50
+STACK_Z_MICROS = 1
 WAVES_MICROS = 500
 SHORT_MICROS = 1
 PACK_ROOM = 60
@@ -38,6 +39,16 @@
     )
 
 
+def split_left(value):
+    high, low = split(value)
+    return jnp.concatenate([high, low, high], 1)
+
+
+def split_right(value, axis):
+    high, low = split(value)
+    return jnp.concatenate([high, high, low], axis)
+
+
 def swap_halves(value):
     return pltpu.roll(value, 64, value.ndim - 1)
 
@@ -45,7 +56,14 @@
 def position_rows(pos_ref, lane):
     pieces = [pos_ref[x, y, d] for x in range(2) for y in range(2) for d in range(3)]
     spread = (iota((8, 128), 1) % 8 == iota((8, 128), 0)).astype(F32)
-    wide = contract(jnp.concatenate(pieces, 0), spread, (((1,), (0,))), HIGH)
+    pieces = jnp.concatenate(pieces, 0)
+    first, rest = split(pieces)
+    last = (pieces - first.astype(F32) - rest.astype(F32)).astype(BF16)
+    wide = contract(
+        jnp.concatenate([first, rest, last], 1),
+        jnp.concatenate([spread] * 3, 0).astype(BF16),
+        (((1,), (0,))),
+    )
     rows = []
     for d in range(3):
         row = jnp.zeros((1, 128), F32)
@@ -57,9 +75,27 @@
 
 
 def pack_kernel(
-    feat_ref, pos_ref, count_ref, near_ref, charge_ref,
-    to_x_ref, to_y_ref, to_xy_ref, rest_ref, message_ref,
+    feat_hbm, pos_hbm, count_hbm, near_hbm, charge_hbm, weight_hbm, shift_hbm,
+    slab_ref, rest_ref, extra_ref, message_ref,
+    feat_ref, pos_ref, count_ref, near_ref, charge_ref, weight_ref, shift_ref, arrived,
 ):
+    copies = [
+        pltpu.make_async_copy(source, target, arrived.at[at])
+        for at, (source, target) in enumerate(
+            (
+                (feat_hbm, feat_ref), (pos_hbm, pos_ref), (count_hbm, count_ref),
+                (near_hbm, near_ref), (charge_hbm, charge_ref), (weight_hbm, weight_ref),
+                (shift_hbm, shift_ref),
+            )
+        )
+    ]
+    for copy in copies:
+        copy.start()
+    for copy in copies:
+        copy.wait()
+    extra_ref[...] = jnp.zeros((8, 128), F32)
+    extra_ref[0:1] = weight_ref[...]
+    extra_ref[1:2, 0:8] = shift_ref[...]
     row = iota((64, 128), 0)
     lane = iota((8, 128), 1)
     count_col = jnp.zeros((64, 128), jnp.int32)
@@ -72,7 +108,9 @@
     occupied_row = (lane % 8 < count_row).astype(F32)
     masked = feat_ref[...] * occupied
     charges = contract(
-        charge_ref[...], jnp.concatenate([masked, masked], 0), (((1,), (1,))), HIGH
+        split_left(charge_ref[...]),
+        split_right(jnp.concatenate([masked, masked], 0), 1),
+        (((1,), (1,))),
     )
     sub = iota((8, 128), 0)
     tile = position_rows(pos_ref, lane)
@@ -86,11 +124,13 @@
     )
     places = tile + corner.astype(F32)
     lane_low = lane < 64
-    message = jnp.concatenate(
-        [jnp.where(lane_low, charges[0:8], charges[8:16]), places], 0
-    )
+    charges = jnp.where(lane_low, charges[0:8], charges[8:16])
+    places = jnp.where(lane_low, places, swap_halves(pltpu.roll(places, 7, 0)))
+    places = jnp.concatenate([places[0:1], places[2:3]], 0)
+    pieces = [charges[2 * k : 2 * k + 2] for k in range(4)] + [places]
     for member in range(message_ref.shape[0]):
-        message_ref[member] = message
+        for k in range(5):
+            message_ref[member, k] = pieces[k]
     turned = jnp.concatenate(
         [jnp.zeros((32, 128), F32), tile, jnp.zeros((88, 128), F32)], 0
     ).T
@@ -108,21 +148,29 @@
     block = (spot_z >> 1) * 4 + (spot_y >> 1) * 2 + (spot_x >> 1)
     cell = (spot_x & 1) * 4 + (spot_y & 1) * 2 + (spot_z & 1)
     target = (block * 64 + cell * 8 + slot).astype(F32)
-    for ref, first in ((to_xy_ref, 0), (to_x_ref, 16), (to_y_ref, 32)):
-        ref[0:64] = masked
-        ref[64:72] = tile
-        ref[72:88] = turned[first : first + 16]
-        ref[72:88, 0:32] = target[first : first + 16]
-    rest_ref[...] = turned[48:64]
-    rest_ref[:, 0:32] = target[48:64]
-
-
-def stack_kernel(own_ref, rest_ref, in_x_ref, in_y_ref, in_xy_ref, out_ref):
-    for block, ref in enumerate((own_ref, in_x_ref, in_y_ref, in_xy_ref)):
-        out_ref[72 * block : 72 * block + 72] = ref[0:72]
-    out_ref[288:296] = rest_ref[0:8]
-    for block, ref in enumerate((in_x_ref, in_y_ref, in_xy_ref)):
-        out_ref[296 + 8 * block : 304 + 8 * block] = ref[72:80]
+    slab_ref[0:64] = masked
+    slab_ref[64:72] = tile
+    slab_ref[72:104] = turned[0:32]
+    slab_ref[72:104, 0:32] = target[0:32]
+    rest_ref[...] = turned[32:64]
+    rest_ref[:, 0:32] = target[32:64]
+
+
+def stack_y_kernel(own_ref, rest_ref, in_x_ref, out_ref):
+    out_ref[0:72] = own_ref[0:72]
+    out_ref[72:144] = in_x_ref[0:72]
+    out_ref[144:160] = rest_ref[0:16]
+    out_ref[160:176] = in_x_ref[72:88]
+
+
+def stack_z_kernel(own_ref, rest_ref, in_x_ref, in_y_ref, out_ref):
+    out_ref[0:72] = own_ref[0:72]
+    out_ref[72:144] = in_x_ref[0:72]
+    out_ref[144:288] = in_y_ref[0:144]
+    out_ref[288:296] = rest_ref[16:24]
+    out_ref[296:304] = in_x_ref[88:96]
+    out_ref[304:312] = in_y_ref[144:152]
+    out_ref[312:320] = in_y_ref[160:168]
 
 
 def wave_numbers(member, shape, dim):
@@ -153,11 +201,22 @@
     low = iota((8, 128), 1) < 64
     upper, lower, places = [], [], []
     for pair in range(16):
-        first, second = atoms_ref[2 * pair], atoms_ref[2 * pair + 1]
-        turned_first, turned_second = swap_halves(first), swap_halves(second)
-        upper.append(jnp.where(low, first[0:8], turned_second[0:8]))
-        lower.append(jnp.where(low, turned_first[0:8], second[0:8]))
-        places.append(jnp.where(low, first[8:16], turned_second[8:16]))
+        first, second = atoms_ref[20 * pair : 20 * pair + 8], atoms_ref[20 * pair + 10 : 20 * pair + 18]
+        upper.append(jnp.where(low, first, swap_halves(second)))
+        lower.append(jnp.where(low, swap_halves(first), second))
+        first, second = (
+            atoms_ref[20 * pair + 8 : 20 * pair + 10],
+            atoms_ref[20 * pair + 18 : 20 * pair + 20],
+        )
+        places.append(
+            jnp.concatenate(
+                [
+                    jnp.where(low[0:2], first, swap_halves(second)),
+                    jnp.where(low[0:2], swap_halves(first), second),
+                ],
+                0,
+            )
+        )
     charges = jnp.concatenate(
         [jnp.concatenate(upper, 1), jnp.concatenate(lower, 1)], 0
     )
@@ -165,8 +224,8 @@
     number_x, number_y, number_z = wave_numbers(member, (32, 1), 0)
     turns = (
         number_x * (places[0:1] * (1.0 / grid[0]))
-        + number_y * (places[1:2] * (1.0 / grid[1]))
-        + number_z * (places[2:3] * (1.0 / grid[2]))
+        + number_y * (places[2:3] * (1.0 / grid[1]))
+        + number_z * (places[1:2] * (1.0 / grid[2]))
     )
     sine, cosine = sine_cosine(turns)
     phases = jnp.concatenate([cosine, sine], 0)
@@ -178,17 +237,6 @@
     partial = sums[0:16] + sums[16:32]
     partial = partial + swap_halves(partial)
     partial_ref[...] = jnp.where(low, partial[0:8], partial[8:16])
-
-
-def join_kernel(partial_ref, kept_ref, sent_ref, message_ref):
-    here = lax.axis_index("gx")
-    count = message_ref.shape[0]
-    partial = partial_ref[...]
-    for other in range(count):
-        message_ref[other, 0:8] = partial
-        message_ref[other, 8:16] = jnp.zeros((8, 128), F32)
-    message_ref[here, 8:16] = kept_ref[...]
-    message_ref[(here + 1) % count, 8:16] = sent_ref[...]
 
 
 def field_kernel(grid, scale, sums_ref, phase_ref, charge_ref, out_ref):
@@ -247,11 +295,11 @@
 
 
 def short_kernel(
-    own_ref, rest_ref, in_x_ref, in_y_ref, in_xy_ref, in_z_ref,
-    radial_ref, vector_ref, mix_ref, out_weight_ref, species_ref, shift_ref, kept_ref, sent_ref,
+    own_ref, rest_ref, in_x_ref, in_y_ref, in_z_ref, extra_ref,
+    radial_ref, vector_ref, mix_ref, species_ref, partial_ref, message_ref,
 ):
     bases = [
-        (own_ref, 0), (in_x_ref, 0), (in_y_ref, 0), (in_xy_ref, 0),
+        (own_ref, 0), (in_x_ref, 0), (in_y_ref, 0), (in_y_ref, 72),
         (in_z_ref, 0), (in_z_ref, 72), (in_z_ref, 144), (in_z_ref, 216),
     ]
     feats = jnp.concatenate([ref[at : at + 64] for ref, at in bases], 0)
@@ -268,7 +316,7 @@
         )
     spots = jnp.concatenate(spots, 1)
     tiles = [
-        rest_ref[8:16], in_x_ref[80:88], in_y_ref[80:88], in_xy_ref[80:88],
+        rest_ref[24:32], in_x_ref[96:104], in_y_ref[152:160], in_y_ref[168:176],
         in_z_ref[288:296], in_z_ref[296:304], in_z_ref[304:312], in_z_ref[312:320],
     ]
     centres = jnp.concatenate(tiles, 0)
@@ -327,12 +375,12 @@
             sums[1 + a] = sums[1 + a] + made[64 * (1 + a) : 64 * (2 + a)] * vector_ref[b : b + 1]
     sums = [value * norm for value in sums]
     product = sums[0] + sums[1] * sums[1] + sums[2] * sums[2] + sums[3] * sums[3]
-    mixed = contract(product, mix_ref[...], (((1,), (0,))), HIGH)
+    mixed = contract(split_left(product), split_right(mix_ref[...], 0), (((1,), (0,))))
     gate = 1.0 / (1.0 + jnp.exp(-mixed))
-    out_weight = out_weight_ref[...]
+    out_weight = extra_ref[0:1]
     energy = jnp.sum((own + mixed * gate) * out_weight, 1, keepdims=True) * occupied
     slope = gate * (1.0 + mixed * (1.0 - gate)) * (out_weight * occupied)
-    grad = contract(slope, mix_ref[...], (((1,), (1,))), HIGH) * norm
+    grad = contract(split_left(slope), split_right(mix_ref[...], 1), (((1,), (1,)))) * norm
     grads = [grad] + [2.0 * grad * sums[1 + a] for a in range(3)]
     right = jnp.concatenate([feat_high, feat_high, feat_low], 1)
     linear = [jnp.zeros((64, 512), F32) for _ in range(3)]
@@ -372,17 +420,25 @@
     spread = (iota((8, 128), 1) % 8 == iota((8, 128), 0)).astype(F32)
     kinds = contract(jnp.concatenate(kinds, 0).astype(F32), spread, (((1,), (0,))))
     shift = jnp.zeros((8, 128), F32)
-    for name in range(shift_ref.shape[1]):
-        shift = jnp.where(kinds == float(name), shift_ref[:, name : name + 1], shift)
+    for name in range(8):
+        shift = jnp.where(kinds == float(name), extra_ref[1:2, name : name + 1], shift)
     mine = iota((8, 128), 1) // 8 == iota((8, 128), 0)
     shift = jnp.sum(jnp.where(mine, shift, 0.0), 0, keepdims=True) * own_ref[67:68]
     shift = jnp.where(iota((4, 128), 0) == 0, shift, 0.0)
+    kept, sent = [], []
     for half in range(2):
         first, second = (rows[:, 128 * k : 128 * k + 128] for k in (2 * half, 2 * half + 1))
-        at = slice(4 * half, 4 * half + 4)
         first = first + shift if half == 0 else first
-        kept_ref[at] = jnp.where(low, first, swap_halves(second))
-        sent_ref[at] = jnp.where(low, swap_halves(first), second)
+        kept.append(jnp.where(low, first, swap_halves(second)))
+        sent.append(jnp.where(low, swap_halves(first), second))
+    here = lax.axis_index("gx")
+    count = message_ref.shape[0]
+    partial = partial_ref[...]
+    for other in range(count):
+        message_ref[other, 0:8] = partial
+        message_ref[other, 8:16] = jnp.zeros((8, 128), F32)
+    message_ref[here, 8:16] = jnp.concatenate(kept, 0)
+    message_ref[(here + 1) % count, 8:16] = jnp.concatenate(sent, 0)
 
 
 def last_kernel(parts_ref, energy_ref, force_ref):
@@ -432,22 +488,32 @@
         cells_z * lax.axis_size("gz"),
     )
     scale = 1.0 / math.sqrt(grid[0] * grid[1] * grid[2] * slots_cell * MODES)
-    to_x, to_y, to_xy, rest, message = call(
-        pack_kernel,
-        [(88, 128), (88, 128), (88, 128), (16, 128), (32, 16, 128)],
+    held = (
         features.reshape(64, 128),
         jnp.transpose(offsets, (0, 1, 3, 2, 4)),
         counts,
         neighbours.reshape(64, 32),
         w_charge.T,
-        room=PACK_ROOM,
-    )
-    atoms = lax.all_to_all(message, ("gy", "gz"), 0, 0)
-    in_x = moved(to_x, ("gx",), -1)
+        w_out.reshape(1, 128),
+        species_shift.reshape(1, 8),
+    )
+    slab, rest, extra, message = pl.pallas_call(
+        pack_kernel,
+        out_shape=[
+            jax.ShapeDtypeStruct(shape, F32)
+            for shape in [(104, 128), (32, 128), (8, 128), (32, 5, 2, 128)]
+        ],
+        in_specs=[pl.BlockSpec(memory_space=pl.ANY)] * len(held),
+        scratch_shapes=[pltpu.VMEM(value.shape, value.dtype) for value in held]
+        + [pltpu.SemaphoreType.DMA((len(held),))],
+        compiler_params=pltpu.CompilerParams(vmem_limit_bytes=PACK_ROOM * 1024 * 1024),
+    )(*held)
+    in_x = moved(slab, ("gx",), -1)
+    atoms = lax.all_to_all(message, ("gy", "gz"), 0, 0).reshape(320, 128)
+    (to_y,) = call(stack_y_kernel, [(176, 128)], slab, rest, in_x, micros=STACK_Y_MICROS)
     in_y = moved(to_y, ("gy",), -1)
-    in_xy = moved(to_xy, ("gx", "gy"), -1, -1)
     (to_z,) = call(
-        stack_kernel, [(320, 128)], to_x, rest, in_x, in_y, in_xy, micros=STACK_MICROS
+        stack_z_kernel, [(320, 128)], slab, rest, in_x, in_y, micros=STACK_Z_MICROS
     )
     in_z = moved(to_z, ("gz",), -1)
     partial, phases, charges = call(
@@ -456,14 +522,13 @@
         atoms,
         micros=WAVES_MICROS,
     )
-    kept, sent = call(
+    (joined,) = call(
         short_kernel,
-        [(8, 128), (8, 128)],
-        to_x, rest, in_x, in_y, in_xy, in_z,
-        w_radial, w_vector, w_mix, w_out.reshape(1, 128), species, species_shift.reshape(1, 8),
+        [(16, 16, 128)],
+        slab, rest, in_x, in_y, in_z, extra,
+        w_radial, w_vector, w_mix, species, partial,
         micros=SHORT_MICROS,
     )
-    (joined,) = call(join_kernel, [(16, 16, 128)], partial, kept, sent)
     sums = lax.all_to_all(joined, "gx", 0, 0)
     (parts,) = call(
         functools.partial(field_kernel, grid, scale), [(32, 4, 128)], sums, phases, charges

time: 73.4 us -> 71.5 us (0.974)
  starting transfers between devices: 29.4 us -> 27.3 us
  blocking collectives: 27.8 us -> 28.8 us
    ppermute x4 -> x3, starting transfers between devices: 24.3 us -> 15.7 us  [moved(): return lax.ppermute(value, axes, pairs)]
    all_to_all x1, starting transfers between devices: 5.18 us -> 11.6 us  [body(): atoms = lax.all_to_all(message, ('gy', 'gz'), 0, 0).reshape(320, 128)]
    pallas_call x7 -> x6, Pallas kernels: 8.23 us -> 5.91 us  [call(): pl.pallas_call(kernel, out_shape=[jax.ShapeDtypeStruct(shape, F32) for sh...]
    pallas_call x0 -> x1, Pallas kernels: none -> 1.91 us  [body(): pl.pallas_call(pack_kernel, out_shape=[jax.ShapeDtypeStruct(shape, F32) f...]
    all_to_all x1, blocking collectives: 14.6 us -> 15.3 us  [body(): parts = lax.all_to_all(parts, ('gy', 'gz'), 0, 0)]
    ppermute x4 -> x3, waiting for transfers between devices: 5.93 us -> 6.3 us  [moved(): return lax.ppermute(value, axes, pairs)]
  transfers between devices with their start and end apart: 5 -> 4, of which waited for: 1 -> 2; matrix products, arithmetic and copies ran while one was open for 0% -> 0% of each run, Pallas kernels for 6% -> 1%
where the time goes in v3:
time: 71.5 us; the launch traced here: 71.1 us
  blocking collectives  28.8 us (40%)
  starting transfers between devices  27.3 us (38%)
  Pallas kernels  7.82 us (11%)
  waiting for transfers between devices  6.31 us (9%)
  between operations  0.8 us (1%)
    ppermute x3, starting transfers between devices, moved(): return lax.ppermute(value, axes, pairs)  15.7 us
    all_to_all x1, blocking collectives, body(): parts = lax.all_to_all(parts, ('gy', 'gz'), 0, 0)  15.3 us
    all_to_all x1, blocking collectives, body(): sums = lax.all_to_all(joined, 'gx', 0, 0)  13.5 us
    all_to_all x1, starting transfers between devices, body(): atoms = lax.all_to_all(message, ('gy', 'gz'), 0, 0).reshape(320, 128)  11.6 us
    ppermute x3, waiting for transfers between devices, moved(): return lax.ppermute(value, axes, pairs)  6.3 us
    pallas_call x6, Pallas kernels, call(): pl.pallas_call(kernel, out_shape=[jax.ShapeDtypeStruct(shape, F32) for sh...  5.91 us
    pallas_call x1, Pallas kernels, body(): pl.pallas_call(pack_kernel, out_shape=[jax.ShapeDtypeStruct(shape, F32) f...  1.91 us
  transfers between devices with their start and end apart: 4, of which 2 were waited for; matrix products, arithmetic and copies ran while one was open for 0% of the time, Pallas kernels for 1%

profile of v3, /device:TPU:1, one launch (start us, length us, event | category | flops | bytes accessed | tf_op | source)
XLA Modules:
  0.0 71.1 jit_solution(13857257542815799493)
XLA Ops:
  0.6 1.9 %shard_map.122 = (f32[104,128]{1,0:T(8,128)}, f32[32,128]{1,0:T(8,128)}, f32[8,128]{1,0:T(8,128)}, f32[32,5,2,128]{3,2,1,0:T(2,128)}) custom-call(f32[64,128]{1,0:T(8,128)} %bitcast.9, f32[2,2,3,2,8]{4,3,2,1,0:T(2,128)} %bitcast.11, s32[2,2,2]{2,1,0:T(2,128)} %count_hbm.1, s32[64,32]{1,0:T(8,128)} %bitcast.10, f32[16,128]{1,0:T(8,128)} %bitcast.12, ...), custom_call_target="tpu_custom_call" | custom-call | tf_op jit(solution)/shard_map/pallas_call | solution.py:500
  2.5 8.4 %collective-permute-start = (f32[104,128]{1,0:T(8,128)}, f32[104,128]{1,0:T(8,128)S(1)}, u32[]{:S(2)}, u32[]{:S(2)}) collective-permute-start(f32[104,128]{1,0:T(8,128)} %get-tuple-element.11.own_ref), channel_id=1, source_target_pairs={{0,480},{32,0},{64,32},{96,64},{128,96},{160,128},{192,160},{224,1... | collective-permute-start | bytes 159752 | tf_op jit(solution)/shard_map/ppermute | solution.py:477
  10.9 0.0 copy-start
  10.9 0.0 copy-start.2
  11.0 11.6 %all-to-all-start = ((f32[32,5,2,128]{3,2,1,0:T(2,128)}), f32[32,5,2,128]{3,2,1,0:T(2,128)S(1)}, u32[]{:S(2)}, u32[]{:S(2)}) async-start(f32[32,5,2,128]{3,2,1,0:T(2,128)} %get-tuple-element.14), calls=%async_computation | async-start | bytes 327680 | tf_op jit(solution)/shard_map/all_to_all | solution.py:512
  22.6 0.0 collective-permute-done.in_x_ref
  22.6 0.0 copy-done
  22.6 0.0 copy-done.2
  22.6 4.6 %collective-permute-start.1 = (f32[176,128]{1,0:T(8,128)S(1)}, f32[176,128]{1,0:T(8,128)S(1)}, u32[]{:S(2)}, u32[]{:S(2)}) collective-permute-start(f32[176,128]{1,0:T(8,128)S(1)} %shard_map.123), channel_id=1, source_target_pairs={{0,28},{4,0},{8,4},{12,8},{16,12},{20,16},{24,20},{28,24},{1,29},{... | collective-permute-start | bytes 270344 | tf_op jit(solution)/shard_map/ppermute | solution.py:477
  27.2 3.1 %collective-permute-done.1.in_y_ref = f32[176,128]{1,0:T(8,128)S(1)} collective-permute-done((f32[176,128]{1,0:T(8,128)S(1)}, f32[176,128]{1,0:T(8,128)S(1)}, u32[]{:S(2)}, u32[]{:S(2)}) %collective-permute-start.1) | collective-permute-done | bytes 90144 | tf_op jit(solution)/shard_map/ppermute | solution.py:477
  30.3 2.8 %collective-permute-start.2 = (f32[320,128]{1,0:T(8,128)S(1)}, f32[320,128]{1,0:T(8,128)S(1)}, u32[]{:S(2)}, u32[]{:S(2)}) collective-permute-start(f32[320,128]{1,0:T(8,128)S(1)} %shard_map.124), channel_id=1, source_target_pairs={{0,3},{1,0},{2,1},{3,2},{4,7},{5,4},{6,5},{7,6},{8,11},{9,8},{10,9... | collective-permute-start | bytes 491528 | tf_op jit(solution)/shard_map/ppermute | solution.py:477
  33.1 0.0 all-to-all-done
  33.1 0.0 copy-start.1
  33.1 0.0 copy-start.3
  33.1 0.0 copy-start.4
  33.1 0.0 copy-start.5
  33.1 0.0 copy-start.6
  33.1 0.7 %shard_map.125 = (f32[8,128]{1,0:T(8,128)S(1)}, f32[64,2048]{1,0:T(8,128)S(1)}, f32[16,2048]{1,0:T(8,128)S(1)}) custom-call(f32[320,128]{1,0:T(8,128)S(1)} %bitcast.8), custom_call_target="tpu_custom_call" | custom-call | flops 49999998976 | bytes 150000000 | tf_op jit(solution)/shard_map/pallas_call | solution.py:460
  33.9 3.2 %collective-permute-done.2.in_z_ref = f32[320,128]{1,0:T(8,128)S(1)} collective-permute-done((f32[320,128]{1,0:T(8,128)S(1)}, f32[320,128]{1,0:T(8,128)S(1)}, u32[]{:S(2)}, u32[]{:S(2)}) %collective-permute-start.2) | collective-permute-done | bytes 163872 | tf_op jit(solution)/shard_map/ppermute | solution.py:477
  37.1 0.0 copy-done.1
  37.1 0.0 copy-done.3
  37.1 0.0 copy-done.4
  37.1 0.0 copy-done.5
  37.1 0.0 copy-done.6
  37.1 3.9 %shard_map.126 = f32[16,16,128]{2,1,0:T(8,128)S(1)} custom-call(f32[104,128]{1,0:T(8,128)S(1)} %copy-done, f32[32,128]{1,0:T(8,128)S(1)} %copy-done.2, f32[104,128]{1,0:T(8,128)S(1)} %collective-permute-done.in_x_ref, f32[176,128]{1,0:T(8,128)S(1)} %collective-permute-done.1.in_y_ref, f32[320,128]{1,0:T(8,128)S(1)} %collective-permute-done.2.in_z_ref, ...), custom_call_target="tpu_custom_call" | custom-call | flops 100000000 | bytes 300000 | tf_op jit(solution)/shard_map/pallas_call | solution.py:460
  41.0 13.5 %all_to_all.15.sums_ref = f32[16,16,128]{2,1,0:T(8,128)S(1)} all-to-all(f32[16,16,128]{2,1,0:T(8,128)S(1)} %shard_map.126), channel_id=1, replica_groups=mesh['gx'=16,'gy'=8,'gz'=4] {'gx'}, dimensions={0} | all-to-all | bytes 262144 | tf_op jit(solution)/shard_map/all_to_all | solution.py:532
  54.5 0.5 shard_map.127
  55.0 15.3 %all_to_all.16.parts_ref = f32[32,4,128]{2,1,0:T(4,128)S(1)} all-to-all(f32[32,4,128]{2,1,0:T(4,128)S(1)} %shard_map.127), channel_id=1, replica_groups=mesh['gx'=16,'gy'=8,'gz'=4] {'gy','gz'}, dimensions={0} | all-to-all | bytes 131072 | tf_op jit(solution)/shard_map/all_to_all | solution.py:536
  70.3 0.8 %shard_map.128 = (f32[2,2,2,8]{3,2,1,0:T(2,128)}, f32[2,2,3,2,8]{4,3,2,1,0:T(2,128)}) custom-call(f32[32,4,128]{2,1,0:T(4,128)S(1)} %all_to_all.16.parts_ref), custom_call_target="tpu_custom_call" | custom-call | flops 1000000000 | bytes 3000000 | tf_op jit(solution)/shard_map/pallas_call | solution.py:460
  (2 shorter events, 0.0 us)
Async XLA Ops:
  2.5 20.0 %collective-permute-start = (f32[104,128]{1,0:T(8,128)}, f32[104,128]{1,0:T(8,128)S(1)}, u32[]{:S(2)}, u32[]{:S(2)}) collective-permute-start(f32[104,128]{1,0:T(8,128)} %get-tuple-element.11.own_ref), channel_id=1, source_target_pairs={{0,480},{32,0},{64,32},{96,64},{128,96},{160,128},{192,160},{224,1... | collective-permute-start | bytes 159752 | tf_op jit(solution)/shard_map/ppermute | solution.py:477
  10.9 11.6 %copy-start = (f32[104,128]{1,0:T(8,128)S(1)}, f32[104,128]{1,0:T(8,128)}, u32[]{:S(2)}) copy-start(f32[104,128]{1,0:T(8,128)} %get-tuple-element.11.own_ref) | copy-start | bytes 159748
  10.9 11.6 %copy-start.2 = (f32[32,128]{1,0:T(8,128)S(1)}, f32[32,128]{1,0:T(8,128)}, u32[]{:S(2)}) copy-start(f32[32,128]{1,0:T(8,128)} %get-tuple-element.12.rest_ref) | copy-start | bytes 49156
  11.0 22.1 %all-to-all-start = ((f32[32,5,2,128]{3,2,1,0:T(2,128)}), f32[32,5,2,128]{3,2,1,0:T(2,128)S(1)}, u32[]{:S(2)}, u32[]{:S(2)}) async-start(f32[32,5,2,128]{3,2,1,0:T(2,128)} %get-tuple-element.14), calls=%async_computation | async-start | bytes 327680 | tf_op jit(solution)/shard_map/all_to_all | solution.py:512
  22.6 7.6 %collective-permute-start.1 = (f32[176,128]{1,0:T(8,128)S(1)}, f32[176,128]{1,0:T(8,128)S(1)}, u32[]{:S(2)}, u32[]{:S(2)}) collective-permute-start(f32[176,128]{1,0:T(8,128)S(1)} %shard_map.123), channel_id=1, source_target_pairs={{0,28},{4,0},{8,4},{12,8},{16,12},{20,16},{24,20},{28,24},{1,29},{... | collective-permute-start | bytes 270344 | tf_op jit(solution)/shard_map/ppermute | solution.py:477
  30.3 6.8 %collective-permute-start.2 = (f32[320,128]{1,0:T(8,128)S(1)}, f32[320,128]{1,0:T(8,128)S(1)}, u32[]{:S(2)}, u32[]{:S(2)}) collective-permute-start(f32[320,128]{1,0:T(8,128)S(1)} %shard_map.124), channel_id=1, source_target_pairs={{0,3},{1,0},{2,1},{3,2},{4,7},{5,4},{6,5},{7,6},{8,11},{9,8},{10,9... | collective-permute-start | bytes 491528 | tf_op jit(solution)/shard_map/ppermute | solution.py:477
  33.1 4.0 %copy-start.1 = (f32[128,128]{1,0:T(8,128)S(1)}, f32[128,128]{1,0:T(8,128)}, u32[]{:S(2)}) copy-start(f32[128,128]{1,0:T(8,128)} %mix_ref.1) | copy-start | bytes 196612
  33.1 4.0 %copy-start.3 = (f32[8,128]{1,0:T(8,128)S(1)}, f32[8,128]{1,0:T(8,128)}, u32[]{:S(2)}) copy-start(f32[8,128]{1,0:T(8,128)} %radial_ref.1) | copy-start | bytes 12292
  33.1 4.0 %copy-start.4 = (f32[8,128]{1,0:T(8,128)S(1)}, f32[8,128]{1,0:T(8,128)}, u32[]{:S(2)}) copy-start(f32[8,128]{1,0:T(8,128)} %vector_ref.1) | copy-start | bytes 12292
  33.1 4.0 %copy-start.5 = (s32[2,2,2,8]{3,2,1,0:T(2,128)S(1)}, s32[2,2,2,8]{3,2,1,0:T(2,128)}, u32[]{:S(2)}) copy-start(s32[2,2,2,8]{3,2,1,0:T(2,128)} %species_ref.1) | copy-start | bytes 772
  33.1 4.0 %copy-start.6 = (f32[8,128]{1,0:T(8,128)S(1)}, f32[8,128]{1,0:T(8,128)}, u32[]{:S(2)}) copy-start(f32[8,128]{1,0:T(8,128)} %get-tuple-element.13.extra_ref) | copy-start | bytes 12292

commit v4 on v3

--- a/solution.py
+++ b/solution.py
@@ -15,8 +15,8 @@
 HIGH = lax.Precision.HIGHEST
 F32 = jnp.float32
 BF16 = jnp.bfloat16
-STACK_Y_MICROS = 50
-STACK_Z_MICROS = 1
+STACK_Z_MICROS = 50
+STACK_Y_MICROS = 1
 WAVES_MICROS = 500
 SHORT_MICROS = 1
 PACK_ROOM = 60
@@ -156,21 +156,23 @@
     rest_ref[:, 0:32] = target[32:64]
 
 
-def stack_y_kernel(own_ref, rest_ref, in_x_ref, out_ref):
+def stack_z_kernel(own_ref, rest_ref, in_x_ref, out_ref):
     out_ref[0:72] = own_ref[0:72]
     out_ref[72:144] = in_x_ref[0:72]
-    out_ref[144:160] = rest_ref[0:16]
-    out_ref[160:176] = in_x_ref[72:88]
-
-
-def stack_z_kernel(own_ref, rest_ref, in_x_ref, in_y_ref, out_ref):
+    out_ref[144:152] = rest_ref[0:8]
+    out_ref[152:160] = rest_ref[16:24]
+    out_ref[160:168] = in_x_ref[72:80]
+    out_ref[168:176] = in_x_ref[88:96]
+
+
+def stack_y_kernel(own_ref, rest_ref, in_x_ref, in_z_ref, out_ref):
     out_ref[0:72] = own_ref[0:72]
     out_ref[72:144] = in_x_ref[0:72]
-    out_ref[144:288] = in_y_ref[0:144]
-    out_ref[288:296] = rest_ref[16:24]
-    out_ref[296:304] = in_x_ref[88:96]
-    out_ref[304:312] = in_y_ref[144:152]
-    out_ref[312:320] = in_y_ref[160:168]
+    out_ref[144:288] = in_z_ref[0:144]
+    out_ref[288:296] = rest_ref[8:16]
+    out_ref[296:304] = in_x_ref[80:88]
+    out_ref[304:312] = in_z_ref[144:152]
+    out_ref[312:320] = in_z_ref[160:168]
 
 
 def wave_numbers(member, shape, dim):
@@ -196,7 +198,7 @@
     return sine * angle, cosine
 
 
-def waves_kernel(grid, atoms_ref, partial_ref, phase_ref, charge_ref):
+def waves_kernel(grid, atoms_ref, message_ref, phase_ref, charge_ref):
     member = lax.axis_index("gy") * 4 + lax.axis_index("gz")
     low = iota((8, 128), 1) < 64
     upper, lower, places = [], [], []
@@ -236,16 +238,17 @@
     sums = contract(charge_stack, phase_stack, (((1,), (1,))))
     partial = sums[0:16] + sums[16:32]
     partial = partial + swap_halves(partial)
-    partial_ref[...] = jnp.where(low, partial[0:8], partial[8:16])
-
-
-def field_kernel(grid, scale, sums_ref, phase_ref, charge_ref, out_ref):
+    partial = jnp.where(low, partial[0:8], partial[8:16])
+    for other in range(message_ref.shape[0]):
+        message_ref[other] = partial
+
+
+def field_kernel(grid, scale, sums_ref, phase_ref, charge_ref, kept_ref, came_ref, out_ref):
     at_y, at_z = lax.axis_index("gy"), lax.axis_index("gz")
     member = at_y * 4 + at_z
     total = sums_ref[0]
     for other in range(1, sums_ref.shape[0]):
         total = total + sums_ref[other]
-    folded = total[8:16]
     turned = swap_halves(total)
     low_lane = iota((8, 128), 1) < 64
     total = jnp.concatenate(
@@ -255,7 +258,8 @@
         ],
         0,
     )
-    turned = turned[8:16]
+    folded = kept_ref[...] + came_ref[...]
+    turned = swap_halves(folded)
     two_pi = 2.0 * math.pi
     number_x, number_y, number_z = wave_numbers(member, (16, 128), 1)
     wave_x, wave_y, wave_z = (
@@ -296,11 +300,11 @@
 
 def short_kernel(
     own_ref, rest_ref, in_x_ref, in_y_ref, in_z_ref, extra_ref,
-    radial_ref, vector_ref, mix_ref, species_ref, partial_ref, message_ref,
+    radial_ref, vector_ref, mix_ref, species_ref, kept_ref, sent_ref,
 ):
     bases = [
         (own_ref, 0), (in_x_ref, 0), (in_y_ref, 0), (in_y_ref, 72),
-        (in_z_ref, 0), (in_z_ref, 72), (in_z_ref, 144), (in_z_ref, 216),
+        (in_z_ref, 0), (in_z_ref, 72), (in_y_ref, 144), (in_y_ref, 216),
     ]
     feats = jnp.concatenate([ref[at : at + 64] for ref, at in bases], 0)
     low_lane = iota((8, 128), 1) < 64
@@ -316,8 +320,8 @@
         )
     spots = jnp.concatenate(spots, 1)
     tiles = [
-        rest_ref[24:32], in_x_ref[96:104], in_y_ref[152:160], in_y_ref[168:176],
-        in_z_ref[288:296], in_z_ref[296:304], in_z_ref[304:312], in_z_ref[312:320],
+        rest_ref[24:32], in_x_ref[96:104], in_y_ref[288:296], in_y_ref[296:304],
+        in_z_ref[152:160], in_z_ref[168:176], in_y_ref[304:312], in_y_ref[312:320],
     ]
     centres = jnp.concatenate(tiles, 0)
     own = []
@@ -425,20 +429,11 @@
     mine = iota((8, 128), 1) // 8 == iota((8, 128), 0)
     shift = jnp.sum(jnp.where(mine, shift, 0.0), 0, keepdims=True) * own_ref[67:68]
     shift = jnp.where(iota((4, 128), 0) == 0, shift, 0.0)
-    kept, sent = [], []
     for half in range(2):
         first, second = (rows[:, 128 * k : 128 * k + 128] for k in (2 * half, 2 * half + 1))
         first = first + shift if half == 0 else first
-        kept.append(jnp.where(low, first, swap_halves(second)))
-        sent.append(jnp.where(low, swap_halves(first), second))
-    here = lax.axis_index("gx")
-    count = message_ref.shape[0]
-    partial = partial_ref[...]
-    for other in range(count):
-        message_ref[other, 0:8] = partial
-        message_ref[other, 8:16] = jnp.zeros((8, 128), F32)
-    message_ref[here, 8:16] = jnp.concatenate(kept, 0)
-    message_ref[(here + 1) % count, 8:16] = jnp.concatenate(sent, 0)
+        kept_ref[4 * half : 4 * half + 4] = jnp.where(low, first, swap_halves(second))
+        sent_ref[4 * half : 4 * half + 4] = jnp.where(low, swap_halves(first), second)
 
 
 def last_kernel(parts_ref, energy_ref, force_ref):
@@ -510,28 +505,31 @@
     )(*held)
     in_x = moved(slab, ("gx",), -1)
     atoms = lax.all_to_all(message, ("gy", "gz"), 0, 0).reshape(320, 128)
-    (to_y,) = call(stack_y_kernel, [(176, 128)], slab, rest, in_x, micros=STACK_Y_MICROS)
+    (to_z,) = call(stack_z_kernel, [(176, 128)], slab, rest, in_x, micros=STACK_Z_MICROS)
+    in_z = moved(to_z, ("gz",), -1)
+    (to_y,) = call(
+        stack_y_kernel, [(320, 128)], slab, rest, in_x, in_z, micros=STACK_Y_MICROS
+    )
     in_y = moved(to_y, ("gy",), -1)
-    (to_z,) = call(
-        stack_z_kernel, [(320, 128)], slab, rest, in_x, in_y, micros=STACK_Z_MICROS
-    )
-    in_z = moved(to_z, ("gz",), -1)
     partial, phases, charges = call(
         functools.partial(waves_kernel, grid),
-        [(8, 128), (64, 2048), (16, 2048)],
+        [(16, 8, 128), (64, 2048), (16, 2048)],
         atoms,
         micros=WAVES_MICROS,
     )
-    (joined,) = call(
+    sums = lax.all_to_all(partial, "gx", 0, 0)
+    kept, sent = call(
         short_kernel,
-        [(16, 16, 128)],
+        [(8, 128), (8, 128)],
         slab, rest, in_x, in_y, in_z, extra,
-        w_radial, w_vector, w_mix, species, partial,
+        w_radial, w_vector, w_mix, species,
         micros=SHORT_MICROS,
     )
-    sums = lax.all_to_all(joined, "gx", 0, 0)
+    came = moved(sent, ("gx",), 1)
     (parts,) = call(
-        functools.partial(field_kernel, grid, scale), [(32, 4, 128)], sums, phases, charges
+        functools.partial(field_kernel, grid, scale),
+        [(32, 4, 128)],
+        sums, phases, charges, kept, came,
     )
     parts = lax.all_to_all(parts, ("gy", "gz"), 0, 0)
     atom_energy, forces = call(last_kernel, [(2, 2, 2, 8), (2, 2, 3, 2, 8)], parts, room=LAST_ROOM)

time: 71.5 us -> 67.4 us (0.943)
  blocking collectives: 28.8 us -> 13.1 us
  starting transfers between devices: 27.3 us -> 34.7 us
  waiting for transfers between devices: 6.31 us -> 9.67 us
    all_to_all x1 -> x0, blocking collectives: 13.5 us -> none  [body(): sums = lax.all_to_all(joined, 'gx', 0, 0)]
    all_to_all x0 -> x1, starting transfers between devices: none -> 4.77 us  [body(): sums = lax.all_to_all(partial, 'gx', 0, 0)]
    ppermute x3 -> x4, waiting for transfers between devices: 6.3 us -> 9.66 us  [moved(): return lax.ppermute(value, axes, pairs)]
    ppermute x3 -> x4, starting transfers between devices: 15.7 us -> 18.4 us  [moved(): return lax.ppermute(value, axes, pairs)]
    all_to_all x1, blocking collectives: 15.3 us -> 13.1 us  [body(): parts = lax.all_to_all(parts, ('gy', 'gz'), 0, 0)]
  transfers between devices with their start and end apart: 4 -> 6, of which waited for: 2 -> 2; matrix products, arithmetic and copies ran while one was open for 0% -> 0% of each run, Pallas kernels for 1% -> 8%
where the time goes in v4:
time: 67.4 us; the launch traced here: 66.9 us
  starting transfers between devices  34.7 us (51%)
  blocking collectives  13.1 us (19%)
  waiting for transfers between devices  9.67 us (14%)
  Pallas kernels  8.48 us (13%)
  between operations  0.81 us (1%)
    ppermute x4, starting transfers between devices, moved(): return lax.ppermute(value, axes, pairs)  18.4 us
    all_to_all x1, blocking collectives, body(): parts = lax.all_to_all(parts, ('gy', 'gz'), 0, 0)  13.1 us
    all_to_all x1, starting transfers between devices, body(): atoms = lax.all_to_all(message, ('gy', 'gz'), 0, 0).reshape(320, 128)  11.6 us
    ppermute x4, waiting for transfers between devices, moved(): return lax.ppermute(value, axes, pairs)  9.66 us
    pallas_call x6, Pallas kernels, call(): pl.pallas_call(kernel, out_shape=[jax.ShapeDtypeStruct(shape, F32) for sh...  6.57 us
    all_to_all x1, starting transfers between devices, body(): sums = lax.all_to_all(partial, 'gx', 0, 0)  4.77 us
    pallas_call x1, Pallas kernels, body(): pl.pallas_call(pack_kernel, out_shape=[jax.ShapeDtypeStruct(shape, F32) f...  1.91 us
  transfers between devices with their start and end apart: 6, of which 2 were waited for; matrix products, arithmetic and copies ran while one was open for 0% of the time, Pallas kernels for 8%

profile of v4, /device:TPU:1, one launch (start us, length us, event | category | flops | bytes accessed | tf_op | source)
XLA Modules:
  0.0 66.9 jit_solution(4162522529679728908)
XLA Ops:
  0.6 1.9 %shard_map.122 = (f32[104,128]{1,0:T(8,128)}, f32[32,128]{1,0:T(8,128)}, f32[8,128]{1,0:T(8,128)}, f32[32,5,2,128]{3,2,1,0:T(2,128)}) custom-call(f32[64,128]{1,0:T(8,128)} %bitcast.9, f32[2,2,3,2,8]{4,3,2,1,0:T(2,128)} %bitcast.11, s32[2,2,2]{2,1,0:T(2,128)} %count_hbm.1, s32[64,32]{1,0:T(8,128)} %bitcast.10, f32[16,128]{1,0:T(8,128)} %bitcast.12, ...), custom_call_target="tpu_custom_call" | custom-call | tf_op jit(solution)/shard_map/pallas_call | solution.py:495
  2.5 8.4 %collective-permute-start = (f32[104,128]{1,0:T(8,128)}, f32[104,128]{1,0:T(8,128)S(1)}, u32[]{:S(2)}, u32[]{:S(2)}) collective-permute-start(f32[104,128]{1,0:T(8,128)} %get-tuple-element.17.own_ref), channel_id=1, source_target_pairs={{0,480},{32,0},{64,32},{96,64},{128,96},{160,128},{192,160},{224,1... | collective-permute-start | bytes 159752 | tf_op jit(solution)/shard_map/ppermute | solution.py:472
  10.9 0.0 copy-start
  11.0 0.0 copy-start.2
  11.0 11.6 %all-to-all-start = ((f32[32,5,2,128]{3,2,1,0:T(2,128)}), f32[32,5,2,128]{3,2,1,0:T(2,128)S(1)}, u32[]{:S(2)}, u32[]{:S(2)}) async-start(f32[32,5,2,128]{3,2,1,0:T(2,128)} %get-tuple-element.13), calls=%async_computation | async-start | bytes 327680 | tf_op jit(solution)/shard_map/all_to_all | solution.py:507
  22.6 0.0 collective-permute-done.in_x_ref
  22.6 0.0 copy-done
  22.6 0.0 copy-done.2
  22.6 2.1 %collective-permute-start.1 = (f32[176,128]{1,0:T(8,128)S(1)}, f32[176,128]{1,0:T(8,128)S(1)}, u32[]{:S(2)}, u32[]{:S(2)}) collective-permute-start(f32[176,128]{1,0:T(8,128)S(1)} %shard_map.124), channel_id=1, source_target_pairs={{0,3},{1,0},{2,1},{3,2},{4,7},{5,4},{6,5},{7,6},{8,11},{9,8},{10,9... | collective-permute-start | bytes 270344 | tf_op jit(solution)/shard_map/ppermute | solution.py:472
  24.8 4.6 %collective-permute-done.1.in_z_ref = f32[176,128]{1,0:T(8,128)S(1)} collective-permute-done((f32[176,128]{1,0:T(8,128)S(1)}, f32[176,128]{1,0:T(8,128)S(1)}, u32[]{:S(2)}, u32[]{:S(2)}) %collective-permute-start.1) | collective-permute-done | bytes 90144 | tf_op jit(solution)/shard_map/ppermute | solution.py:472
  29.4 4.6 %collective-permute-start.2 = (f32[320,128]{1,0:T(8,128)S(1)}, f32[320,128]{1,0:T(8,128)S(1)}, u32[]{:S(2)}, u32[]{:S(2)}) collective-permute-start(f32[320,128]{1,0:T(8,128)S(1)} %shard_map.125), channel_id=1, source_target_pairs={{0,28},{4,0},{8,4},{12,8},{16,12},{20,16},{24,20},{28,24},{1,29},{... | collective-permute-start | bytes 491528 | tf_op jit(solution)/shard_map/ppermute | solution.py:472
  34.0 0.0 all-to-all-done
  34.0 1.4 %shard_map.123 = (f32[16,8,128]{2,1,0:T(8,128)}, f32[64,2048]{1,0:T(8,128)S(1)}, f32[16,2048]{1,0:T(8,128)S(1)}) custom-call(f32[320,128]{1,0:T(8,128)S(1)} %bitcast.8), custom_call_target="tpu_custom_call" | custom-call | flops 49999998976 | bytes 150000000 | tf_op jit(solution)/shard_map/pallas_call | solution.py:455
  35.4 0.0 copy-start.1
  35.4 0.0 copy-start.3
  35.4 0.0 copy-start.4
  35.4 0.0 copy-start.5
  35.4 0.0 copy-start.6
  35.4 4.8 %all-to-all-start.1 = ((f32[16,8,128]{2,1,0:T(8,128)}), f32[16,8,128]{2,1,0:T(8,128)S(1)}, u32[]{:S(2)}, u32[]{:S(2)}) async-start(f32[16,8,128]{2,1,0:T(8,128)} %get-tuple-element.14), calls=%async_computation.1 | async-start | bytes 131072 | tf_op jit(solution)/shard_map/all_to_all | solution.py:520
  40.2 0.0 collective-permute-done.2.in_y_ref
  40.2 0.0 copy-done.1
  40.2 0.0 copy-done.3
  40.3 0.0 copy-done.4
  40.3 0.0 copy-done.5
  40.3 0.0 copy-done.6
  40.3 3.9 %shard_map.126 = (f32[8,128]{1,0:T(8,128)S(1)}, f32[8,128]{1,0:T(8,128)S(1)}) custom-call(f32[104,128]{1,0:T(8,128)S(1)} %copy-done, f32[32,128]{1,0:T(8,128)S(1)} %copy-done.2, f32[104,128]{1,0:T(8,128)S(1)} %collective-permute-done.in_x_ref, f32[320,128]{1,0:T(8,128)S(1)} %collective-permute-done.2.in_y_ref, ...), custom_call_target="tpu_custom_call" | custom-call | flops 100000000 | bytes 300000 | tf_op jit(solution)/shard_map/pallas_call | solution.py:455
  44.2 3.3 %collective-permute-start.3 = (f32[8,128]{1,0:T(8,128)S(1)}, f32[8,128]{1,0:T(8,128)S(1)}, u32[]{:S(2)}, u32[]{:S(2)}) collective-permute-start(f32[8,128]{1,0:T(8,128)S(1)} %get-tuple-element.21), channel_id=1, source_target_pairs={{0,32},{32,64},{64,96},{96,128},{128,160},{160,192},{192,224},{224... | collective-permute-start | bytes 12296 | tf_op jit(solution)/shard_map/ppermute | solution.py:472
  47.4 5.0 %collective-permute-done.3.came_ref = f32[8,128]{1,0:T(8,128)S(1)} collective-permute-done((f32[8,128]{1,0:T(8,128)S(1)}, f32[8,128]{1,0:T(8,128)S(1)}, u32[]{:S(2)}, u32[]{:S(2)}) %collective-permute-start.3) | collective-permute-done | bytes 4128 | tf_op jit(solution)/shard_map/ppermute | solution.py:472
  52.4 0.0 all-to-all-done.1.sums_ref
  52.5 0.5 shard_map.127
  52.9 13.1 %all_to_all.15.parts_ref = f32[32,4,128]{2,1,0:T(4,128)S(1)} all-to-all(f32[32,4,128]{2,1,0:T(4,128)S(1)} %shard_map.127), channel_id=1, replica_groups=mesh['gx'=16,'gy'=8,'gz'=4] {'gy','gz'}, dimensions={0} | all-to-all | bytes 131072 | tf_op jit(solution)/shard_map/all_to_all | solution.py:534
  66.1 0.8 %shard_map.128 = (f32[2,2,2,8]{3,2,1,0:T(2,128)}, f32[2,2,3,2,8]{4,3,2,1,0:T(2,128)}) custom-call(f32[32,4,128]{2,1,0:T(4,128)S(1)} %all_to_all.15.parts_ref), custom_call_target="tpu_custom_call" | custom-call | flops 1000000000 | bytes 3000000 | tf_op jit(solution)/shard_map/pallas_call | solution.py:455
  (2 shorter events, 0.0 us)
Async XLA Ops:
  2.5 20.0 %collective-permute-start = (f32[104,128]{1,0:T(8,128)}, f32[104,128]{1,0:T(8,128)S(1)}, u32[]{:S(2)}, u32[]{:S(2)}) collective-permute-start(f32[104,128]{1,0:T(8,128)} %get-tuple-element.17.own_ref), channel_id=1, source_target_pairs={{0,480},{32,0},{64,32},{96,64},{128,96},{160,128},{192,160},{224,1... | collective-permute-start | bytes 159752 | tf_op jit(solution)/shard_map/ppermute | solution.py:472
  10.9 11.6 %copy-start = (f32[104,128]{1,0:T(8,128)S(1)}, f32[104,128]{1,0:T(8,128)}, u32[]{:S(2)}) copy-start(f32[104,128]{1,0:T(8,128)} %get-tuple-element.17.own_ref) | copy-start | bytes 159748
  11.0 11.6 %copy-start.2 = (f32[32,128]{1,0:T(8,128)S(1)}, f32[32,128]{1,0:T(8,128)}, u32[]{:S(2)}) copy-start(f32[32,128]{1,0:T(8,128)} %get-tuple-element.18.rest_ref) | copy-start | bytes 49156
  11.0 23.1 %all-to-all-start = ((f32[32,5,2,128]{3,2,1,0:T(2,128)}), f32[32,5,2,128]{3,2,1,0:T(2,128)S(1)}, u32[]{:S(2)}, u32[]{:S(2)}) async-start(f32[32,5,2,128]{3,2,1,0:T(2,128)} %get-tuple-element.13), calls=%async_computation | async-start | bytes 327680 | tf_op jit(solution)/shard_map/all_to_all | solution.py:507
  22.6 6.8 %collective-permute-start.1 = (f32[176,128]{1,0:T(8,128)S(1)}, f32[176,128]{1,0:T(8,128)S(1)}, u32[]{:S(2)}, u32[]{:S(2)}) collective-permute-start(f32[176,128]{1,0:T(8,128)S(1)} %shard_map.124), channel_id=1, source_target_pairs={{0,3},{1,0},{2,1},{3,2},{4,7},{5,4},{6,5},{7,6},{8,11},{9,8},{10,9... | collective-permute-start | bytes 270344 | tf_op jit(solution)/shard_map/ppermute | solution.py:472
  29.4 10.8 %collective-permute-start.2 = (f32[320,128]{1,0:T(8,128)S(1)}, f32[320,128]{1,0:T(8,128)S(1)}, u32[]{:S(2)}, u32[]{:S(2)}) collective-permute-start(f32[320,128]{1,0:T(8,128)S(1)} %shard_map.125), channel_id=1, source_target_pairs={{0,28},{4,0},{8,4},{12,8},{16,12},{20,16},{24,20},{28,24},{1,29},{... | collective-permute-start | bytes 491528 | tf_op jit(solution)/shard_map/ppermute | solution.py:472
  35.4 4.8 %copy-start.1 = (f32[128,128]{1,0:T(8,128)S(1)}, f32[128,128]{1,0:T(8,128)}, u32[]{:S(2)}) copy-start(f32[128,128]{1,0:T(8,128)} %mix_ref.1) | copy-start | bytes 196612
  35.4 4.8 %copy-start.3 = (f32[8,128]{1,0:T(8,128)S(1)}, f32[8,128]{1,0:T(8,128)}, u32[]{:S(2)}) copy-start(f32[8,128]{1,0:T(8,128)} %radial_ref.1) | copy-start | bytes 12292
  35.4 4.8 %copy-start.4 = (f32[8,128]{1,0:T(8,128)S(1)}, f32[8,128]{1,0:T(8,128)}, u32[]{:S(2)}) copy-start(f32[8,128]{1,0:T(8,128)} %vector_ref.1) | copy-start | bytes 12292
  35.4 4.8 %copy-start.5 = (s32[2,2,2,8]{3,2,1,0:T(2,128)S(1)}, s32[2,2,2,8]{3,2,1,0:T(2,128)}, u32[]{:S(2)}) copy-start(s32[2,2,2,8]{3,2,1,0:T(2,128)} %species_ref.1) | copy-start | bytes 772
  35.4 4.8 %copy-start.6 = (f32[8,128]{1,0:T(8,128)S(1)}, f32[8,128]{1,0:T(8,128)}, u32[]{:S(2)}) copy-start(f32[8,128]{1,0:T(8,128)} %get-tuple-element.19.extra_ref) | copy-start | bytes 12292
  35.4 17.0 %all-to-all-start.1 = ((f32[16,8,128]{2,1,0:T(8,128)}), f32[16,8,128]{2,1,0:T(8,128)S(1)}, u32[]{:S(2)}, u32[]{:S(2)}) async-start(f32[16,8,128]{2,1,0:T(8,128)} %get-tuple-element.14), calls=%async_computation.1 | async-start | bytes 131072 | tf_op jit(solution)/shard_map/all_to_all | solution.py:520
  44.2 8.3 %collective-permute-start.3 = (f32[8,128]{1,0:T(8,128)S(1)}, f32[8,128]{1,0:T(8,128)S(1)}, u32[]{:S(2)}, u32[]{:S(2)}) collective-permute-start(f32[8,128]{1,0:T(8,128)S(1)} %get-tuple-element.21), channel_id=1, source_target_pairs={{0,32},{32,64},{64,96},{96,128},{128,160},{160,192},{192,224},{224... | collective-permute-start | bytes 12296 | tf_op jit(solution)/shard_map/ppermute | solution.py:472

commit v5 on v4

--- a/solution.py
+++ b/solution.py
@@ -134,26 +134,13 @@
     turned = jnp.concatenate(
         [jnp.zeros((32, 128), F32), tile, jnp.zeros((88, 128), F32)], 0
     ).T
-    near = near_ref[...]
-    atom = iota((64, 32), 0)
-    stencil = near >> 3
-    slot = near & 7
-    step_x = (stencil * 57) >> 9
-    line = (stencil * 171) >> 9
-    step_z = stencil - 3 * line
-    step_y = line - 3 * step_x
-    spot_x = step_x + 1 - ((atom >> 5) & 1)
-    spot_y = step_y + 1 - ((atom >> 4) & 1)
-    spot_z = step_z + 1 - ((atom >> 3) & 1)
-    block = (spot_z >> 1) * 4 + (spot_y >> 1) * 2 + (spot_x >> 1)
-    cell = (spot_x & 1) * 4 + (spot_y & 1) * 2 + (spot_z & 1)
-    target = (block * 64 + cell * 8 + slot).astype(F32)
+    near = near_ref[...].astype(F32)
     slab_ref[0:64] = masked
     slab_ref[64:72] = tile
     slab_ref[72:104] = turned[0:32]
-    slab_ref[72:104, 0:32] = target[0:32]
+    slab_ref[72:104, 0:32] = near[0:32]
     rest_ref[...] = turned[32:64]
-    rest_ref[:, 0:32] = target[32:64]
+    rest_ref[:, 0:32] = near[32:64]
 
 
 def stack_z_kernel(own_ref, rest_ref, in_x_ref, out_ref):
@@ -285,74 +272,92 @@
     pull_x = (number_x * (two_pi / grid[0])) * jnp.sum(turning, 0, keepdims=True)
     pull_y = jnp.sum(turning * (number_y * (two_pi / grid[1])), 0, keepdims=True)
     pull_z = jnp.sum(turning * (number_z * (two_pi / grid[2])), 0, keepdims=True)
-    rows = jnp.concatenate([energy, pull_x, pull_y, pull_z], 0)
-    for target in range(32):
-        out_ref[target] = rows[:, target // 2 * 128 : target // 2 * 128 + 128]
-    half = iota((4, 128), 1) // 64
+    first = jnp.concatenate([energy, pull_y], 0)
+    second = jnp.concatenate([pull_x, pull_z], 0)
+    low = iota((2, 128), 1) < 64
+    for pair in range(16):
+        lanes = slice(128 * pair, 128 * pair + 128)
+        left_part, right_part = first[:, lanes], second[:, lanes]
+        out_ref[2 * pair] = jnp.where(low, left_part, swap_halves(right_part))
+        out_ref[2 * pair + 1] = jnp.where(low, swap_halves(left_part), right_part)
     for block in range(4):
         by, bz = block % 2, block // 2
-        to_z = (at_z + bz) % 4
-        to = ((at_y + by) % 8) * 4 + to_z
-        rows_at = slice(4 * bz, 4 * bz + 4)
-        piece = jnp.where(to_z % 2 == by, folded[rows_at], turned[rows_at])
-        out_ref[to] = out_ref[to] + jnp.where(half == to_z % 2, piece, 0.0)
+        to = ((at_y + by) % 8) * 4 + (at_z + bz) % 4
+        here, there = (folded, turned) if by == 0 else (turned, folded)
+        row = 4 * bz
+        piece = jnp.where(
+            low,
+            jnp.concatenate([here[row : row + 1], here[row + 2 : row + 3]], 0),
+            jnp.concatenate([there[row + 1 : row + 2], there[row + 3 : row + 4]], 0),
+        )
+        out_ref[to] = out_ref[to] + piece
 
 
 def short_kernel(
-    own_ref, rest_ref, in_x_ref, in_y_ref, in_z_ref, extra_ref,
+    own_ref, rest_ref, in_x_ref, in_z_ref, in_y_ref, extra_ref,
     radial_ref, vector_ref, mix_ref, species_ref, kept_ref, sent_ref,
 ):
     bases = [
         (own_ref, 0), (in_x_ref, 0), (in_y_ref, 0), (in_y_ref, 72),
         (in_z_ref, 0), (in_z_ref, 72), (in_y_ref, 144), (in_y_ref, 216),
     ]
-    feats = jnp.concatenate([ref[at : at + 64] for ref, at in bases], 0)
-    low_lane = iota((8, 128), 1) < 64
-    spots = []
-    for pair in range(4):
-        (ref_a, at_a), (ref_b, at_b) = bases[2 * pair], bases[2 * pair + 1]
-        spots.append(
-            jnp.where(
-                low_lane,
-                ref_a[at_a + 64 : at_a + 72],
-                swap_halves(ref_b[at_b + 64 : at_b + 72]),
-            )
-        )
-    spots = jnp.concatenate(spots, 1)
-    tiles = [
+
+    def local_row(x, y, z):
+        return (x % 2 * 4 + y % 2 * 2 + z % 2) * 8
+
+    def block_of(x, y, z):
+        return z // 2 * 4 + y // 2 * 2 + x // 2
+
+    def cell_tile(x, y, z):
+        ref, at = bases[block_of(x, y, z)]
+        at = at + local_row(x, y, z)
+        return ref[at : at + 8]
+
+    units = [(x, y, z) for z in (1, 2) for y in (1, 2) for x in (1, 2)]
+    steps = [(dx, dy, dz) for dx in range(3) for dy in range(3) for dz in range(3)]
+    centres = [
         rest_ref[24:32], in_x_ref[96:104], in_y_ref[288:296], in_y_ref[296:304],
         in_z_ref[152:160], in_z_ref[168:176], in_y_ref[304:312], in_y_ref[312:320],
     ]
-    centres = jnp.concatenate(tiles, 0)
-    own = []
-    for unit in range(8):
-        ux, uy, uz = unit % 2, unit // 2 % 2, unit // 4
-        ref, at = bases[unit]
-        at = at + ((1 - ux) * 4 + (1 - uy) * 2 + (1 - uz)) * 8
-        own.append(ref[at : at + 8])
-    own = jnp.concatenate(own, 0)
+    centres = jnp.concatenate(centres, 0)
+    own = jnp.concatenate([cell_tile(*unit) for unit in units], 0)
     occupied = centres[:, 35:36]
-    lane = iota((1, 512), 1)
-    block = lane // 64
-    cell = lane // 8 % 8
-    spot = (
-        spots[0:1] + ((block % 2) * 2 + cell // 4).astype(F32),
-        spots[1:2] + ((block // 2 % 2) * 2 + cell // 2 % 2).astype(F32),
-        spots[2:3] + ((block // 4) * 2 + cell % 2).astype(F32),
-    )
-    atom = iota((64, 1), 0)
-    unit = atom // 8
-    middle = (
-        centres[:, 32:33] + (unit % 2 + 1).astype(F32),
-        centres[:, 33:34] + (unit // 2 % 2 + 1).astype(F32),
-        centres[:, 34:35] + (unit // 4 + 1).astype(F32),
-    )
-    delta = [spot[a] - middle[a] for a in range(3)]
+    group = iota((8, 128), 1) // 8
+    group_long = iota((64, 128), 1) // 8
+    rows = [ref[at + 64 : at + 72] for ref, at in bases]
+    columns = jnp.concatenate(rows + [jnp.zeros((64, 128), F32)], 0).T[0:64]
+    copies = []
+    for block in range(8):
+        wide = jnp.where(group_long == block, columns, 0.0)
+        for shift in (8, 16, 32, 64):
+            wide = wide + pltpu.roll(wide, shift, 1)
+        copies.append(wide)
+    tiles = []
+    for dx, dy, dz in steps:
+        tile = jnp.zeros((8, 128), F32)
+        for unit, (x, y, z) in enumerate(units):
+            tx, ty, tz = x - 1 + dx, y - 1 + dy, z - 1 + dz
+            row = local_row(tx, ty, tz)
+            tile = jnp.where(group == unit, copies[block_of(tx, ty, tz)][row : row + 8], tile)
+        tiles.append(tile)
+    spots = jnp.concatenate(tiles + [jnp.zeros((40, 128), F32)], 0).T
+    stencil = iota((1, 256), 1) // 8
+    crossing = (stencil // 9 - 1, stencil // 3 % 3 - 1, stencil % 3 - 1)
+    delta = []
+    for a in range(3):
+        spread = jnp.concatenate(
+            [
+                jnp.broadcast_to(spots[8 * unit + a : 8 * unit + a + 1], (8, 256))
+                for unit in range(8)
+            ],
+            0,
+        )
+        delta.append(crossing[a].astype(F32) + spread - centres[:, 32 + a : 33 + a])
     dist_sq = delta[0] * delta[0] + delta[1] * delta[1] + delta[2] * delta[2]
     near = 1.0 - dist_sq * (1.0 / 16.0)
     envelope = near * near
-    lane_f = iota((64, 512), 1).astype(F32)
-    times = jnp.zeros((64, 512), F32)
+    lane_f = iota((64, 256), 1).astype(F32)
+    times = jnp.zeros((64, 256), F32)
     for entry in range(32):
         times = times + jnp.where(centres[:, entry : entry + 1] == lane_f, 1.0, 0.0)
     bases_m = []
@@ -363,21 +368,37 @@
         else:
             power = power * power
         bases_m.append(power * times)
-    feat_high, feat_low = split(feats)
-    feat_both = jnp.concatenate([feat_high, feat_low], 1)
     norm = 1.0 / math.sqrt(32.0)
-    sums = [jnp.zeros((64, 128), F32) for _ in range(4)]
-    for b in range(8):
-        weight = bases_m[b] * envelope
-        left = jnp.concatenate([weight] + [weight * delta[a] for a in range(3)], 0)
-        left_high, left_low = split(left)
-        first = contract(left_high, feat_both, (((1,), (0,))))
-        second = contract(left_low, feat_high, (((1,), (0,))))
-        made = first[:, 0:128] + first[:, 128:256] + second
-        sums[0] = sums[0] + made[0:64] * radial_ref[b : b + 1]
-        for a in range(3):
-            sums[1 + a] = sums[1 + a] + made[64 * (1 + a) : 64 * (2 + a)] * vector_ref[b : b + 1]
-    sums = [value * norm for value in sums]
+    windows = []
+    sums = [[], [], [], []]
+    for unit, (x, y, z) in enumerate(units):
+        window = jnp.concatenate(
+            [cell_tile(x - 1 + dx, y - 1 + dy, z - 1 + dz) for dx, dy, dz in steps]
+            + [jnp.zeros((40, 128), F32)],
+            0,
+        )
+        high, low = split(window)
+        windows.append((high, low))
+        at = slice(8 * unit, 8 * unit + 8)
+        left = []
+        for b in range(8):
+            weight = bases_m[b][at] * envelope[at]
+            left += [weight] + [weight * delta[a][at] for a in range(3)]
+        left_high, left_low = split(jnp.concatenate(left, 0))
+        made = contract(
+            jnp.concatenate([left_high, left_low], 0),
+            jnp.concatenate([high, low], 1),
+            (((1,), (0,))),
+        )
+        made = made[0:256, 0:128] + made[0:256, 128:256] + made[256:512, 0:128]
+        for part in range(4):
+            weights = radial_ref if part == 0 else vector_ref
+            total = made[8 * part : 8 * part + 8] * weights[0:1]
+            for b in range(1, 8):
+                row = 8 * (4 * b + part)
+                total = total + made[row : row + 8] * weights[b : b + 1]
+            sums[part].append(total)
+    sums = [jnp.concatenate(part, 0) * norm for part in sums]
     product = sums[0] + sums[1] * sums[1] + sums[2] * sums[2] + sums[3] * sums[3]
     mixed = contract(split_left(product), split_right(mix_ref[...], 0), (((1,), (0,))))
     gate = 1.0 / (1.0 + jnp.exp(-mixed))
@@ -386,40 +407,62 @@
     slope = gate * (1.0 + mixed * (1.0 - gate)) * (out_weight * occupied)
     grad = contract(split_left(slope), split_right(mix_ref[...], 1), (((1,), (1,)))) * norm
     grads = [grad] + [2.0 * grad * sums[1 + a] for a in range(3)]
-    right = jnp.concatenate([feat_high, feat_high, feat_low], 1)
-    linear = [jnp.zeros((64, 512), F32) for _ in range(3)]
-    plain = jnp.zeros((64, 512), F32)
-    decayed = jnp.zeros((64, 512), F32)
-    for b in range(8):
-        left = jnp.concatenate(
-            [grads[0] * radial_ref[b : b + 1]]
-            + [grads[1 + a] * vector_ref[b : b + 1] for a in range(3)],
-            0,
-        )
-        left_high, left_low = split(left)
+    sub = iota((8, 256), 0)
+    column = iota((8, 128), 1)
+    pushes, ends = [], {}
+    for unit, spot in enumerate(units):
+        at = slice(8 * unit, 8 * unit + 8)
+        left = []
+        for b in range(8):
+            left.append(grads[0][at] * radial_ref[b : b + 1])
+            left += [grads[1 + a][at] * vector_ref[b : b + 1] for a in range(3)]
+        high, low = windows[unit]
         pulled = contract(
-            jnp.concatenate([left_high, left_low, left_high], 1), right, (((1,), (1,)))
-        )
-        parts = [pulled[64 * (1 + a) : 64 * (2 + a)] for a in range(3)]
-        full = pulled[0:64] + parts[0] * delta[0] + parts[1] * delta[1] + parts[2] * delta[2]
-        weighted = bases_m[b] * full
-        plain = plain + weighted
-        decayed = decayed + weighted * (2.0 ** (b - 4))
+            split_left(jnp.concatenate(left, 0)),
+            jnp.concatenate([high, high, low], 1),
+            (((1,), (1,))),
+        )
+        linear = [jnp.zeros((8, 256), F32) for _ in range(3)]
+        plain = jnp.zeros((8, 256), F32)
+        decayed = jnp.zeros((8, 256), F32)
+        here = [delta[a][at] for a in range(3)]
+        for b in range(8):
+            parts = [pulled[32 * b + 8 * part : 32 * b + 8 * part + 8] for part in range(4)]
+            full = parts[0] + parts[1] * here[0] + parts[2] * here[1] + parts[3] * here[2]
+            basis = bases_m[b][at]
+            weighted = basis * full
+            plain = plain + weighted
+            decayed = decayed + weighted * (2.0 ** (b - 4))
+            for a in range(3):
+                linear[a] = linear[a] + basis * parts[1 + a]
+        radial_slope = 2.0 * (near[at] * (-0.125) * plain - envelope[at] * decayed)
+        gathered = jnp.zeros((8, 256), F32)
+        end = jnp.where(column == 0, energy[at], 0.0)
         for a in range(3):
-            linear[a] = linear[a] + bases_m[b] * parts[a]
-    radial_slope = 2.0 * (near * (-0.125) * plain - envelope * decayed)
-    lane_i = iota((64, 512), 1)
-    row_i = iota((64, 512), 0)
-    ux, uy, uz = row_i // 8 % 2, row_i // 16 % 2, row_i // 32
-    self_at = (row_i // 8) * 64 + ((1 - ux) * 4 + (1 - uy) * 2 + (1 - uz)) * 8 + row_i % 8
-    own_slot = lane_i == self_at
-    rows = [jnp.sum(jnp.where(own_slot, energy, 0.0), 0, keepdims=True)]
-    for a in range(3):
-        push = envelope * linear[a] + delta[a] * radial_slope
-        back = jnp.sum(push, 1, keepdims=True)
-        rows.append(jnp.sum(push - jnp.where(own_slot, back, 0.0), 0, keepdims=True))
-    rows = jnp.concatenate(rows, 0)
-    low = iota((4, 128), 1) < 64
+            push = envelope[at] * linear[a] + here[a] * radial_slope
+            gathered = jnp.where(sub == 1 + a, jnp.sum(push, 0, keepdims=True), gathered)
+            end = jnp.where(column == 1 + a, -jnp.sum(push, 1, keepdims=True), end)
+        pushes.append(gathered)
+        ends[spot] = end
+    pushes = jnp.concatenate(pushes + [jnp.zeros((64, 256), F32)], 0).T
+    folded = []
+    for block in range(8):
+        for local in range(8):
+            x = block % 2 * 2 + local // 4
+            y = block // 2 % 2 * 2 + local // 2 % 2
+            z = block // 4 * 2 + local % 2
+            total = ends.get((x, y, z), jnp.zeros((8, 128), F32))
+            for unit, (ux, uy, uz) in enumerate(units):
+                step = (x - ux + 1, y - uy + 1, z - uz + 1)
+                if step in steps:
+                    row = 8 * steps.index(step)
+                    total = total + jnp.where(group == unit, pushes[row : row + 8], 0.0)
+            folded.append(total)
+    folded = jnp.concatenate(folded, 0).T
+    rows = folded[0:8]
+    for unit in range(1, 8):
+        rows = rows + folded[8 * unit : 8 * unit + 8]
+    rows = rows[0:4]
     kinds = [species_ref[x, y] for x in range(2) for y in range(2)]
     spread = (iota((8, 128), 1) % 8 == iota((8, 128), 0)).astype(F32)
     kinds = contract(jnp.concatenate(kinds, 0).astype(F32), spread, (((1,), (0,))))
@@ -429,6 +472,7 @@
     mine = iota((8, 128), 1) // 8 == iota((8, 128), 0)
     shift = jnp.sum(jnp.where(mine, shift, 0.0), 0, keepdims=True) * own_ref[67:68]
     shift = jnp.where(iota((4, 128), 0) == 0, shift, 0.0)
+    low = iota((4, 128), 1) < 64
     for half in range(2):
         first, second = (rows[:, 128 * k : 128 * k + 128] for k in (2 * half, 2 * half + 1))
         first = first + shift if half == 0 else first
@@ -437,11 +481,13 @@
 
 
 def last_kernel(parts_ref, energy_ref, force_ref):
-    total = parts_ref[0]
-    for member in range(1, parts_ref.shape[0]):
-        total = total + parts_ref[member]
-    odd = lax.axis_index("gz") % 2
-    total = jnp.where(odd == 1, swap_halves(total), total)
+    total = parts_ref[0:8]
+    for at in range(8, 64, 8):
+        total = total + parts_ref[at : at + 8]
+    total = total + pltpu.roll(total, 4, 0)
+    total = total + pltpu.roll(total, 2, 0)
+    turned = swap_halves(total)
+    total = jnp.concatenate([total[0:1], turned[0:1], total[1:2], turned[1:2]], 0)
     for cell in range(8):
         x, y, z = cell // 4, cell // 2 % 2, cell % 2
         here = total if cell == 0 else pltpu.roll(total, 128 - 8 * cell, 1)
@@ -521,17 +567,17 @@
     kept, sent = call(
         short_kernel,
         [(8, 128), (8, 128)],
-        slab, rest, in_x, in_y, in_z, extra,
+        slab, rest, in_x, in_z, in_y, extra,
         w_radial, w_vector, w_mix, species,
         micros=SHORT_MICROS,
     )
     came = moved(sent, ("gx",), 1)
     (parts,) = call(
         functools.partial(field_kernel, grid, scale),
-        [(32, 4, 128)],
+        [(32, 2, 128)],
         sums, phases, charges, kept, came,
     )
-    parts = lax.all_to_all(parts, ("gy", "gz"), 0, 0)
+    parts = lax.all_to_all(parts, ("gy", "gz"), 0, 0).reshape(64, 128)
     atom_energy, forces = call(last_kernel, [(2, 2, 2, 8), (2, 2, 3, 2, 8)], parts, room=LAST_ROOM)
     return (atom_energy, jnp.transpose(forces, (0, 1, 3, 2, 4)))
 

time: 67.4 us -> 66 us (0.979)
  Pallas kernels: 8.48 us -> 7.32 us
    pallas_call x6, Pallas kernels: 6.57 us -> 5.41 us  [call(): pl.pallas_call(kernel, out_shape=[jax.ShapeDtypeStruct(shape, F32) for sh...]
  transfers between devices with their start and end apart: 6 -> 6, of which waited for: 2 -> 2; matrix products, arithmetic and copies ran while one was open for 0% -> 0% of each run, Pallas kernels for 8% -> 6%
where the time goes in v5:
time: 66 us; the launch traced here: 65.5 us
  starting transfers between devices  34.7 us (53%)
  blocking collectives  12.9 us (20%)
  waiting for transfers between devices  9.67 us (15%)
  Pallas kernels  7.32 us (11%)
  between operations  0.81 us (1%)
    ppermute x4, starting transfers between devices, moved(): return lax.ppermute(value, axes, pairs)  18.4 us
    all_to_all x1, blocking collectives, body(): parts = lax.all_to_all(parts, ('gy', 'gz'), 0, 0).reshape(64, 128)  12.9 us
    all_to_all x1, starting transfers between devices, body(): atoms = lax.all_to_all(message, ('gy', 'gz'), 0, 0).reshape(320, 128)  11.6 us
    ppermute x4, waiting for transfers between devices, moved(): return lax.ppermute(value, axes, pairs)  9.66 us
    pallas_call x6, Pallas kernels, call(): pl.pallas_call(kernel, out_shape=[jax.ShapeDtypeStruct(shape, F32) for sh...  5.41 us
    all_to_all x1, starting transfers between devices, body(): sums = lax.all_to_all(partial, 'gx', 0, 0)  4.77 us
    pallas_call x1, Pallas kernels, body(): pl.pallas_call(pack_kernel, out_shape=[jax.ShapeDtypeStruct(shape, F32) f...  1.91 us
  transfers between devices with their start and end apart: 6, of which 2 were waited for; matrix products, arithmetic and copies ran while one was open for 0% of the time, Pallas kernels for 6%

profile of v5, /device:TPU:1, one launch (start us, length us, event | category | flops | bytes accessed | tf_op | source)
XLA Modules:
  0.0 65.5 jit_solution(4648755284423019417)
XLA Ops:
  0.6 1.9 %shard_map.122 = (f32[104,128]{1,0:T(8,128)}, f32[32,128]{1,0:T(8,128)}, f32[8,128]{1,0:T(8,128)}, f32[32,5,2,128]{3,2,1,0:T(2,128)}) custom-call(f32[64,128]{1,0:T(8,128)} %bitcast.11, f32[2,2,3,2,8]{4,3,2,1,0:T(2,128)} %bitcast.13, s32[2,2,2]{2,1,0:T(2,128)} %count_hbm.1, s32[64,32]{1,0:T(8,128)} %bitcast.12, f32[16,128]{1,0:T(8,128)} %bitcast.14, ...), custom_call_target="tpu_custom_call" | custom-call | tf_op jit(solution)/shard_map/pallas_call | solution.py:541
  2.5 8.4 %collective-permute-start = (f32[104,128]{1,0:T(8,128)}, f32[104,128]{1,0:T(8,128)S(1)}, u32[]{:S(2)}, u32[]{:S(2)}) collective-permute-start(f32[104,128]{1,0:T(8,128)} %get-tuple-element.17.own_ref), channel_id=1, source_target_pairs={{0,480},{32,0},{64,32},{96,64},{128,96},{160,128},{192,160},{224,1... | collective-permute-start | bytes 159752 | tf_op jit(solution)/shard_map/ppermute | solution.py:518
  10.9 0.0 copy-start
  11.0 0.0 copy-start.2
  11.0 11.6 %all-to-all-start = ((f32[32,5,2,128]{3,2,1,0:T(2,128)}), f32[32,5,2,128]{3,2,1,0:T(2,128)S(1)}, u32[]{:S(2)}, u32[]{:S(2)}) async-start(f32[32,5,2,128]{3,2,1,0:T(2,128)} %get-tuple-element.13), calls=%async_computation | async-start | bytes 327680 | tf_op jit(solution)/shard_map/all_to_all | solution.py:553
  22.6 0.0 collective-permute-done.in_x_ref
  22.6 0.0 copy-done
  22.6 0.0 copy-done.2
  22.6 2.1 %collective-permute-start.1 = (f32[176,128]{1,0:T(8,128)S(1)}, f32[176,128]{1,0:T(8,128)S(1)}, u32[]{:S(2)}, u32[]{:S(2)}) collective-permute-start(f32[176,128]{1,0:T(8,128)S(1)} %shard_map.124), channel_id=1, source_target_pairs={{0,3},{1,0},{2,1},{3,2},{4,7},{5,4},{6,5},{7,6},{8,11},{9,8},{10,9... | collective-permute-start | bytes 270344 | tf_op jit(solution)/shard_map/ppermute | solution.py:518
  24.8 4.6 %collective-permute-done.1.in_z_ref = f32[176,128]{1,0:T(8,128)S(1)} collective-permute-done((f32[176,128]{1,0:T(8,128)S(1)}, f32[176,128]{1,0:T(8,128)S(1)}, u32[]{:S(2)}, u32[]{:S(2)}) %collective-permute-start.1) | collective-permute-done | bytes 90144 | tf_op jit(solution)/shard_map/ppermute | solution.py:518
  29.4 4.6 %collective-permute-start.2 = (f32[320,128]{1,0:T(8,128)S(1)}, f32[320,128]{1,0:T(8,128)S(1)}, u32[]{:S(2)}, u32[]{:S(2)}) collective-permute-start(f32[320,128]{1,0:T(8,128)S(1)} %shard_map.125), channel_id=1, source_target_pairs={{0,28},{4,0},{8,4},{12,8},{16,12},{20,16},{24,20},{28,24},{1,29},{... | collective-permute-start | bytes 491528 | tf_op jit(solution)/shard_map/ppermute | solution.py:518
  34.0 0.0 all-to-all-done
  34.0 1.4 %shard_map.123 = (f32[16,8,128]{2,1,0:T(8,128)}, f32[64,2048]{1,0:T(8,128)S(1)}, f32[16,2048]{1,0:T(8,128)S(1)}) custom-call(f32[320,128]{1,0:T(8,128)S(1)} %bitcast.9), custom_call_target="tpu_custom_call" | custom-call | flops 49999998976 | bytes 150000000 | tf_op jit(solution)/shard_map/pallas_call | solution.py:501
  35.4 0.0 copy-start.1
  35.4 0.0 copy-start.3
  35.4 0.0 copy-start.4
  35.4 0.0 copy-start.5
  35.4 0.0 copy-start.6
  35.4 4.8 %all-to-all-start.1 = ((f32[16,8,128]{2,1,0:T(8,128)}), f32[16,8,128]{2,1,0:T(8,128)S(1)}, u32[]{:S(2)}, u32[]{:S(2)}) async-start(f32[16,8,128]{2,1,0:T(8,128)} %get-tuple-element.14), calls=%async_computation.1 | async-start | bytes 131072 | tf_op jit(solution)/shard_map/all_to_all | solution.py:566
  40.2 0.0 collective-permute-done.2.in_y_ref
  40.2 0.0 copy-done.1
  40.2 0.0 copy-done.3
  40.3 0.0 copy-done.4
  40.3 0.0 copy-done.5
  40.3 0.0 copy-done.6
  40.3 2.7 %shard_map.126 = (f32[8,128]{1,0:T(8,128)S(1)}, f32[8,128]{1,0:T(8,128)S(1)}) custom-call(f32[104,128]{1,0:T(8,128)S(1)} %copy-done, f32[32,128]{1,0:T(8,128)S(1)} %copy-done.2, f32[104,128]{1,0:T(8,128)S(1)} %collective-permute-done.in_x_ref, f32[176,128]{1,0:T(8,128)S(1)} %collective-permute-done.1.in_z_ref, ...), custom_call_target="tpu_custom_call" | custom-call | flops 100000000 | bytes 300000 | tf_op jit(solution)/shard_map/pallas_call | solution.py:501
  43.0 3.3 %collective-permute-start.3 = (f32[8,128]{1,0:T(8,128)S(1)}, f32[8,128]{1,0:T(8,128)S(1)}, u32[]{:S(2)}, u32[]{:S(2)}) collective-permute-start(f32[8,128]{1,0:T(8,128)S(1)} %get-tuple-element.21), channel_id=1, source_target_pairs={{0,32},{32,64},{64,96},{96,128},{128,160},{160,192},{192,224},{224... | collective-permute-start | bytes 12296 | tf_op jit(solution)/shard_map/ppermute | solution.py:518
  46.2 5.0 %collective-permute-done.3.came_ref = f32[8,128]{1,0:T(8,128)S(1)} collective-permute-done((f32[8,128]{1,0:T(8,128)S(1)}, f32[8,128]{1,0:T(8,128)S(1)}, u32[]{:S(2)}, u32[]{:S(2)}) %collective-permute-start.3) | collective-permute-done | bytes 4128 | tf_op jit(solution)/shard_map/ppermute | solution.py:518
  51.2 0.0 all-to-all-done.1.sums_ref
  51.2 0.6 shard_map.127
  51.8 12.9 %all_to_all.15 = f32[32,2,128]{2,1,0:T(2,128)S(1)} all-to-all(f32[32,2,128]{2,1,0:T(2,128)S(1)} %shard_map.127), channel_id=1, replica_groups=mesh['gx'=16,'gy'=8,'gz'=4] {'gy','gz'}, dimensions={0} | all-to-all | bytes 65536 | tf_op jit(solution)/shard_map/all_to_all | solution.py:580
  64.7 0.8 %shard_map.128 = (f32[2,2,2,8]{3,2,1,0:T(2,128)}, f32[2,2,3,2,8]{4,3,2,1,0:T(2,128)}) custom-call(f32[64,128]{1,0:T(8,128)S(1)} %bitcast.10), custom_call_target="tpu_custom_call" | custom-call | flops 1000000000 | bytes 3000000 | tf_op jit(solution)/shard_map/pallas_call | solution.py:501
  (2 shorter events, 0.0 us)
Async XLA Ops:
  2.5 20.0 %collective-permute-start = (f32[104,128]{1,0:T(8,128)}, f32[104,128]{1,0:T(8,128)S(1)}, u32[]{:S(2)}, u32[]{:S(2)}) collective-permute-start(f32[104,128]{1,0:T(8,128)} %get-tuple-element.17.own_ref), channel_id=1, source_target_pairs={{0,480},{32,0},{64,32},{96,64},{128,96},{160,128},{192,160},{224,1... | collective-permute-start | bytes 159752 | tf_op jit(solution)/shard_map/ppermute | solution.py:518
  10.9 11.6 %copy-start = (f32[104,128]{1,0:T(8,128)S(1)}, f32[104,128]{1,0:T(8,128)}, u32[]{:S(2)}) copy-start(f32[104,128]{1,0:T(8,128)} %get-tuple-element.17.own_ref) | copy-start | bytes 159748
  11.0 11.6 %copy-start.2 = (f32[32,128]{1,0:T(8,128)S(1)}, f32[32,128]{1,0:T(8,128)}, u32[]{:S(2)}) copy-start(f32[32,128]{1,0:T(8,128)} %get-tuple-element.18.rest_ref) | copy-start | bytes 49156
  11.0 23.1 %all-to-all-start = ((f32[32,5,2,128]{3,2,1,0:T(2,128)}), f32[32,5,2,128]{3,2,1,0:T(2,128)S(1)}, u32[]{:S(2)}, u32[]{:S(2)}) async-start(f32[32,5,2,128]{3,2,1,0:T(2,128)} %get-tuple-element.13), calls=%async_computation | async-start | bytes 327680 | tf_op jit(solution)/shard_map/all_to_all | solution.py:553
  22.6 6.8 %collective-permute-start.1 = (f32[176,128]{1,0:T(8,128)S(1)}, f32[176,128]{1,0:T(8,128)S(1)}, u32[]{:S(2)}, u32[]{:S(2)}) collective-permute-start(f32[176,128]{1,0:T(8,128)S(1)} %shard_map.124), channel_id=1, source_target_pairs={{0,3},{1,0},{2,1},{3,2},{4,7},{5,4},{6,5},{7,6},{8,11},{9,8},{10,9... | collective-permute-start | bytes 270344 | tf_op jit(solution)/shard_map/ppermute | solution.py:518
  29.4 10.8 %collective-permute-start.2 = (f32[320,128]{1,0:T(8,128)S(1)}, f32[320,128]{1,0:T(8,128)S(1)}, u32[]{:S(2)}, u32[]{:S(2)}) collective-permute-start(f32[320,128]{1,0:T(8,128)S(1)} %shard_map.125), channel_id=1, source_target_pairs={{0,28},{4,0},{8,4},{12,8},{16,12},{20,16},{24,20},{28,24},{1,29},{... | collective-permute-start | bytes 491528 | tf_op jit(solution)/shard_map/ppermute | solution.py:518
  35.4 4.8 %copy-start.1 = (f32[128,128]{1,0:T(8,128)S(1)}, f32[128,128]{1,0:T(8,128)}, u32[]{:S(2)}) copy-start(f32[128,128]{1,0:T(8,128)} %mix_ref.1) | copy-start | bytes 196612
  35.4 4.8 %copy-start.3 = (f32[8,128]{1,0:T(8,128)S(1)}, f32[8,128]{1,0:T(8,128)}, u32[]{:S(2)}) copy-start(f32[8,128]{1,0:T(8,128)} %radial_ref.1) | copy-start | bytes 12292
  35.4 4.8 %copy-start.4 = (f32[8,128]{1,0:T(8,128)S(1)}, f32[8,128]{1,0:T(8,128)}, u32[]{:S(2)}) copy-start(f32[8,128]{1,0:T(8,128)} %vector_ref.1) | copy-start | bytes 12292
  35.4 4.8 %copy-start.5 = (s32[2,2,2,8]{3,2,1,0:T(2,128)S(1)}, s32[2,2,2,8]{3,2,1,0:T(2,128)}, u32[]{:S(2)}) copy-start(s32[2,2,2,8]{3,2,1,0:T(2,128)} %species_ref.1) | copy-start | bytes 772
  35.4 4.8 %copy-start.6 = (f32[8,128]{1,0:T(8,128)S(1)}, f32[8,128]{1,0:T(8,128)}, u32[]{:S(2)}) copy-start(f32[8,128]{1,0:T(8,128)} %get-tuple-element.19.extra_ref) | copy-start | bytes 12292
  35.4 15.8 %all-to-all-start.1 = ((f32[16,8,128]{2,1,0:T(8,128)}), f32[16,8,128]{2,1,0:T(8,128)S(1)}, u32[]{:S(2)}, u32[]{:S(2)}) async-start(f32[16,8,128]{2,1,0:T(8,128)} %get-tuple-element.14), calls=%async_computation.1 | async-start | bytes 131072 | tf_op jit(solution)/shard_map/all_to_all | solution.py:566
  43.0 8.3 %collective-permute-start.3 = (f32[8,128]{1,0:T(8,128)S(1)}, f32[8,128]{1,0:T(8,128)S(1)}, u32[]{:S(2)}, u32[]{:S(2)}) collective-permute-start(f32[8,128]{1,0:T(8,128)S(1)} %get-tuple-element.21), channel_id=1, source_target_pairs={{0,32},{32,64},{64,96},{96,128},{128,160},{160,192},{192,224},{224... | collective-permute-start | bytes 12296 | tf_op jit(solution)/shard_map/ppermute | solution.py:518

commit v6 on v5

--- a/solution.py
+++ b/solution.py
@@ -18,6 +18,7 @@
 STACK_Z_MICROS = 50
 STACK_Y_MICROS = 1
 WAVES_MICROS = 500
+FIELD_MICROS = 50
 SHORT_MICROS = 1
 PACK_ROOM = 60
 LAST_ROOM = 48
@@ -230,7 +231,7 @@
         message_ref[other] = partial
 
 
-def field_kernel(grid, scale, sums_ref, phase_ref, charge_ref, kept_ref, came_ref, out_ref):
+def field_kernel(grid, scale, sums_ref, phase_ref, charge_ref, out_ref):
     at_y, at_z = lax.axis_index("gy"), lax.axis_index("gz")
     member = at_y * 4 + at_z
     total = sums_ref[0]
@@ -245,8 +246,6 @@
         ],
         0,
     )
-    folded = kept_ref[...] + came_ref[...]
-    turned = swap_halves(folded)
     two_pi = 2.0 * math.pi
     number_x, number_y, number_z = wave_numbers(member, (16, 128), 1)
     wave_x, wave_y, wave_z = (
@@ -280,6 +279,14 @@
         left_part, right_part = first[:, lanes], second[:, lanes]
         out_ref[2 * pair] = jnp.where(low, left_part, swap_halves(right_part))
         out_ref[2 * pair + 1] = jnp.where(low, swap_halves(left_part), right_part)
+
+
+def fold_kernel(parts_ref, kept_ref, came_ref, out_ref):
+    at_y, at_z = lax.axis_index("gy"), lax.axis_index("gz")
+    folded = kept_ref[...] + came_ref[...]
+    turned = swap_halves(folded)
+    low = iota((2, 128), 1) < 64
+    out_ref[...] = parts_ref[...]
     for block in range(4):
         by, bz = block % 2, block // 2
         to = ((at_y + by) % 8) * 4 + (at_z + bz) % 4
@@ -575,8 +582,10 @@
     (parts,) = call(
         functools.partial(field_kernel, grid, scale),
         [(32, 2, 128)],
-        sums, phases, charges, kept, came,
-    )
+        sums, phases, charges,
+        micros=FIELD_MICROS,
+    )
+    (parts,) = call(fold_kernel, [(32, 2, 128)], parts, kept, came)
     parts = lax.all_to_all(parts, ("gy", "gz"), 0, 0).reshape(64, 128)
     atom_energy, forces = call(last_kernel, [(2, 2, 2, 8), (2, 2, 3, 2, 8)], parts, room=LAST_ROOM)
     return (atom_energy, jnp.transpose(forces, (0, 1, 3, 2, 4)))

time: 66 us -> 65.5 us (level)
    ppermute x4, waiting for transfers between devices: 9.66 us -> 5.9 us  [moved(): return lax.ppermute(value, axes, pairs)]
    all_to_all x1, waiting for transfers between devices: 0.01 us -> 3.21 us  [body(): sums = lax.all_to_all(partial, 'gx', 0, 0)]
    pallas_call x6 -> x7, Pallas kernels: 5.41 us -> 5.47 us  [call(): pl.pallas_call(kernel, out_shape=[jax.ShapeDtypeStruct(shape, F32) for sh...]
  transfers between devices with their start and end apart: 6 -> 6, of which waited for: 2 -> 3; matrix products, arithmetic and copies ran while one was open for 0% -> 0% of each run, Pallas kernels for 6% -> 7%
where the time goes in v6:
time: 65.5 us; the launch traced here: 65 us
  starting transfers between devices  34.7 us (53%)
  blocking collectives  12.9 us (20%)
  waiting for transfers between devices  9.11 us (14%)
  Pallas kernels  7.38 us (11%)
  between operations  0.82 us (1%)
    ppermute x4, starting transfers between devices, moved(): return lax.ppermute(value, axes, pairs)  18.4 us
    all_to_all x1, blocking collectives, body(): parts = lax.all_to_all(parts, ('gy', 'gz'), 0, 0).reshape(64, 128)  12.9 us
    all_to_all x1, starting transfers between devices, body(): atoms = lax.all_to_all(message, ('gy', 'gz'), 0, 0).reshape(320, 128)  11.6 us
    ppermute x4, waiting for transfers between devices, moved(): return lax.ppermute(value, axes, pairs)  5.9 us
    pallas_call x7, Pallas kernels, call(): pl.pallas_call(kernel, out_shape=[jax.ShapeDtypeStruct(shape, F32) for sh...  5.47 us
    all_to_all x1, starting transfers between devices, body(): sums = lax.all_to_all(partial, 'gx', 0, 0)  4.77 us
    all_to_all x1, waiting for transfers between devices, body(): sums = lax.all_to_all(partial, 'gx', 0, 0)  3.21 us
    pallas_call x1, Pallas kernels, body(): pl.pallas_call(pack_kernel, out_shape=[jax.ShapeDtypeStruct(shape, F32) f...  1.91 us
  transfers between devices with their start and end apart: 6, of which 3 were waited for; matrix products, arithmetic and copies ran while one was open for 0% of the time, Pallas kernels for 7%

profile of v6, /device:TPU:1, one launch (start us, length us, event | category | flops | bytes accessed | tf_op | source)
XLA Modules:
  0.0 65.0 jit_solution(5507482984689411635)
XLA Ops:
  0.6 1.9 %shard_map.122 = (f32[104,128]{1,0:T(8,128)}, f32[32,128]{1,0:T(8,128)}, f32[8,128]{1,0:T(8,128)}, f32[32,5,2,128]{3,2,1,0:T(2,128)}) custom-call(f32[64,128]{1,0:T(8,128)} %bitcast.11, f32[2,2,3,2,8]{4,3,2,1,0:T(2,128)} %bitcast.13, s32[2,2,2]{2,1,0:T(2,128)} %count_hbm.1, s32[64,32]{1,0:T(8,128)} %bitcast.12, f32[16,128]{1,0:T(8,128)} %bitcast.14, ...), custom_call_target="tpu_custom_call" | custom-call | tf_op jit(solution)/shard_map/pallas_call | solution.py:548
  2.5 8.4 %collective-permute-start = (f32[104,128]{1,0:T(8,128)}, f32[104,128]{1,0:T(8,128)S(1)}, u32[]{:S(2)}, u32[]{:S(2)}) collective-permute-start(f32[104,128]{1,0:T(8,128)} %get-tuple-element.17.own_ref), channel_id=1, source_target_pairs={{0,480},{32,0},{64,32},{96,64},{128,96},{160,128},{192,160},{224,1... | collective-permute-start | bytes 159752 | tf_op jit(solution)/shard_map/ppermute | solution.py:525
  10.9 0.0 copy-start
  11.0 0.0 copy-start.2
  11.0 11.6 %all-to-all-start = ((f32[32,5,2,128]{3,2,1,0:T(2,128)}), f32[32,5,2,128]{3,2,1,0:T(2,128)S(1)}, u32[]{:S(2)}, u32[]{:S(2)}) async-start(f32[32,5,2,128]{3,2,1,0:T(2,128)} %get-tuple-element.13), calls=%async_computation | async-start | bytes 327680 | tf_op jit(solution)/shard_map/all_to_all | solution.py:560
  22.6 0.0 collective-permute-done.in_x_ref
  22.6 0.0 copy-done
  22.6 0.0 copy-done.2
  22.6 2.1 %collective-permute-start.1 = (f32[176,128]{1,0:T(8,128)S(1)}, f32[176,128]{1,0:T(8,128)S(1)}, u32[]{:S(2)}, u32[]{:S(2)}) collective-permute-start(f32[176,128]{1,0:T(8,128)S(1)} %shard_map.125), channel_id=1, source_target_pairs={{0,3},{1,0},{2,1},{3,2},{4,7},{5,4},{6,5},{7,6},{8,11},{9,8},{10,9... | collective-permute-start | bytes 270344 | tf_op jit(solution)/shard_map/ppermute | solution.py:525
  24.8 4.6 %collective-permute-done.1.in_z_ref = f32[176,128]{1,0:T(8,128)S(1)} collective-permute-done((f32[176,128]{1,0:T(8,128)S(1)}, f32[176,128]{1,0:T(8,128)S(1)}, u32[]{:S(2)}, u32[]{:S(2)}) %collective-permute-start.1) | collective-permute-done | bytes 90144 | tf_op jit(solution)/shard_map/ppermute | solution.py:525
  29.4 4.6 %collective-permute-start.2 = (f32[320,128]{1,0:T(8,128)S(1)}, f32[320,128]{1,0:T(8,128)S(1)}, u32[]{:S(2)}, u32[]{:S(2)}) collective-permute-start(f32[320,128]{1,0:T(8,128)S(1)} %shard_map.126), channel_id=1, source_target_pairs={{0,28},{4,0},{8,4},{12,8},{16,12},{20,16},{24,20},{28,24},{1,29},{... | collective-permute-start | bytes 491528 | tf_op jit(solution)/shard_map/ppermute | solution.py:525
  34.0 0.0 all-to-all-done
  34.0 1.4 %shard_map.123 = (f32[16,8,128]{2,1,0:T(8,128)}, f32[64,2048]{1,0:T(8,128)S(1)}, f32[16,2048]{1,0:T(8,128)S(1)}) custom-call(f32[320,128]{1,0:T(8,128)S(1)} %bitcast.9), custom_call_target="tpu_custom_call" | custom-call | flops 49999998976 | bytes 150000000 | tf_op jit(solution)/shard_map/pallas_call | solution.py:508
  35.4 0.0 copy-start.1
  35.4 0.0 copy-start.3
  35.4 0.0 copy-start.4
  35.4 0.0 copy-start.6
  35.4 4.8 %all-to-all-start.1 = ((f32[16,8,128]{2,1,0:T(8,128)}), f32[16,8,128]{2,1,0:T(8,128)S(1)}, u32[]{:S(2)}, u32[]{:S(2)}) async-start(f32[16,8,128]{2,1,0:T(8,128)} %get-tuple-element.14), calls=%async_computation.1 | async-start | bytes 131072 | tf_op jit(solution)/shard_map/all_to_all | solution.py:573
  40.2 0.0 collective-permute-done.2.in_y_ref
  40.2 0.0 copy-done.1
  40.2 0.0 copy-done.3
  40.3 0.0 copy-done.4
  40.3 0.0 copy-done.5
  40.3 0.0 copy-done.6
  40.3 2.7 %shard_map.127 = (f32[8,128]{1,0:T(8,128)S(1)}, f32[8,128]{1,0:T(8,128)S(1)}) custom-call(f32[104,128]{1,0:T(8,128)S(1)} %copy-done, f32[32,128]{1,0:T(8,128)S(1)} %copy-done.2, f32[104,128]{1,0:T(8,128)S(1)} %collective-permute-done.in_x_ref, f32[176,128]{1,0:T(8,128)S(1)} %collective-permute-done.1.in_z_ref, ...), custom_call_target="tpu_custom_call" | custom-call | flops 100000000 | bytes 300000 | tf_op jit(solution)/shard_map/pallas_call | solution.py:508
  43.0 3.3 %collective-permute-start.3 = (f32[8,128]{1,0:T(8,128)S(1)}, f32[8,128]{1,0:T(8,128)S(1)}, u32[]{:S(2)}, u32[]{:S(2)}) collective-permute-start(f32[8,128]{1,0:T(8,128)S(1)} %get-tuple-element.21), channel_id=1, source_target_pairs={{0,32},{32,64},{64,96},{96,128},{128,160},{160,192},{192,224},{224... | collective-permute-start | bytes 12296 | tf_op jit(solution)/shard_map/ppermute | solution.py:525
  46.2 3.2 %all-to-all-done.1.sums_ref = f32[16,8,128]{2,1,0:T(8,128)S(1)} async-done(((f32[16,8,128]{2,1,0:T(8,128)}), f32[16,8,128]{2,1,0:T(8,128)S(1)}, u32[]{:S(2)}, u32[]{:S(2)}) %all-to-all-start.1) | async-done | bytes 65568 | tf_op jit(solution)/shard_map/all_to_all | solution.py:573
  49.4 0.5 shard_map.124.parts_ref
  50.0 1.2 %collective-permute-done.3.came_ref = f32[8,128]{1,0:T(8,128)S(1)} collective-permute-done((f32[8,128]{1,0:T(8,128)S(1)}, f32[8,128]{1,0:T(8,128)S(1)}, u32[]{:S(2)}, u32[]{:S(2)}) %collective-permute-start.3) | collective-permute-done | bytes 4128 | tf_op jit(solution)/shard_map/ppermute | solution.py:525
  51.2 0.1 shard_map.128
  51.3 12.9 %all_to_all.15 = f32[32,2,128]{2,1,0:T(2,128)S(1)} all-to-all(f32[32,2,128]{2,1,0:T(2,128)S(1)} %shard_map.128), channel_id=1, replica_groups=mesh['gx'=16,'gy'=8,'gz'=4] {'gy','gz'}, dimensions={0} | all-to-all | bytes 65536 | tf_op jit(solution)/shard_map/all_to_all | solution.py:589
  64.2 0.8 %shard_map.129 = (f32[2,2,2,8]{3,2,1,0:T(2,128)}, f32[2,2,3,2,8]{4,3,2,1,0:T(2,128)}) custom-call(f32[64,128]{1,0:T(8,128)S(1)} %bitcast.10), custom_call_target="tpu_custom_call" | custom-call | flops 1000000000 | bytes 3000000 | tf_op jit(solution)/shard_map/pallas_call | solution.py:508
  (3 shorter events, 0.0 us)
Async XLA Ops:
  2.5 20.0 %collective-permute-start = (f32[104,128]{1,0:T(8,128)}, f32[104,128]{1,0:T(8,128)S(1)}, u32[]{:S(2)}, u32[]{:S(2)}) collective-permute-start(f32[104,128]{1,0:T(8,128)} %get-tuple-element.17.own_ref), channel_id=1, source_target_pairs={{0,480},{32,0},{64,32},{96,64},{128,96},{160,128},{192,160},{224,1... | collective-permute-start | bytes 159752 | tf_op jit(solution)/shard_map/ppermute | solution.py:525
  10.9 11.6 %copy-start = (f32[104,128]{1,0:T(8,128)S(1)}, f32[104,128]{1,0:T(8,128)}, u32[]{:S(2)}) copy-start(f32[104,128]{1,0:T(8,128)} %get-tuple-element.17.own_ref) | copy-start | bytes 159748
  11.0 11.6 %copy-start.2 = (f32[32,128]{1,0:T(8,128)S(1)}, f32[32,128]{1,0:T(8,128)}, u32[]{:S(2)}) copy-start(f32[32,128]{1,0:T(8,128)} %get-tuple-element.18.rest_ref) | copy-start | bytes 49156
  11.0 23.1 %all-to-all-start = ((f32[32,5,2,128]{3,2,1,0:T(2,128)}), f32[32,5,2,128]{3,2,1,0:T(2,128)S(1)}, u32[]{:S(2)}, u32[]{:S(2)}) async-start(f32[32,5,2,128]{3,2,1,0:T(2,128)} %get-tuple-element.13), calls=%async_computation | async-start | bytes 327680 | tf_op jit(solution)/shard_map/all_to_all | solution.py:560
  22.6 6.8 %collective-permute-start.1 = (f32[176,128]{1,0:T(8,128)S(1)}, f32[176,128]{1,0:T(8,128)S(1)}, u32[]{:S(2)}, u32[]{:S(2)}) collective-permute-start(f32[176,128]{1,0:T(8,128)S(1)} %shard_map.125), channel_id=1, source_target_pairs={{0,3},{1,0},{2,1},{3,2},{4,7},{5,4},{6,5},{7,6},{8,11},{9,8},{10,9... | collective-permute-start | bytes 270344 | tf_op jit(solution)/shard_map/ppermute | solution.py:525
  29.4 10.8 %collective-permute-start.2 = (f32[320,128]{1,0:T(8,128)S(1)}, f32[320,128]{1,0:T(8,128)S(1)}, u32[]{:S(2)}, u32[]{:S(2)}) collective-permute-start(f32[320,128]{1,0:T(8,128)S(1)} %shard_map.126), channel_id=1, source_target_pairs={{0,28},{4,0},{8,4},{12,8},{16,12},{20,16},{24,20},{28,24},{1,29},{... | collective-permute-start | bytes 491528 | tf_op jit(solution)/shard_map/ppermute | solution.py:525
  35.4 4.8 %copy-start.1 = (f32[128,128]{1,0:T(8,128)S(1)}, f32[128,128]{1,0:T(8,128)}, u32[]{:S(2)}) copy-start(f32[128,128]{1,0:T(8,128)} %mix_ref.1) | copy-start | bytes 196612
  35.4 4.8 %copy-start.3 = (f32[8,128]{1,0:T(8,128)S(1)}, f32[8,128]{1,0:T(8,128)}, u32[]{:S(2)}) copy-start(f32[8,128]{1,0:T(8,128)} %radial_ref.1) | copy-start | bytes 12292
  35.4 4.8 %copy-start.4 = (f32[8,128]{1,0:T(8,128)S(1)}, f32[8,128]{1,0:T(8,128)}, u32[]{:S(2)}) copy-start(f32[8,128]{1,0:T(8,128)} %vector_ref.1) | copy-start | bytes 12292
  35.4 4.8 %copy-start.5 = (s32[2,2,2,8]{3,2,1,0:T(2,128)S(1)}, s32[2,2,2,8]{3,2,1,0:T(2,128)}, u32[]{:S(2)}) copy-start(s32[2,2,2,8]{3,2,1,0:T(2,128)} %species_ref.1) | copy-start | bytes 772
  35.4 4.8 %copy-start.6 = (f32[8,128]{1,0:T(8,128)S(1)}, f32[8,128]{1,0:T(8,128)}, u32[]{:S(2)}) copy-start(f32[8,128]{1,0:T(8,128)} %get-tuple-element.19.extra_ref) | copy-start | bytes 12292
  35.4 14.0 %all-to-all-start.1 = ((f32[16,8,128]{2,1,0:T(8,128)}), f32[16,8,128]{2,1,0:T(8,128)S(1)}, u32[]{:S(2)}, u32[]{:S(2)}) async-start(f32[16,8,128]{2,1,0:T(8,128)} %get-tuple-element.14), calls=%async_computation.1 | async-start | bytes 131072 | tf_op jit(solution)/shard_map/all_to_all | solution.py:573
  43.0 8.3 %collective-permute-start.3 = (f32[8,128]{1,0:T(8,128)S(1)}, f32[8,128]{1,0:T(8,128)S(1)}, u32[]{:S(2)}, u32[]{:S(2)}) collective-permute-start(f32[8,128]{1,0:T(8,128)S(1)} %get-tuple-element.21), channel_id=1, source_target_pairs={{0,32},{32,64},{64,96},{96,128},{128,160},{160,192},{192,224},{224... | collective-permute-start | bytes 12296 | tf_op jit(solution)/shard_map/ppermute | solution.py:525

commit v7 on v6

--- a/solution.py
+++ b/solution.py
@@ -211,13 +211,27 @@
         [jnp.concatenate(upper, 1), jnp.concatenate(lower, 1)], 0
     )
     places = jnp.concatenate(places, 1)
-    number_x, number_y, number_z = wave_numbers(member, (32, 1), 0)
+    row = iota((16, 1), 0)
+    along_z = jnp.where(row < 8, (row - KZ // 2).astype(F32), 0.0)
+    along_y = (row - 8 + (member % 2) * 4 - KY // 2).astype(F32)
+    along_y = jnp.where((row >= 8) & (row < 12), along_y, 0.0)
+    along_x = jnp.where(row == 12, (member // 2 - KX // 2).astype(F32), 0.0)
     turns = (
-        number_x * (places[0:1] * (1.0 / grid[0]))
-        + number_y * (places[2:3] * (1.0 / grid[1]))
-        + number_z * (places[1:2] * (1.0 / grid[2]))
+        along_x * (places[0:1] * (1.0 / grid[0]))
+        + along_y * (places[2:3] * (1.0 / grid[1]))
+        + along_z * (places[1:2] * (1.0 / grid[2]))
     )
     sine, cosine = sine_cosine(turns)
+    sine_z, cosine_z = sine[0:8], cosine[0:8]
+    sine_x, cosine_x = sine[12:13], cosine[12:13]
+    flat_sine = sine_x * cosine[8:12] + cosine_x * sine[8:12]
+    flat_cosine = cosine_x * cosine[8:12] - sine_x * sine[8:12]
+    sines, cosines = [], []
+    for k in range(4):
+        sine_xy, cosine_xy = flat_sine[k : k + 1], flat_cosine[k : k + 1]
+        sines.append(sine_xy * cosine_z + cosine_xy * sine_z)
+        cosines.append(cosine_xy * cosine_z - sine_xy * sine_z)
+    sine, cosine = jnp.concatenate(sines, 0), jnp.concatenate(cosines, 0)
     phases = jnp.concatenate([cosine, sine], 0)
     phase_ref[...] = phases
     charge_ref[...] = charges

time: 65.5 us -> 65.4 us (level)
  no operation moved by 1% of the time
where the time goes in v7:
time: 65.4 us; the launch traced here: 64.9 us
  starting transfers between devices  34.7 us (53%)
  blocking collectives  12.9 us (20%)
  waiting for transfers between devices  9.13 us (14%)
  Pallas kernels  7.3 us (11%)
  between operations  0.82 us (1%)
    ppermute x4, starting transfers between devices, moved(): return lax.ppermute(value, axes, pairs)  18.4 us
    all_to_all x1, blocking collectives, body(): parts = lax.all_to_all(parts, ('gy', 'gz'), 0, 0).reshape(64, 128)  12.9 us
    all_to_all x1, starting transfers between devices, body(): atoms = lax.all_to_all(message, ('gy', 'gz'), 0, 0).reshape(320, 128)  11.6 us
    ppermute x4, waiting for transfers between devices, moved(): return lax.ppermute(value, axes, pairs)  5.92 us
    pallas_call x7, Pallas kernels, call(): pl.pallas_call(kernel, out_shape=[jax.ShapeDtypeStruct(shape, F32) for sh...  5.39 us
    all_to_all x1, starting transfers between devices, body(): sums = lax.all_to_all(partial, 'gx', 0, 0)  4.77 us
    all_to_all x1, waiting for transfers between devices, body(): sums = lax.all_to_all(partial, 'gx', 0, 0)  3.21 us
    pallas_call x1, Pallas kernels, body(): pl.pallas_call(pack_kernel, out_shape=[jax.ShapeDtypeStruct(shape, F32) f...  1.91 us
  transfers between devices with their start and end apart: 6, of which 3 were waited for; matrix products, arithmetic and copies ran while one was open for 0% of the time, Pallas kernels for 7%

profile of v7, /device:TPU:1, one launch (start us, length us, event | category | flops | bytes accessed | tf_op | source)
XLA Modules:
  0.0 64.9 jit_solution(11939313820048029193)
XLA Ops:
  0.6 1.9 %shard_map.122 = (f32[104,128]{1,0:T(8,128)}, f32[32,128]{1,0:T(8,128)}, f32[8,128]{1,0:T(8,128)}, f32[32,5,2,128]{3,2,1,0:T(2,128)}) custom-call(f32[64,128]{1,0:T(8,128)} %bitcast.11, f32[2,2,3,2,8]{4,3,2,1,0:T(2,128)} %bitcast.13, s32[2,2,2]{2,1,0:T(2,128)} %count_hbm.1, s32[64,32]{1,0:T(8,128)} %bitcast.12, f32[16,128]{1,0:T(8,128)} %bitcast.14, ...), custom_call_target="tpu_custom_call" | custom-call | tf_op jit(solution)/shard_map/pallas_call | solution.py:562
  2.5 8.4 %collective-permute-start = (f32[104,128]{1,0:T(8,128)}, f32[104,128]{1,0:T(8,128)S(1)}, u32[]{:S(2)}, u32[]{:S(2)}) collective-permute-start(f32[104,128]{1,0:T(8,128)} %get-tuple-element.17.own_ref), channel_id=1, source_target_pairs={{0,480},{32,0},{64,32},{96,64},{128,96},{160,128},{192,160},{224,1... | collective-permute-start | bytes 159752 | tf_op jit(solution)/shard_map/ppermute | solution.py:539
  10.9 0.0 copy-start
  11.0 0.0 copy-start.2
  11.0 11.6 %all-to-all-start = ((f32[32,5,2,128]{3,2,1,0:T(2,128)}), f32[32,5,2,128]{3,2,1,0:T(2,128)S(1)}, u32[]{:S(2)}, u32[]{:S(2)}) async-start(f32[32,5,2,128]{3,2,1,0:T(2,128)} %get-tuple-element.13), calls=%async_computation | async-start | bytes 327680 | tf_op jit(solution)/shard_map/all_to_all | solution.py:574
  22.6 0.0 collective-permute-done.in_x_ref
  22.6 0.0 copy-done
  22.6 0.0 copy-done.2
  22.6 2.1 %collective-permute-start.1 = (f32[176,128]{1,0:T(8,128)S(1)}, f32[176,128]{1,0:T(8,128)S(1)}, u32[]{:S(2)}, u32[]{:S(2)}) collective-permute-start(f32[176,128]{1,0:T(8,128)S(1)} %shard_map.125), channel_id=1, source_target_pairs={{0,3},{1,0},{2,1},{3,2},{4,7},{5,4},{6,5},{7,6},{8,11},{9,8},{10,9... | collective-permute-start | bytes 270344 | tf_op jit(solution)/shard_map/ppermute | solution.py:539
  24.8 4.6 %collective-permute-done.1.in_z_ref = f32[176,128]{1,0:T(8,128)S(1)} collective-permute-done((f32[176,128]{1,0:T(8,128)S(1)}, f32[176,128]{1,0:T(8,128)S(1)}, u32[]{:S(2)}, u32[]{:S(2)}) %collective-permute-start.1) | collective-permute-done | bytes 90144 | tf_op jit(solution)/shard_map/ppermute | solution.py:539
  29.4 4.6 %collective-permute-start.2 = (f32[320,128]{1,0:T(8,128)S(1)}, f32[320,128]{1,0:T(8,128)S(1)}, u32[]{:S(2)}, u32[]{:S(2)}) collective-permute-start(f32[320,128]{1,0:T(8,128)S(1)} %shard_map.126), channel_id=1, source_target_pairs={{0,28},{4,0},{8,4},{12,8},{16,12},{20,16},{24,20},{28,24},{1,29},{... | collective-permute-start | bytes 491528 | tf_op jit(solution)/shard_map/ppermute | solution.py:539
  34.0 0.0 all-to-all-done
  34.0 1.3 %shard_map.123 = (f32[16,8,128]{2,1,0:T(8,128)}, f32[64,2048]{1,0:T(8,128)S(1)}, f32[16,2048]{1,0:T(8,128)S(1)}) custom-call(f32[320,128]{1,0:T(8,128)S(1)} %bitcast.9), custom_call_target="tpu_custom_call" | custom-call | flops 49999998976 | bytes 150000000 | tf_op jit(solution)/shard_map/pallas_call | solution.py:522
  35.3 0.0 copy-start.1
  35.4 0.0 copy-start.4
  35.4 0.0 copy-start.5
  35.4 0.0 copy-start.6
  35.4 4.8 %all-to-all-start.1 = ((f32[16,8,128]{2,1,0:T(8,128)}), f32[16,8,128]{2,1,0:T(8,128)S(1)}, u32[]{:S(2)}, u32[]{:S(2)}) async-start(f32[16,8,128]{2,1,0:T(8,128)} %get-tuple-element.14), calls=%async_computation.1 | async-start | bytes 131072 | tf_op jit(solution)/shard_map/all_to_all | solution.py:587
  40.1 0.0 collective-permute-done.2.in_y_ref
  40.2 0.0 copy-done.1
  40.2 0.0 copy-done.3
  40.2 0.0 copy-done.4
  40.2 0.0 copy-done.5
  40.2 0.0 copy-done.6
  40.2 2.7 %shard_map.127 = (f32[8,128]{1,0:T(8,128)S(1)}, f32[8,128]{1,0:T(8,128)S(1)}) custom-call(f32[104,128]{1,0:T(8,128)S(1)} %copy-done, f32[32,128]{1,0:T(8,128)S(1)} %copy-done.2, f32[104,128]{1,0:T(8,128)S(1)} %collective-permute-done.in_x_ref, f32[176,128]{1,0:T(8,128)S(1)} %collective-permute-done.1.in_z_ref, ...), custom_call_target="tpu_custom_call" | custom-call | flops 100000000 | bytes 300000 | tf_op jit(solution)/shard_map/pallas_call | solution.py:522
  42.9 3.3 %collective-permute-start.3 = (f32[8,128]{1,0:T(8,128)S(1)}, f32[8,128]{1,0:T(8,128)S(1)}, u32[]{:S(2)}, u32[]{:S(2)}) collective-permute-start(f32[8,128]{1,0:T(8,128)S(1)} %get-tuple-element.21), channel_id=1, source_target_pairs={{0,32},{32,64},{64,96},{96,128},{128,160},{160,192},{192,224},{224... | collective-permute-start | bytes 12296 | tf_op jit(solution)/shard_map/ppermute | solution.py:539
  46.1 3.2 %all-to-all-done.1.sums_ref = f32[16,8,128]{2,1,0:T(8,128)S(1)} async-done(((f32[16,8,128]{2,1,0:T(8,128)}), f32[16,8,128]{2,1,0:T(8,128)S(1)}, u32[]{:S(2)}, u32[]{:S(2)}) %all-to-all-start.1) | async-done | bytes 65568 | tf_op jit(solution)/shard_map/all_to_all | solution.py:587
  49.4 0.5 shard_map.124.parts_ref
  49.9 1.3 %collective-permute-done.3.came_ref = f32[8,128]{1,0:T(8,128)S(1)} collective-permute-done((f32[8,128]{1,0:T(8,128)S(1)}, f32[8,128]{1,0:T(8,128)S(1)}, u32[]{:S(2)}, u32[]{:S(2)}) %collective-permute-start.3) | collective-permute-done | bytes 4128 | tf_op jit(solution)/shard_map/ppermute | solution.py:539
  51.2 0.1 shard_map.128
  51.2 12.9 %all_to_all.15 = f32[32,2,128]{2,1,0:T(2,128)S(1)} all-to-all(f32[32,2,128]{2,1,0:T(2,128)S(1)} %shard_map.128), channel_id=1, replica_groups=mesh['gx'=16,'gy'=8,'gz'=4] {'gy','gz'}, dimensions={0} | all-to-all | bytes 65536 | tf_op jit(solution)/shard_map/all_to_all | solution.py:603
  64.2 0.8 %shard_map.129 = (f32[2,2,2,8]{3,2,1,0:T(2,128)}, f32[2,2,3,2,8]{4,3,2,1,0:T(2,128)}) custom-call(f32[64,128]{1,0:T(8,128)S(1)} %bitcast.10), custom_call_target="tpu_custom_call" | custom-call | flops 1000000000 | bytes 3000000 | tf_op jit(solution)/shard_map/pallas_call | solution.py:522
  (3 shorter events, 0.0 us)
Async XLA Ops:
  2.5 20.0 %collective-permute-start = (f32[104,128]{1,0:T(8,128)}, f32[104,128]{1,0:T(8,128)S(1)}, u32[]{:S(2)}, u32[]{:S(2)}) collective-permute-start(f32[104,128]{1,0:T(8,128)} %get-tuple-element.17.own_ref), channel_id=1, source_target_pairs={{0,480},{32,0},{64,32},{96,64},{128,96},{160,128},{192,160},{224,1... | collective-permute-start | bytes 159752 | tf_op jit(solution)/shard_map/ppermute | solution.py:539
  10.9 11.6 %copy-start = (f32[104,128]{1,0:T(8,128)S(1)}, f32[104,128]{1,0:T(8,128)}, u32[]{:S(2)}) copy-start(f32[104,128]{1,0:T(8,128)} %get-tuple-element.17.own_ref) | copy-start | bytes 159748
  11.0 11.6 %copy-start.2 = (f32[32,128]{1,0:T(8,128)S(1)}, f32[32,128]{1,0:T(8,128)}, u32[]{:S(2)}) copy-start(f32[32,128]{1,0:T(8,128)} %get-tuple-element.18.rest_ref) | copy-start | bytes 49156
  11.0 23.1 %all-to-all-start = ((f32[32,5,2,128]{3,2,1,0:T(2,128)}), f32[32,5,2,128]{3,2,1,0:T(2,128)S(1)}, u32[]{:S(2)}, u32[]{:S(2)}) async-start(f32[32,5,2,128]{3,2,1,0:T(2,128)} %get-tuple-element.13), calls=%async_computation | async-start | bytes 327680 | tf_op jit(solution)/shard_map/all_to_all | solution.py:574
  22.6 6.8 %collective-permute-start.1 = (f32[176,128]{1,0:T(8,128)S(1)}, f32[176,128]{1,0:T(8,128)S(1)}, u32[]{:S(2)}, u32[]{:S(2)}) collective-permute-start(f32[176,128]{1,0:T(8,128)S(1)} %shard_map.125), channel_id=1, source_target_pairs={{0,3},{1,0},{2,1},{3,2},{4,7},{5,4},{6,5},{7,6},{8,11},{9,8},{10,9... | collective-permute-start | bytes 270344 | tf_op jit(solution)/shard_map/ppermute | solution.py:539
  29.4 10.7 %collective-permute-start.2 = (f32[320,128]{1,0:T(8,128)S(1)}, f32[320,128]{1,0:T(8,128)S(1)}, u32[]{:S(2)}, u32[]{:S(2)}) collective-permute-start(f32[320,128]{1,0:T(8,128)S(1)} %shard_map.126), channel_id=1, source_target_pairs={{0,28},{4,0},{8,4},{12,8},{16,12},{20,16},{24,20},{28,24},{1,29},{... | collective-permute-start | bytes 491528 | tf_op jit(solution)/shard_map/ppermute | solution.py:539
  35.3 4.8 %copy-start.1 = (f32[128,128]{1,0:T(8,128)S(1)}, f32[128,128]{1,0:T(8,128)}, u32[]{:S(2)}) copy-start(f32[128,128]{1,0:T(8,128)} %mix_ref.1) | copy-start | bytes 196612
  35.3 4.8 %copy-start.3 = (f32[8,128]{1,0:T(8,128)S(1)}, f32[8,128]{1,0:T(8,128)}, u32[]{:S(2)}) copy-start(f32[8,128]{1,0:T(8,128)} %radial_ref.1) | copy-start | bytes 12292
  35.4 4.8 %copy-start.4 = (f32[8,128]{1,0:T(8,128)S(1)}, f32[8,128]{1,0:T(8,128)}, u32[]{:S(2)}) copy-start(f32[8,128]{1,0:T(8,128)} %vector_ref.1) | copy-start | bytes 12292
  35.4 4.8 %copy-start.5 = (s32[2,2,2,8]{3,2,1,0:T(2,128)S(1)}, s32[2,2,2,8]{3,2,1,0:T(2,128)}, u32[]{:S(2)}) copy-start(s32[2,2,2,8]{3,2,1,0:T(2,128)} %species_ref.1) | copy-start | bytes 772
  35.4 4.8 %copy-start.6 = (f32[8,128]{1,0:T(8,128)S(1)}, f32[8,128]{1,0:T(8,128)}, u32[]{:S(2)}) copy-start(f32[8,128]{1,0:T(8,128)} %get-tuple-element.19.extra_ref) | copy-start | bytes 12292
  35.4 14.0 %all-to-all-start.1 = ((f32[16,8,128]{2,1,0:T(8,128)}), f32[16,8,128]{2,1,0:T(8,128)S(1)}, u32[]{:S(2)}, u32[]{:S(2)}) async-start(f32[16,8,128]{2,1,0:T(8,128)} %get-tuple-element.14), calls=%async_computation.1 | async-start | bytes 131072 | tf_op jit(solution)/shard_map/all_to_all | solution.py:587
  42.9 8.3 %collective-permute-start.3 = (f32[8,128]{1,0:T(8,128)S(1)}, f32[8,128]{1,0:T(8,128)S(1)}, u32[]{:S(2)}, u32[]{:S(2)}) collective-permute-start(f32[8,128]{1,0:T(8,128)S(1)} %get-tuple-element.21), channel_id=1, source_target_pairs={{0,32},{32,64},{64,96},{96,128},{128,160},{160,192},{192,224},{224... | collective-permute-start | bytes 12296 | tf_op jit(solution)/shard_map/ppermute | solution.py:539

commit v8 on v7

--- a/solution.py
+++ b/solution.py
@@ -20,7 +20,7 @@
 WAVES_MICROS = 500
 FIELD_MICROS = 50
 SHORT_MICROS = 1
-PACK_ROOM = 60
+PACK_ROOM = 55
 LAST_ROOM = 48
 
 

time: 65.4 us -> 65.4 us (level)
  no operation moved by 1% of the time
where the time goes in v8:
time: 65.4 us; the launch traced here: 64.9 us
  starting transfers between devices  34.7 us (53%)
  blocking collectives  12.9 us (20%)
  waiting for transfers between devices  9.13 us (14%)
  Pallas kernels  7.3 us (11%)
  between operations  0.82 us (1%)
    ppermute x4, starting transfers between devices, moved(): return lax.ppermute(value, axes, pairs)  18.4 us
    all_to_all x1, blocking collectives, body(): parts = lax.all_to_all(parts, ('gy', 'gz'), 0, 0).reshape(64, 128)  12.9 us
    all_to_all x1, starting transfers between devices, body(): atoms = lax.all_to_all(message, ('gy', 'gz'), 0, 0).reshape(320, 128)  11.6 us
    ppermute x4, waiting for transfers between devices, moved(): return lax.ppermute(value, axes, pairs)  5.92 us
    pallas_call x7, Pallas kernels, call(): pl.pallas_call(kernel, out_shape=[jax.ShapeDtypeStruct(shape, F32) for sh...  5.39 us
    all_to_all x1, starting transfers between devices, body(): sums = lax.all_to_all(partial, 'gx', 0, 0)  4.77 us
    all_to_all x1, waiting for transfers between devices, body(): sums = lax.all_to_all(partial, 'gx', 0, 0)  3.21 us
    pallas_call x1, Pallas kernels, body(): pl.pallas_call(pack_kernel, out_shape=[jax.ShapeDtypeStruct(shape, F32) f...  1.91 us
  transfers between devices with their start and end apart: 6, of which 3 were waited for; matrix products, arithmetic and copies ran while one was open for 0% of the time, Pallas kernels for 7%

profile of v8, /device:TPU:1, one launch (start us, length us, event | category | flops | bytes accessed | tf_op | source)
XLA Modules:
  0.0 64.9 jit_solution(11939313820048029193)
XLA Ops:
  0.6 1.9 %shard_map.122 = (f32[104,128]{1,0:T(8,128)}, f32[32,128]{1,0:T(8,128)}, f32[8,128]{1,0:T(8,128)}, f32[32,5,2,128]{3,2,1,0:T(2,128)}) custom-call(f32[64,128]{1,0:T(8,128)} %bitcast.11, f32[2,2,3,2,8]{4,3,2,1,0:T(2,128)} %bitcast.13, s32[2,2,2]{2,1,0:T(2,128)} %count_hbm.1, s32[64,32]{1,0:T(8,128)} %bitcast.12, f32[16,128]{1,0:T(8,128)} %bitcast.14, ...), custom_call_target="tpu_custom_call" | custom-call | tf_op jit(solution)/shard_map/pallas_call | solution.py:562
  2.5 8.4 %collective-permute-start = (f32[104,128]{1,0:T(8,128)}, f32[104,128]{1,0:T(8,128)S(1)}, u32[]{:S(2)}, u32[]{:S(2)}) collective-permute-start(f32[104,128]{1,0:T(8,128)} %get-tuple-element.17.own_ref), channel_id=1, source_target_pairs={{0,480},{32,0},{64,32},{96,64},{128,96},{160,128},{192,160},{224,1... | collective-permute-start | bytes 159752 | tf_op jit(solution)/shard_map/ppermute | solution.py:539
  10.9 0.0 copy-start
  11.0 0.0 copy-start.2
  11.0 11.6 %all-to-all-start = ((f32[32,5,2,128]{3,2,1,0:T(2,128)}), f32[32,5,2,128]{3,2,1,0:T(2,128)S(1)}, u32[]{:S(2)}, u32[]{:S(2)}) async-start(f32[32,5,2,128]{3,2,1,0:T(2,128)} %get-tuple-element.13), calls=%async_computation | async-start | bytes 327680 | tf_op jit(solution)/shard_map/all_to_all | solution.py:574
  22.6 0.0 collective-permute-done.in_x_ref
  22.6 0.0 copy-done
  22.6 0.0 copy-done.2
  22.6 2.1 %collective-permute-start.1 = (f32[176,128]{1,0:T(8,128)S(1)}, f32[176,128]{1,0:T(8,128)S(1)}, u32[]{:S(2)}, u32[]{:S(2)}) collective-permute-start(f32[176,128]{1,0:T(8,128)S(1)} %shard_map.125), channel_id=1, source_target_pairs={{0,3},{1,0},{2,1},{3,2},{4,7},{5,4},{6,5},{7,6},{8,11},{9,8},{10,9... | collective-permute-start | bytes 270344 | tf_op jit(solution)/shard_map/ppermute | solution.py:539
  24.8 4.6 %collective-permute-done.1.in_z_ref = f32[176,128]{1,0:T(8,128)S(1)} collective-permute-done((f32[176,128]{1,0:T(8,128)S(1)}, f32[176,128]{1,0:T(8,128)S(1)}, u32[]{:S(2)}, u32[]{:S(2)}) %collective-permute-start.1) | collective-permute-done | bytes 90144 | tf_op jit(solution)/shard_map/ppermute | solution.py:539
  29.4 4.6 %collective-permute-start.2 = (f32[320,128]{1,0:T(8,128)S(1)}, f32[320,128]{1,0:T(8,128)S(1)}, u32[]{:S(2)}, u32[]{:S(2)}) collective-permute-start(f32[320,128]{1,0:T(8,128)S(1)} %shard_map.126), channel_id=1, source_target_pairs={{0,28},{4,0},{8,4},{12,8},{16,12},{20,16},{24,20},{28,24},{1,29},{... | collective-permute-start | bytes 491528 | tf_op jit(solution)/shard_map/ppermute | solution.py:539
  34.0 0.0 all-to-all-done
  34.0 1.3 %shard_map.123 = (f32[16,8,128]{2,1,0:T(8,128)}, f32[64,2048]{1,0:T(8,128)S(1)}, f32[16,2048]{1,0:T(8,128)S(1)}) custom-call(f32[320,128]{1,0:T(8,128)S(1)} %bitcast.9), custom_call_target="tpu_custom_call" | custom-call | flops 49999998976 | bytes 150000000 | tf_op jit(solution)/shard_map/pallas_call | solution.py:522
  35.3 0.0 copy-start.1
  35.4 0.0 copy-start.4
  35.4 0.0 copy-start.5
  35.4 0.0 copy-start.6
  35.4 4.8 %all-to-all-start.1 = ((f32[16,8,128]{2,1,0:T(8,128)}), f32[16,8,128]{2,1,0:T(8,128)S(1)}, u32[]{:S(2)}, u32[]{:S(2)}) async-start(f32[16,8,128]{2,1,0:T(8,128)} %get-tuple-element.14), calls=%async_computation.1 | async-start | bytes 131072 | tf_op jit(solution)/shard_map/all_to_all | solution.py:587
  40.1 0.0 collective-permute-done.2.in_y_ref
  40.2 0.0 copy-done.1
  40.2 0.0 copy-done.3
  40.2 0.0 copy-done.4
  40.2 0.0 copy-done.5
  40.2 0.0 copy-done.6
  40.2 2.7 %shard_map.127 = (f32[8,128]{1,0:T(8,128)S(1)}, f32[8,128]{1,0:T(8,128)S(1)}) custom-call(f32[104,128]{1,0:T(8,128)S(1)} %copy-done, f32[32,128]{1,0:T(8,128)S(1)} %copy-done.2, f32[104,128]{1,0:T(8,128)S(1)} %collective-permute-done.in_x_ref, f32[176,128]{1,0:T(8,128)S(1)} %collective-permute-done.1.in_z_ref, ...), custom_call_target="tpu_custom_call" | custom-call | flops 100000000 | bytes 300000 | tf_op jit(solution)/shard_map/pallas_call | solution.py:522
  42.9 3.3 %collective-permute-start.3 = (f32[8,128]{1,0:T(8,128)S(1)}, f32[8,128]{1,0:T(8,128)S(1)}, u32[]{:S(2)}, u32[]{:S(2)}) collective-permute-start(f32[8,128]{1,0:T(8,128)S(1)} %get-tuple-element.21), channel_id=1, source_target_pairs={{0,32},{32,64},{64,96},{96,128},{128,160},{160,192},{192,224},{224... | collective-permute-start | bytes 12296 | tf_op jit(solution)/shard_map/ppermute | solution.py:539
  46.1 3.2 %all-to-all-done.1.sums_ref = f32[16,8,128]{2,1,0:T(8,128)S(1)} async-done(((f32[16,8,128]{2,1,0:T(8,128)}), f32[16,8,128]{2,1,0:T(8,128)S(1)}, u32[]{:S(2)}, u32[]{:S(2)}) %all-to-all-start.1) | async-done | bytes 65568 | tf_op jit(solution)/shard_map/all_to_all | solution.py:587
  49.4 0.5 shard_map.124.parts_ref
  49.9 1.3 %collective-permute-done.3.came_ref = f32[8,128]{1,0:T(8,128)S(1)} collective-permute-done((f32[8,128]{1,0:T(8,128)S(1)}, f32[8,128]{1,0:T(8,128)S(1)}, u32[]{:S(2)}, u32[]{:S(2)}) %collective-permute-start.3) | collective-permute-done | bytes 4128 | tf_op jit(solution)/shard_map/ppermute | solution.py:539
  51.2 0.1 shard_map.128
  51.2 12.9 %all_to_all.15 = f32[32,2,128]{2,1,0:T(2,128)S(1)} all-to-all(f32[32,2,128]{2,1,0:T(2,128)S(1)} %shard_map.128), channel_id=1, replica_groups=mesh['gx'=16,'gy'=8,'gz'=4] {'gy','gz'}, dimensions={0} | all-to-all | bytes 65536 | tf_op jit(solution)/shard_map/all_to_all | solution.py:603
  64.2 0.8 %shard_map.129 = (f32[2,2,2,8]{3,2,1,0:T(2,128)}, f32[2,2,3,2,8]{4,3,2,1,0:T(2,128)}) custom-call(f32[64,128]{1,0:T(8,128)S(1)} %bitcast.10), custom_call_target="tpu_custom_call" | custom-call | flops 1000000000 | bytes 3000000 | tf_op jit(solution)/shard_map/pallas_call | solution.py:522
  (3 shorter events, 0.0 us)
Async XLA Ops:
  2.5 20.0 %collective-permute-start = (f32[104,128]{1,0:T(8,128)}, f32[104,128]{1,0:T(8,128)S(1)}, u32[]{:S(2)}, u32[]{:S(2)}) collective-permute-start(f32[104,128]{1,0:T(8,128)} %get-tuple-element.17.own_ref), channel_id=1, source_target_pairs={{0,480},{32,0},{64,32},{96,64},{128,96},{160,128},{192,160},{224,1... | collective-permute-start | bytes 159752 | tf_op jit(solution)/shard_map/ppermute | solution.py:539
  10.9 11.6 %copy-start = (f32[104,128]{1,0:T(8,128)S(1)}, f32[104,128]{1,0:T(8,128)}, u32[]{:S(2)}) copy-start(f32[104,128]{1,0:T(8,128)} %get-tuple-element.17.own_ref) | copy-start | bytes 159748
  11.0 11.6 %copy-start.2 = (f32[32,128]{1,0:T(8,128)S(1)}, f32[32,128]{1,0:T(8,128)}, u32[]{:S(2)}) copy-start(f32[32,128]{1,0:T(8,128)} %get-tuple-element.18.rest_ref) | copy-start | bytes 49156
  11.0 23.1 %all-to-all-start = ((f32[32,5,2,128]{3,2,1,0:T(2,128)}), f32[32,5,2,128]{3,2,1,0:T(2,128)S(1)}, u32[]{:S(2)}, u32[]{:S(2)}) async-start(f32[32,5,2,128]{3,2,1,0:T(2,128)} %get-tuple-element.13), calls=%async_computation | async-start | bytes 327680 | tf_op jit(solution)/shard_map/all_to_all | solution.py:574
  22.6 6.8 %collective-permute-start.1 = (f32[176,128]{1,0:T(8,128)S(1)}, f32[176,128]{1,0:T(8,128)S(1)}, u32[]{:S(2)}, u32[]{:S(2)}) collective-permute-start(f32[176,128]{1,0:T(8,128)S(1)} %shard_map.125), channel_id=1, source_target_pairs={{0,3},{1,0},{2,1},{3,2},{4,7},{5,4},{6,5},{7,6},{8,11},{9,8},{10,9... | collective-permute-start | bytes 270344 | tf_op jit(solution)/shard_map/ppermute | solution.py:539
  29.4 10.7 %collective-permute-start.2 = (f32[320,128]{1,0:T(8,128)S(1)}, f32[320,128]{1,0:T(8,128)S(1)}, u32[]{:S(2)}, u32[]{:S(2)}) collective-permute-start(f32[320,128]{1,0:T(8,128)S(1)} %shard_map.126), channel_id=1, source_target_pairs={{0,28},{4,0},{8,4},{12,8},{16,12},{20,16},{24,20},{28,24},{1,29},{... | collective-permute-start | bytes 491528 | tf_op jit(solution)/shard_map/ppermute | solution.py:539
  35.3 4.8 %copy-start.1 = (f32[128,128]{1,0:T(8,128)S(1)}, f32[128,128]{1,0:T(8,128)}, u32[]{:S(2)}) copy-start(f32[128,128]{1,0:T(8,128)} %mix_ref.1) | copy-start | bytes 196612
  35.3 4.8 %copy-start.3 = (f32[8,128]{1,0:T(8,128)S(1)}, f32[8,128]{1,0:T(8,128)}, u32[]{:S(2)}) copy-start(f32[8,128]{1,0:T(8,128)} %radial_ref.1) | copy-start | bytes 12292
  35.4 4.8 %copy-start.4 = (f32[8,128]{1,0:T(8,128)S(1)}, f32[8,128]{1,0:T(8,128)}, u32[]{:S(2)}) copy-start(f32[8,128]{1,0:T(8,128)} %vector_ref.1) | copy-start | bytes 12292
  35.4 4.8 %copy-start.5 = (s32[2,2,2,8]{3,2,1,0:T(2,128)S(1)}, s32[2,2,2,8]{3,2,1,0:T(2,128)}, u32[]{:S(2)}) copy-start(s32[2,2,2,8]{3,2,1,0:T(2,128)} %species_ref.1) | copy-start | bytes 772
  35.4 4.8 %copy-start.6 = (f32[8,128]{1,0:T(8,128)S(1)}, f32[8,128]{1,0:T(8,128)}, u32[]{:S(2)}) copy-start(f32[8,128]{1,0:T(8,128)} %get-tuple-element.19.extra_ref) | copy-start | bytes 12292
  35.4 14.0 %all-to-all-start.1 = ((f32[16,8,128]{2,1,0:T(8,128)}), f32[16,8,128]{2,1,0:T(8,128)S(1)}, u32[]{:S(2)}, u32[]{:S(2)}) async-start(f32[16,8,128]{2,1,0:T(8,128)} %get-tuple-element.14), calls=%async_computation.1 | async-start | bytes 131072 | tf_op jit(solution)/shard_map/all_to_all | solution.py:587
  42.9 8.3 %collective-permute-start.3 = (f32[8,128]{1,0:T(8,128)S(1)}, f32[8,128]{1,0:T(8,128)S(1)}, u32[]{:S(2)}, u32[]{:S(2)}) collective-permute-start(f32[8,128]{1,0:T(8,128)S(1)} %get-tuple-element.21), channel_id=1, source_target_pairs={{0,32},{32,64},{64,96},{96,128},{128,160},{160,192},{192,224},{224... | collective-permute-start | bytes 12296 | tf_op jit(solution)/shard_map/ppermute | solution.py:539
